TPU v7x, 128 devices: a whole 4x4x4 slice. The times are simulated.
128 devices in a mesh: outer: 2 (over core), inner: 16 (over z, y), head: 4 (over x).
Axes of the slice: x: 4, y: 4, z: 4, core: 2. Of those that a mesh axis runs over, the one named last changes fastest.
Arguments:
- queries: bfloat16 [4096, 8192], P(('outer', 'inner'), 'head'), may hold values from -5.5 to 5.5
- keys: bfloat16 [4096, 1024], P(('outer', 'inner'), 'head'), may hold values from -5.5 to 5.5
- values: bfloat16 [4096, 1024], P(('outer', 'inner'), 'head'), may hold values from -6 to 6
- output_cotangent: bfloat16 [4096, 8192], P(('outer', 'inner'), 'head'), may hold values from -6 to 6
- positions: int32 [4096], P(('outer', 'inner')), may hold values from 0 to 4095, as said below
Outputs:
- attn_out: bfloat16 [4096, 8192], P(('outer', 'inner'), 'head')
- grad_queries: bfloat16 [4096, 8192], P(('outer', 'inner'), 'head')
- key_gradient: bfloat16 [4096, 1024], P(('outer', 'inner'), 'head')
- value_gradient: bfloat16 [4096, 1024], P(('outer', 'inner'), 'head')
Inputs may be any that keep to these rules, and one draw needn't show every extreme that they name: The 128 positions of each index of outer+inner are two runs of 64 consecutive ascending positions, each starting at a multiple of 64; all 4096 together are a permutation.
All inputs are finite; a program needn't handle non-finite values.
Results may differ from a plain program's by a relative error of at most 0.039.
Values may be sent and summed in bfloat16 or wider, within the bound.
No kernel may reach another device: no remote copies, remote signals or barrier semaphores. Data moves between devices by JAX's collectives and lax.ppermute only.
A program may use at most 64 MiB of HBM per device.

v0:
```python
import functools
import math

import jax
import jax.numpy as jnp
from jax import lax
from jax.experimental import pallas as pl
from jax.experimental.pallas import tpu as pltpu
from jax.sharding import PartitionSpec as P

HEAD = 128
HEADS = 8
RUN = 64
ROWS = RUN * HEADS
TOK = 128
TAIL = 16
SIDE = 4
BLOCKS = 64
CHUNK = 1024
SCALE = HEAD**-0.5
SCALE2 = SCALE * math.log2(math.e)
NEG = -1e30

bf16 = jnp.bfloat16
f32 = jnp.float32


def dot(a, b):
    return lax.dot_general(a, b, (((1,), (0,)), ((), ())), preferred_element_type=f32)


def attention_kernel(*refs):
    own_ref, q_ref, do_ref = refs[:3]
    kv_refs = refs[3:11]
    out_ref, gq_ref = refs[11:13]
    dkv_refs = refs[13:21]
    (ids_v, ids_s, sem, ka, va, kt, vt, qn, qt, don, dot_t, sbuf, wbuf, dka, dva) = refs[21:]
    tokens = BLOCKS * RUN
    step = TOK + TAIL
    lane = lax.broadcasted_iota(jnp.int32, (RUN, HEAD), 1)
    sub = lax.broadcasted_iota(jnp.int32, (RUN, HEAD), 0)
    diff = jnp.where(lane < RUN, sub - lane, -(1 << 30))

    for part in range(8):
        for unit in range(SIDE):
            tail = kv_refs[part][unit * step + TOK : (unit + 1) * step, 0:HEAD]
            row = part * SIDE + unit
            ids_v[row : row + 1, :] = tail.astype(f32)[0:1, :].astype(jnp.int32)
    fetch = pltpu.make_async_copy(ids_v, ids_s, sem)
    fetch.start()
    fetch.wait()

    for part in range(8):
        for unit in range(SIDE):
            for run in range(2):
                where = ids_s[part * SIDE + unit, run]
                place = pl.ds(pl.multiple_of(where * RUN, RUN), RUN)
                first = unit * step + run * RUN
                ka[place, 0:HEAD] = kv_refs[part][first : first + RUN, 0:HEAD]
                va[place, 0:HEAD] = kv_refs[part][first : first + RUN, HEAD : 2 * HEAD]
    ones3 = jnp.where(lax.broadcasted_iota(jnp.int32, (CHUNK, HEAD), 1) < 3, 1.0, 0.0).astype(bf16)
    ones1 = jnp.where(lax.broadcasted_iota(jnp.int32, (TAIL, CHUNK), 0) < 1, 1.0, 0.0).astype(bf16)

    @pl.loop(0, tokens // CHUNK)
    def _(c):
        s = pl.ds(pl.multiple_of(c * CHUNK, CHUNK), CHUNK)
        va[s, HEAD : 2 * HEAD] = ones3
        kt[:, s] = jnp.transpose(ka[s, 0:HEAD])
        vt[0:HEAD, s] = jnp.transpose(va[s, 0:HEAD])
        vt[HEAD : HEAD + TAIL, s] = ones1
        dka[s, :] = jnp.zeros((CHUNK, HEAD), f32)
        dva[s, :] = jnp.zeros((CHUNK, HEAD), f32)

    token_of = lax.broadcasted_iota(jnp.int32, (HEAD, ROWS), 1) & (RUN - 1)
    depth_of = lax.broadcasted_iota(jnp.int32, (HEAD, ROWS), 0)
    qt[HEAD : 2 * HEAD, :] = jnp.where(token_of == depth_of, 1.0, 0.0).astype(bf16)

    @pl.loop(0, 4)
    def _(a):
        position = own_ref[a]
        turns = position * RUN // CHUNK + 1
        rows = pl.ds(pl.multiple_of(a * RUN, RUN), RUN)
        for h in range(HEADS):
            qn[h * RUN : (h + 1) * RUN, :] = q_ref[rows, h * HEAD : (h + 1) * HEAD]
            don[h * RUN : (h + 1) * RUN, :] = do_ref[rows, h * HEAD : (h + 1) * HEAD]
        qt[0:HEAD, :] = jnp.transpose(qn[...])

        def score_turn(c, largest):
            base = pl.multiple_of(c * CHUNK, CHUNK)
            for j in range(CHUNK // RUN):
                limit = (position - c * (CHUNK // RUN) - j) * RUN
                place = pl.ds(pl.multiple_of(base + j * RUN, RUN), RUN)
                ka[place, HEAD : 2 * HEAD] = jnp.where(diff <= limit, 0.0, NEG).astype(bf16)
            scores = dot(ka[pl.ds(base, CHUNK), :], qt[...]) * SCALE2
            sbuf[pl.ds(base, CHUNK), :] = scores
            return jnp.maximum(largest, jnp.max(scores.reshape(CHUNK // 8, 8, ROWS), axis=0))

        largest = lax.fori_loop(0, turns, score_turn, jnp.full((8, ROWS), NEG, f32))
        row_max = jnp.max(largest, axis=0, keepdims=True)

        def weight_turn(c, mixed):
            s = pl.ds(pl.multiple_of(c * CHUNK, CHUNK), CHUNK)
            weights = jnp.exp2(sbuf[s, :] - row_max).astype(bf16)
            wbuf[s, :] = weights
            return mixed + dot(vt[:, s], weights)

        mixed = lax.fori_loop(0, turns, weight_turn, jnp.zeros((HEAD + TAIL, ROWS), f32))
        inverse = 1.0 / mixed[HEAD : HEAD + 1, :]
        out_t = (mixed[0:HEAD, :] * inverse).astype(bf16)
        out_n = jnp.transpose(out_t)
        do_t = (jnp.transpose(don[...]).astype(f32) * inverse).astype(bf16)
        don[...] = jnp.transpose(do_t)
        delta = -jnp.sum(do_t.astype(f32) * out_t.astype(f32), axis=0, keepdims=True)
        high = delta.astype(bf16).astype(f32)
        middle = (delta - high).astype(bf16).astype(f32)
        low = delta - high - middle
        dot_t[0:HEAD, :] = do_t
        dot_t[HEAD : 2 * HEAD, :] = jnp.where(
            depth_of == 0,
            high,
            jnp.where(depth_of == 1, middle, jnp.where(depth_of == 2, low, 0.0)),
        ).astype(bf16)
        for h in range(HEADS):
            out_ref[rows, h * HEAD : (h + 1) * HEAD] = out_n[h * RUN : (h + 1) * RUN, :]

        def gradient_turn(c, grad_q):
            s = pl.ds(pl.multiple_of(c * CHUNK, CHUNK), CHUNK)
            weights = wbuf[s, :]
            dscore = weights * dot(va[s, :], dot_t[...]).astype(bf16)
            dva[s, :] += dot(weights, don[...])
            dka[s, :] += dot(dscore, qn[...])
            return grad_q + dot(kt[:, s], dscore)

        grad_q = lax.fori_loop(0, turns, gradient_turn, jnp.zeros((HEAD, ROWS), f32))
        grad_n = jnp.transpose((grad_q * SCALE).astype(bf16))
        for h in range(HEADS):
            gq_ref[rows, h * HEAD : (h + 1) * HEAD] = grad_n[h * RUN : (h + 1) * RUN, :]

    for part in range(8):
        for unit in range(SIDE):
            for run in range(2):
                where = ids_s[part * SIDE + unit, run]
                place = pl.ds(pl.multiple_of(where * RUN, RUN), RUN)
                first = unit * TOK + run * RUN
                dkv_refs[part][first : first + RUN, 0:HEAD] = (dka[place, :] * SCALE).astype(bf16)
                dkv_refs[part][first : first + RUN, HEAD : 2 * HEAD] = dva[place, :].astype(bf16)


def attention(own, q, do, kv):
    vmem = pl.BlockSpec(memory_space=pltpu.VMEM)
    smem = pl.BlockSpec(memory_space=pltpu.SMEM)
    tokens = BLOCKS * RUN
    wide = jax.ShapeDtypeStruct(q.shape, bf16)
    part = jax.ShapeDtypeStruct((SIDE * TOK, 2 * HEAD), bf16)
    return pl.pallas_call(
        attention_kernel,
        out_shape=(wide, wide) + (part,) * 8,
        in_specs=[smem] + [vmem] * 10,
        out_specs=(vmem,) * 10,
        scratch_shapes=[
            pltpu.VMEM((32, HEAD), jnp.int32),
            pltpu.SMEM((32, HEAD), jnp.int32),
            pltpu.SemaphoreType.DMA,
            pltpu.VMEM((tokens, 2 * HEAD), bf16),
            pltpu.VMEM((tokens, 2 * HEAD), bf16),
            pltpu.VMEM((HEAD, tokens), bf16),
            pltpu.VMEM((HEAD + TAIL, tokens), bf16),
            pltpu.VMEM((ROWS, HEAD), bf16),
            pltpu.VMEM((2 * HEAD, ROWS), bf16),
            pltpu.VMEM((ROWS, HEAD), bf16),
            pltpu.VMEM((2 * HEAD, ROWS), bf16),
            pltpu.VMEM((tokens, ROWS), f32),
            pltpu.VMEM((tokens, ROWS), bf16),
            pltpu.VMEM((tokens, HEAD), f32),
            pltpu.VMEM((tokens, HEAD), f32),
        ],
        compiler_params=pltpu.CompilerParams(vmem_limit_bytes=56 * 2**20),
        name="attention",
    )(own, q, do, *kv)


def swap(x):
    return lax.ppermute(x, "outer", [(0, 1), (1, 0)])


def shift(x, dz, dy):
    pairs = [
        (z * SIDE + y, (z + dz) % SIDE * SIDE + (y + dy) % SIDE)
        for z in range(SIDE)
        for y in range(SIDE)
    ]
    return lax.ppermute(x, "inner", pairs)


def body(queries, keys, values, output_cotangent, positions):
    core = lax.axis_index("outer")

    def halves(x):
        width = x.shape[1] // 2
        first, second = x[:, :width], x[:, width:]
        mine = jnp.where(core == 0, first, second)
        other = jnp.where(core == 0, second, first)
        return mine, other

    keys_mine, keys_other = halves(keys)
    values_mine, values_other = halves(values)
    own_ids = positions.reshape(2, RUN)[:, 0] // RUN
    tail = jnp.zeros((TAIL, 2 * HEAD), bf16).at[0, 0:2].set(own_ids.astype(bf16))
    kv_mine = jnp.concatenate([jnp.concatenate([keys_mine, values_mine], 1), tail], 0)
    kv_other = swap(jnp.concatenate([jnp.concatenate([keys_other, values_other], 1), tail], 0))
    q_mine, q_other = halves(queries)
    do_mine, do_other = halves(output_cotangent)
    q_other = swap(q_other)
    do_other = swap(do_other)

    def along_y(x, d):
        return shift(x, 0, d)

    def along_z(x, d):
        return shift(x, d, 0)

    def gather(x, first, second):
        line = jnp.concatenate([x] + [first(x, d) for d in range(1, SIDE)], 0)
        return [line] + [second(line, d) for d in range(1, SIDE)]

    kv = gather(kv_mine, along_y, along_z) + gather(kv_other, along_z, along_y)
    q = jnp.concatenate([q_mine, q_other], 0)
    do = jnp.concatenate([do_mine, do_other], 0)
    partner_ids = kv_other[TOK, 0:2].astype(jnp.int32)
    own = jnp.concatenate([own_ids, partner_ids])

    results = attention(own, q, do, kv)
    out, grad_q = results[:2]
    parts = results[2:]

    def total(terms):
        return functools.reduce(jnp.add, [t.astype(f32) for t in terms]).astype(bf16)

    def scatter(lines, first, second):
        line = total([lines[0]] + [second(lines[d], -d) for d in range(1, SIDE)])
        units = [line[d * TOK : (d + 1) * TOK] for d in range(SIDE)]
        return total([units[0]] + [first(units[d], -d) for d in range(1, SIDE)])

    dkv_mine = scatter(parts[:4], along_y, along_z)
    dkv_other = swap(scatter(parts[4:], along_z, along_y))

    def join(mine, other):
        return jnp.where(
            core == 0, jnp.concatenate([mine, other], 1), jnp.concatenate([other, mine], 1)
        )

    attn_out = join(out[:TOK], swap(out[TOK:]))
    grad_queries = join(grad_q[:TOK], swap(grad_q[TOK:]))
    key_gradient = join(dkv_mine[:, :HEAD], dkv_other[:, :HEAD])
    value_gradient = join(dkv_mine[:, HEAD:], dkv_other[:, HEAD:])
    return attn_out, grad_queries, key_gradient, value_gradient


def solution(mesh):
    tokens = ("outer", "inner")
    split = P(tokens, "head")
    return jax.shard_map(
        body,
        mesh=mesh,
        in_specs=(split, split, split, split, P(tokens)),
        out_specs=(split, split, split, split),
        check_vma=False,
    )
```

profile of v0, /device:TPU:1, one launch (start us, length us, event | category | flops | bytes accessed | tf_op | source)
XLA Modules:
  0.0 134.7 jit_solution(14499225533917911582)
XLA Ops:
  3.2 3.6 %collective-permute-start.5 = (bf16[144,256]{1,0:T(8,128)(2,1)S(1)}, bf16[144,256]{1,0:T(8,128)(2,1)S(1)}, u32[]{:S(2)}, u32[]{:S(2)}) collective-permute-start(bf16[144,256]{1,0:T(8,128)(2,1)S(1)} %get-tuple-element.58), channel_id=1, source_target_pairs={{0,12},{4,0},{8,4},{12,8},{16,28},{20,16},{24,20},{28,24},{32,44},... | collective-permute-start | bytes 221192 | tf_op jit(solution)/shard_map/ppermute | solution.py:192
  7.9 1.5 %collective-permute-start = (bf16[144,256]{1,0:T(8,128)(2,1)S(1)}, bf16[144,256]{1,0:T(8,128)(2,1)S(1)}, u32[]{:S(2)}, u32[]{:S(2)}) collective-permute-start(bf16[144,256]{1,0:T(8,128)(2,1)S(1)} %get-tuple-element.59), channel_id=1, source_target_pairs={{0,64},{64,0},{1,65},{65,1},{2,66},{66,2},{3,67},{67,3},{4,68},{68... | collective-permute-start | bytes 221192 | tf_op jit(solution)/shard_map/ppermute | solution.py:183
  9.6 3.1 %collective-permute-done.3 = bf16[144,256]{1,0:T(8,128)(2,1)S(1)} collective-permute-done((bf16[144,256]{1,0:T(8,128)(2,1)S(1)}, bf16[144,256]{1,0:T(8,128)(2,1)S(1)}, u32[]{:S(2)}, u32[]{:S(2)}) %collective-permute-start.3) | collective-permute-done | bytes 73760 | tf_op jit(solution)/shard_map/ppermute | solution.py:192
  12.7 1.9 %collective-permute-start.2 = (bf16[128,1024]{1,0:T(8,128)(2,1)S(1)}, bf16[128,1024]{1,0:T(8,128)(2,1)S(1)}, u32[]{:S(2)}, u32[]{:S(2)}) collective-permute-start(bf16[128,1024]{1,0:T(8,128)(2,1)S(1)} %get-tuple-element.41), channel_id=1, source_target_pairs={{0,64},{64,0},{1,65},{65,1},{2,66},{66,2},{3,67},{67,3},{4,68},{68... | collective-permute-start | bytes 786440 | tf_op jit(solution)/shard_map/ppermute | solution.py:183
  14.7 3.8 %collective-permute-start.8 = (bf16[576,256]{1,0:T(8,128)(2,1)S(1)}, bf16[576,256]{1,0:T(8,128)(2,1)S(1)}, u32[]{:S(2)}, u32[]{:S(2)}) collective-permute-start(bf16[576,256]{1,0:T(8,128)(2,1)S(1)} %constant_dynamic-update-slice_fusion.refs_3_), channel_id=1, source_target_pairs={{0,48},{4,52},{8,56},{12,60},{16,0},{20,4},{24,8},{28,12},{32,16},... | collective-permute-start | bytes 884744 | tf_op jit(solution)/shard_map/ppermute | solution.py:192
  19.2 10.9 %collective-permute-done.9 = bf16[144,256]{1,0:T(8,128)(2,1)S(1)} collective-permute-done((bf16[144,256]{1,0:T(8,128)(2,1)S(1)}, bf16[144,256]{1,0:T(8,128)(2,1)S(1)}, u32[]{:S(2)}, u32[]{:S(2)}) %collective-permute-start.9) | collective-permute-done | bytes 73760 | tf_op jit(solution)/shard_map/ppermute | solution.py:192
  30.5 4.3 %collective-permute-done.10 = bf16[144,256]{1,0:T(8,128)(2,1)S(1)} collective-permute-done((bf16[144,256]{1,0:T(8,128)(2,1)S(1)}, bf16[144,256]{1,0:T(8,128)(2,1)S(1)}, u32[]{:S(2)}, u32[]{:S(2)}) %collective-permute-start.10) | collective-permute-done | bytes 73760 | tf_op jit(solution)/shard_map/ppermute | solution.py:192
  35.0 3.0 %collective-permute-done.11 = bf16[144,256]{1,0:T(8,128)(2,1)S(1)} collective-permute-done((bf16[144,256]{1,0:T(8,128)(2,1)S(1)}, bf16[144,256]{1,0:T(8,128)(2,1)S(1)}, u32[]{:S(2)}, u32[]{:S(2)}) %collective-permute-start.11) | collective-permute-done | bytes 73760 | tf_op jit(solution)/shard_map/ppermute | solution.py:192
  42.0 2.8 %collective-permute-done.6.refs_4_ = bf16[576,256]{1,0:T(8,128)(2,1)S(1)} collective-permute-done((bf16[576,256]{1,0:T(8,128)(2,1)S(1)}, bf16[576,256]{1,0:T(8,128)(2,1)S(1)}, u32[]{:S(2)}, u32[]{:S(2)}) %collective-permute-start.6) | collective-permute-done | bytes 294944 | tf_op jit(solution)/shard_map/ppermute | solution.py:192
  45.6 8.7 %collective-permute-done.12.refs_8_ = bf16[576,256]{1,0:T(8,128)(2,1)S(1)} collective-permute-done((bf16[576,256]{1,0:T(8,128)(2,1)S(1)}, bf16[576,256]{1,0:T(8,128)(2,1)S(1)}, u32[]{:S(2)}, u32[]{:S(2)}) %collective-permute-start.12) | collective-permute-done | bytes 294944 | tf_op jit(solution)/shard_map/ppermute | solution.py:192
  55.0 27.0 %attention.1 = (bf16[256,1024]{1,0:T(8,128)(2,1)}, bf16[256,1024]{1,0:T(8,128)(2,1)}, bf16[512,256]{1,0:T(8,128)(2,1)}, bf16[512,256]{1,0:T(8,128)(2,1)}, bf16[5...) custom-call(s32[4]{0:T(128)} %pad_add_fusion.refs_0_, ...), custom_call_target="tpu_custom_call" | custom-call | tf_op jit(solution)/shard_map/attention/pallas_call | solution.py:155
  82.0 13.0 %collective-permute-start.17 = (bf16[512,256]{1,0:T(8,128)(2,1)}, bf16[512,256]{1,0:T(8,128)(2,1)S(1)}, u32[]{:S(2)}, u32[]{:S(2)}) collective-permute-start(bf16[512,256]{1,0:T(8,128)(2,1)} %get-tuple-element.29), channel_id=1, source_target_pairs={{0,48},{4,52},{8,56},{12,60},{16,0},{20,4},{24,8},{28,12},{32,16},... | collective-permute-start | bytes 786440 | tf_op jit(solution)/shard_map/ppermute | solution.py:192
  95.7 1.1 fusion.3
  96.8 2.3 %collective-permute-start.15 = (bf16[128,1024]{1,0:T(8,128)(2,1)S(1)}, bf16[128,1024]{1,0:T(8,128)(2,1)S(1)}, u32[]{:S(2)}, u32[]{:S(2)}) collective-permute-start(bf16[128,1024]{1,0:T(8,128)(2,1)S(1)} %get-tuple-element.39), channel_id=1, source_target_pairs={{0,64},{64,0},{1,65},{65,1},{2,66},{66,2},{3,67},{67,3},{4,68},{68... | collective-permute-start | bytes 786440 | tf_op jit(solution)/shard_map/ppermute | solution.py:183
  99.2 7.3 %collective-permute-done.17 = bf16[512,256]{1,0:T(8,128)(2,1)S(1)} collective-permute-done((bf16[512,256]{1,0:T(8,128)(2,1)}, bf16[512,256]{1,0:T(8,128)(2,1)S(1)}, u32[]{:S(2)}, u32[]{:S(2)}) %collective-permute-start.17) | collective-permute-done | bytes 262176 | tf_op jit(solution)/shard_map/ppermute | solution.py:192
  106.6 3.3 %collective-permute-done.19 = bf16[512,256]{1,0:T(8,128)(2,1)S(1)} collective-permute-done((bf16[512,256]{1,0:T(8,128)(2,1)}, bf16[512,256]{1,0:T(8,128)(2,1)S(1)}, u32[]{:S(2)}, u32[]{:S(2)}) %collective-permute-start.19) | collective-permute-done | bytes 262176 | tf_op jit(solution)/shard_map/ppermute | solution.py:192
  111.3 3.7 %collective-permute-done.24 = bf16[512,256]{1,0:T(8,128)(2,1)S(1)} collective-permute-done((bf16[512,256]{1,0:T(8,128)(2,1)S(1)}, bf16[512,256]{1,0:T(8,128)(2,1)S(1)}, u32[]{:S(2)}, u32[]{:S(2)}) %collective-permute-start.24) | collective-permute-done | bytes 262176 | tf_op jit(solution)/shard_map/ppermute | solution.py:192
  115.0 6.5 %collective-permute-done.25 = bf16[512,256]{1,0:T(8,128)(2,1)S(1)} collective-permute-done((bf16[512,256]{1,0:T(8,128)(2,1)S(1)}, bf16[512,256]{1,0:T(8,128)(2,1)S(1)}, u32[]{:S(2)}, u32[]{:S(2)}) %collective-permute-start.25) | collective-permute-done | bytes 262176 | tf_op jit(solution)/shard_map/ppermute | solution.py:192
  121.6 3.4 %collective-permute-start.26 = (bf16[128,256]{1,0:T(8,128)(2,1)S(1)}, bf16[128,256]{1,0:T(8,128)(2,1)S(1)}, u32[]{:S(2)}, u32[]{:S(2)}) collective-permute-start(bf16[128,256]{1,0:T(8,128)(2,1)S(1)} %get-tuple-element.47), channel_id=1, source_target_pairs={{0,48},{4,52},{8,56},{12,60},{16,0},{20,4},{24,8},{28,12},{32,16},... | collective-permute-start | bytes 196616 | tf_op jit(solution)/shard_map/ppermute | solution.py:192
  125.0 0.9 maximum_select_fusion
  125.9 1.3 collective-permute-start.27
  127.2 0.9 maximum_select_fusion.1
  129.3 1.2 collective-permute-done.27
  130.6 2.5 %collective-permute-start.29 = (bf16[128,256]{1,0:T(8,128)(2,1)S(1)}, bf16[128,256]{1,0:T(8,128)(2,1)S(1)}, u32[]{:S(2)}, u32[]{:S(2)}) collective-permute-start(bf16[128,256]{1,0:T(8,128)(2,1)S(1)} %add_convert_fusion.2), channel_id=1, source_target_pairs={{0,64},{64,0},{1,65},{65,1},{2,66},{66,2},{3,67},{67,3},{4,68},{68... | collective-permute-start | bytes 196616 | tf_op jit(solution)/shard_map/ppermute | solution.py:183
  (104 shorter events, 15.8 us)
Async XLA Ops:
  3.2 11.4 %collective-permute-start.5 = (bf16[144,256]{1,0:T(8,128)(2,1)S(1)}, bf16[144,256]{1,0:T(8,128)(2,1)S(1)}, u32[]{:S(2)}, u32[]{:S(2)}) collective-permute-start(bf16[144,256]{1,0:T(8,128)(2,1)S(1)} %get-tuple-element.58), channel_id=1, source_target_pairs={{0,12},{4,0},{8,4},{12,8},{16,28},{20,16},{24,20},{28,24},{32,44},... | collective-permute-start | bytes 221192 | tf_op jit(solution)/shard_map/ppermute | solution.py:192
  6.8 7.8 %collective-permute-start.4 = (bf16[144,256]{1,0:T(8,128)(2,1)S(1)}, bf16[144,256]{1,0:T(8,128)(2,1)S(1)}, u32[]{:S(2)}, u32[]{:S(2)}) collective-permute-start(bf16[144,256]{1,0:T(8,128)(2,1)S(1)} %get-tuple-element.58), channel_id=1, source_target_pairs={{0,8},{4,12},{8,0},{12,4},{16,24},{20,28},{24,16},{28,20},{32,40},... | collective-permute-start | bytes 221192 | tf_op jit(solution)/shard_map/ppermute | solution.py:192
  7.2 5.6 %collective-permute-start.3 = (bf16[144,256]{1,0:T(8,128)(2,1)S(1)}, bf16[144,256]{1,0:T(8,128)(2,1)S(1)}, u32[]{:S(2)}, u32[]{:S(2)}) collective-permute-start(bf16[144,256]{1,0:T(8,128)(2,1)S(1)} %get-tuple-element.58), channel_id=1, source_target_pairs={{0,4},{4,8},{8,12},{12,0},{16,20},{20,24},{24,28},{28,16},{32,36},... | collective-permute-start | bytes 221192 | tf_op jit(solution)/shard_map/ppermute | solution.py:192
  7.9 10.6 %collective-permute-start = (bf16[144,256]{1,0:T(8,128)(2,1)S(1)}, bf16[144,256]{1,0:T(8,128)(2,1)S(1)}, u32[]{:S(2)}, u32[]{:S(2)}) collective-permute-start(bf16[144,256]{1,0:T(8,128)(2,1)S(1)} %get-tuple-element.59), channel_id=1, source_target_pairs={{0,64},{64,0},{1,65},{65,1},{2,66},{66,2},{3,67},{67,3},{4,68},{68... | collective-permute-start | bytes 221192 | tf_op jit(solution)/shard_map/ppermute | solution.py:183
  9.4 28.6 %collective-permute-start.1 = (bf16[128,1024]{1,0:T(8,128)(2,1)S(1)}, bf16[128,1024]{1,0:T(8,128)(2,1)S(1)}, u32[]{:S(2)}, u32[]{:S(2)}) collective-permute-start(bf16[128,1024]{1,0:T(8,128)(2,1)S(1)} %get-tuple-element.43), channel_id=1, source_target_pairs={{0,64},{64,0},{1,65},{65,1},{2,66},{66,2},{3,67},{67,3},{4,68},{68... | collective-permute-start | bytes 786440 | tf_op jit(solution)/shard_map/ppermute | solution.py:183
  12.7 25.7 %collective-permute-start.2 = (bf16[128,1024]{1,0:T(8,128)(2,1)S(1)}, bf16[128,1024]{1,0:T(8,128)(2,1)S(1)}, u32[]{:S(2)}, u32[]{:S(2)}) collective-permute-start(bf16[128,1024]{1,0:T(8,128)(2,1)S(1)} %get-tuple-element.41), channel_id=1, source_target_pairs={{0,64},{64,0},{1,65},{65,1},{2,66},{66,2},{3,67},{67,3},{4,68},{68... | collective-permute-start | bytes 786440 | tf_op jit(solution)/shard_map/ppermute | solution.py:183
  14.7 24.3 %collective-permute-start.8 = (bf16[576,256]{1,0:T(8,128)(2,1)S(1)}, bf16[576,256]{1,0:T(8,128)(2,1)S(1)}, u32[]{:S(2)}, u32[]{:S(2)}) collective-permute-start(bf16[576,256]{1,0:T(8,128)(2,1)S(1)} %constant_dynamic-update-slice_fusion.refs_3_), channel_id=1, source_target_pairs={{0,48},{4,52},{8,56},{12,60},{16,0},{20,4},{24,8},{28,12},{32,16},... | collective-permute-start | bytes 884744 | tf_op jit(solution)/shard_map/ppermute | solution.py:192
  18.5 23.5 %collective-permute-start.7 = (bf16[576,256]{1,0:T(8,128)(2,1)S(1)}, bf16[576,256]{1,0:T(8,128)(2,1)S(1)}, u32[]{:S(2)}, u32[]{:S(2)}) collective-permute-start(bf16[576,256]{1,0:T(8,128)(2,1)S(1)} %constant_dynamic-update-slice_fusion.refs_3_), channel_id=1, source_target_pairs={{0,32},{4,36},{8,40},{12,44},{16,48},{20,52},{24,56},{28,60},{32,0... | collective-permute-start | bytes 884744 | tf_op jit(solution)/shard_map/ppermute | solution.py:192
  18.5 11.6 %collective-permute-start.9 = (bf16[144,256]{1,0:T(8,128)(2,1)S(1)}, bf16[144,256]{1,0:T(8,128)(2,1)S(1)}, u32[]{:S(2)}, u32[]{:S(2)}) collective-permute-start(bf16[144,256]{1,0:T(8,128)(2,1)S(1)} %collective-permute-done), channel_id=1, source_target_pairs={{0,16},{4,20},{8,24},{12,28},{16,32},{20,36},{24,40},{28,44},{32,4... | collective-permute-start | bytes 221192 | tf_op jit(solution)/shard_map/ppermute | solution.py:192
  38.0 6.8 %collective-permute-start.6 = (bf16[576,256]{1,0:T(8,128)(2,1)S(1)}, bf16[576,256]{1,0:T(8,128)(2,1)S(1)}, u32[]{:S(2)}, u32[]{:S(2)}) collective-permute-start(bf16[576,256]{1,0:T(8,128)(2,1)S(1)} %constant_dynamic-update-slice_fusion.refs_3_), channel_id=1, source_target_pairs={{0,16},{4,20},{8,24},{12,28},{16,32},{20,36},{24,40},{28,44},{32,4... | collective-permute-start | bytes 884744 | tf_op jit(solution)/shard_map/ppermute | solution.py:192
  38.0 6.7 %collective-permute-start.14 = (bf16[576,256]{1,0:T(8,128)(2,1)S(1)}, bf16[576,256]{1,0:T(8,128)(2,1)S(1)}, u32[]{:S(2)}, u32[]{:S(2)}) collective-permute-start(bf16[576,256]{1,0:T(8,128)(2,1)S(1)} %constant_dynamic-update-slice_fusion.4.refs_7_), channel_id=1, source_target_pairs={{0,12},{4,0},{8,4},{12,8},{16,28},{20,16},{24,20},{28,24},{32,44},... | collective-permute-start | bytes 884744 | tf_op jit(solution)/shard_map/ppermute | solution.py:192
  38.4 7.2 %collective-permute-start.13 = (bf16[576,256]{1,0:T(8,128)(2,1)S(1)}, bf16[576,256]{1,0:T(8,128)(2,1)S(1)}, u32[]{:S(2)}, u32[]{:S(2)}) collective-permute-start(bf16[576,256]{1,0:T(8,128)(2,1)S(1)} %constant_dynamic-update-slice_fusion.4.refs_7_), channel_id=1, source_target_pairs={{0,8},{4,12},{8,0},{12,4},{16,24},{20,28},{24,16},{28,20},{32,40},... | collective-permute-start | bytes 884744 | tf_op jit(solution)/shard_map/ppermute | solution.py:192
  39.0 15.2 %collective-permute-start.12 = (bf16[576,256]{1,0:T(8,128)(2,1)S(1)}, bf16[576,256]{1,0:T(8,128)(2,1)S(1)}, u32[]{:S(2)}, u32[]{:S(2)}) collective-permute-start(bf16[576,256]{1,0:T(8,128)(2,1)S(1)} %constant_dynamic-update-slice_fusion.4.refs_7_), channel_id=1, source_target_pairs={{0,4},{4,8},{8,12},{12,0},{16,20},{20,24},{24,28},{28,16},{32,36},... | collective-permute-start | bytes 884744 | tf_op jit(solution)/shard_map/ppermute | solution.py:192
  82.0 24.6 %collective-permute-start.17 = (bf16[512,256]{1,0:T(8,128)(2,1)}, bf16[512,256]{1,0:T(8,128)(2,1)S(1)}, u32[]{:S(2)}, u32[]{:S(2)}) collective-permute-start(bf16[512,256]{1,0:T(8,128)(2,1)} %get-tuple-element.29), channel_id=1, source_target_pairs={{0,48},{4,52},{8,56},{12,60},{16,0},{20,4},{24,8},{28,12},{32,16},... | collective-permute-start | bytes 786440 | tf_op jit(solution)/shard_map/ppermute | solution.py:192
  95.0 11.5 %collective-permute-start.18 = (bf16[512,256]{1,0:T(8,128)(2,1)}, bf16[512,256]{1,0:T(8,128)(2,1)S(1)}, u32[]{:S(2)}, u32[]{:S(2)}) collective-permute-start(bf16[512,256]{1,0:T(8,128)(2,1)} %get-tuple-element.30), channel_id=1, source_target_pairs={{0,32},{4,36},{8,40},{12,44},{16,48},{20,52},{24,56},{28,60},{32,0... | collective-permute-start | bytes 786440 | tf_op jit(solution)/shard_map/ppermute | solution.py:192
  95.0 14.9 %collective-permute-start.19 = (bf16[512,256]{1,0:T(8,128)(2,1)}, bf16[512,256]{1,0:T(8,128)(2,1)S(1)}, u32[]{:S(2)}, u32[]{:S(2)}) collective-permute-start(bf16[512,256]{1,0:T(8,128)(2,1)} %get-tuple-element.31), channel_id=1, source_target_pairs={{0,16},{4,20},{8,24},{12,28},{16,32},{20,36},{24,40},{28,44},{32,4... | collective-permute-start | bytes 786440 | tf_op jit(solution)/shard_map/ppermute | solution.py:192
  96.8 28.2 %collective-permute-start.15 = (bf16[128,1024]{1,0:T(8,128)(2,1)S(1)}, bf16[128,1024]{1,0:T(8,128)(2,1)S(1)}, u32[]{:S(2)}, u32[]{:S(2)}) collective-permute-start(bf16[128,1024]{1,0:T(8,128)(2,1)S(1)} %get-tuple-element.39), channel_id=1, source_target_pairs={{0,64},{64,0},{1,65},{65,1},{2,66},{66,2},{3,67},{67,3},{4,68},{68... | collective-permute-start | bytes 786440 | tf_op jit(solution)/shard_map/ppermute | solution.py:183
  99.1 11.8 %collective-permute-start.23 = (bf16[512,256]{1,0:T(8,128)(2,1)S(1)}, bf16[512,256]{1,0:T(8,128)(2,1)S(1)}, u32[]{:S(2)}, u32[]{:S(2)}) collective-permute-start(bf16[512,256]{1,0:T(8,128)(2,1)S(1)} %copy-done.15), channel_id=1, source_target_pairs={{0,12},{4,0},{8,4},{12,8},{16,28},{20,16},{24,20},{28,24},{32,44},... | collective-permute-start | bytes 786440 | tf_op jit(solution)/shard_map/ppermute | solution.py:192
  106.5 8.5 %collective-permute-start.24 = (bf16[512,256]{1,0:T(8,128)(2,1)S(1)}, bf16[512,256]{1,0:T(8,128)(2,1)S(1)}, u32[]{:S(2)}, u32[]{:S(2)}) collective-permute-start(bf16[512,256]{1,0:T(8,128)(2,1)S(1)} %copy-done.14), channel_id=1, source_target_pairs={{0,8},{4,12},{8,0},{12,4},{16,24},{20,28},{24,16},{28,20},{32,40},... | collective-permute-start | bytes 786440 | tf_op jit(solution)/shard_map/ppermute | solution.py:192
  106.5 14.9 %collective-permute-start.25 = (bf16[512,256]{1,0:T(8,128)(2,1)S(1)}, bf16[512,256]{1,0:T(8,128)(2,1)S(1)}, u32[]{:S(2)}, u32[]{:S(2)}) collective-permute-start(bf16[512,256]{1,0:T(8,128)(2,1)S(1)} %copy-done.13), channel_id=1, source_target_pairs={{0,4},{4,8},{8,12},{12,0},{16,20},{20,24},{24,28},{28,16},{32,36},... | collective-permute-start | bytes 786440 | tf_op jit(solution)/shard_map/ppermute | solution.py:192
  109.9 16.0 %collective-permute-start.16 = (bf16[128,1024]{1,0:T(8,128)(2,1)S(1)}, bf16[128,1024]{1,0:T(8,128)(2,1)S(1)}, u32[]{:S(2)}, u32[]{:S(2)}) collective-permute-start(bf16[128,1024]{1,0:T(8,128)(2,1)S(1)} %get-tuple-element.37), channel_id=1, source_target_pairs={{0,64},{64,0},{1,65},{65,1},{2,66},{66,2},{3,67},{67,3},{4,68},{68... | collective-permute-start | bytes 786440 | tf_op jit(solution)/shard_map/ppermute | solution.py:183
  111.0 22.1 %collective-permute-start.20 = (bf16[128,256]{1,0:T(8,128)(2,1)S(1)}, bf16[128,256]{1,0:T(8,128)(2,1)S(1)}, u32[]{:S(2)}, u32[]{:S(2)}) collective-permute-start(bf16[128,256]{1,0:T(8,128)(2,1)S(1)} %get-tuple-element.44), channel_id=1, source_target_pairs={{0,12},{4,0},{8,4},{12,8},{16,28},{20,16},{24,20},{28,24},{32,44},... | collective-permute-start | bytes 196616 | tf_op jit(solution)/shard_map/ppermute | solution.py:192
  115.0 18.1 %collective-permute-start.22 = (bf16[128,256]{1,0:T(8,128)(2,1)S(1)}, bf16[128,256]{1,0:T(8,128)(2,1)S(1)}, u32[]{:S(2)}, u32[]{:S(2)}) collective-permute-start(bf16[128,256]{1,0:T(8,128)(2,1)S(1)} %get-tuple-element.45), channel_id=1, source_target_pairs={{0,4},{4,8},{8,12},{12,0},{16,20},{20,24},{24,28},{28,16},{32,36},... | collective-permute-start | bytes 196616 | tf_op jit(solution)/shard_map/ppermute | solution.py:192
  121.6 6.5 %collective-permute-start.26 = (bf16[128,256]{1,0:T(8,128)(2,1)S(1)}, bf16[128,256]{1,0:T(8,128)(2,1)S(1)}, u32[]{:S(2)}, u32[]{:S(2)}) collective-permute-start(bf16[128,256]{1,0:T(8,128)(2,1)S(1)} %get-tuple-element.47), channel_id=1, source_target_pairs={{0,48},{4,52},{8,56},{12,60},{16,0},{20,4},{24,8},{28,12},{32,16},... | collective-permute-start | bytes 196616 | tf_op jit(solution)/shard_map/ppermute | solution.py:192
  (22 other events, 148.8 us)
where the time goes:
time: 133 us; the launch traced here: 135 us
  waiting for transfers between devices  57.1 us (43%)
  starting transfers between devices  39.9 us (30%)
  Pallas kernels  27 us (20%)
  other arithmetic  6.82 us (5%)
  local copies, waits for them, and re-layouts  2.93 us (2%)
    ppermute x24, waiting for transfers between devices, shift(): return lax.ppermute(x, 'inner', pairs)  56.2 us
    ppermute x24, starting transfers between devices, shift(): return lax.ppermute(x, 'inner', pairs)  30.8 us
    pallas_call x1, Pallas kernels, attention(): pl.pallas_call(attention_kernel, out_shape=(wide, wide) + (part,) * 8, in...  27 us
    ppermute x6, starting transfers between devices, swap(): return lax.ppermute(x, 'outer', [(0, 1), (1, 0)])  9.11 us
  transfers between devices with their start and end apart: 30, of which 14 were waited for; matrix products, arithmetic and copies ran while one was open for 4% of the time, Pallas kernels for 0%

commit v1 on v0

v1 whole, which is shorter than its diff:
```python
import functools
import math

import jax
import jax.numpy as jnp
from jax import lax
from jax.experimental import pallas as pl
from jax.experimental.pallas import tpu as pltpu
from jax.sharding import PartitionSpec as P

HEAD = 128
HEADS = 8
RUN = 64
ROWS = RUN * HEADS
TOK = 128
TAIL = 16
SIDE = 4
UNITS = 2 * SIDE
BLOCKS = 64
CHUNK = 1024
GRAIN = 1024
SCALE = HEAD**-0.5
SCALE2 = SCALE * math.log2(math.e)
NEG = -1e30

bf16 = jnp.bfloat16
f32 = jnp.float32


def dot(a, b):
    return lax.dot_general(a, b, (((1,), (0,)), ((), ())), preferred_element_type=f32)


def dot_t0(a, b):
    return lax.dot_general(a, b, (((0,), (0,)), ((), ())), preferred_element_type=f32)


def attention_kernel(*refs):
    core_ref = refs[0]
    q_refs, do_refs = refs[1:3], refs[3:5]
    kv_refs = refs[5:9]
    out_refs, gq_refs = refs[9:11], refs[11:13]
    dkv_refs = refs[13:17]
    (ids_v, ids_s, kv, qs, dos, outs, gqs, ka, va, qn, qt, don, dot_t, sbuf, wbuf) = refs[17:32]
    (dka, dva, kv_sem, q_sem, ids_sem, out_sem) = refs[32:]
    tokens = BLOCKS * RUN
    step = TOK + TAIL
    width = HEADS * HEAD

    kv_copies = [
        pltpu.make_async_copy(kv_refs[part], kv.at[part], kv_sem.at[part]) for part in range(SIDE)
    ]
    own_columns = pl.ds(pl.multiple_of(core_ref[0] * width, width), width)
    q_copies = [
        pltpu.make_async_copy(q_refs[0].at[:, own_columns], qs.at[0:TOK], q_sem.at[0]),
        pltpu.make_async_copy(q_refs[1], qs.at[TOK : 2 * TOK], q_sem.at[1]),
        pltpu.make_async_copy(do_refs[0].at[:, own_columns], dos.at[0:TOK], q_sem.at[2]),
        pltpu.make_async_copy(do_refs[1], dos.at[TOK : 2 * TOK], q_sem.at[3]),
    ]
    for copy in kv_copies + q_copies:
        copy.start()

    lane = lax.broadcasted_iota(jnp.int32, (RUN, HEAD), 1)
    sub = lax.broadcasted_iota(jnp.int32, (RUN, HEAD), 0)
    diff = jnp.where(lane < RUN, sub - lane, -(1 << 30))
    ones3 = jnp.where(lax.broadcasted_iota(jnp.int32, (CHUNK, HEAD), 1) < 3, 1.0, 0.0).astype(bf16)
    token_of = lax.broadcasted_iota(jnp.int32, (HEAD, ROWS), 1) & (RUN - 1)
    depth_of = lax.broadcasted_iota(jnp.int32, (HEAD, ROWS), 0)
    qt[HEAD : 2 * HEAD, :] = jnp.where(token_of == depth_of, 1.0, 0.0).astype(bf16)

    @pl.loop(0, tokens // CHUNK)
    def _(c):
        s = pl.ds(pl.multiple_of(c * CHUNK, CHUNK), CHUNK)
        va[s, HEAD : 2 * HEAD] = ones3
        dka[s, :] = jnp.zeros((CHUNK, HEAD), f32)
        dva[s, :] = jnp.zeros((CHUNK, HEAD), f32)

    for part in range(SIDE):
        kv_copies[part].wait()
        for unit in range(UNITS):
            tail = kv[part, unit * step + TOK : (unit + 1) * step, 0:HEAD]
            row = part * UNITS + unit
            ids_v[row : row + 1, :] = tail.astype(f32)[0:1, :].astype(jnp.int32)
    fetch = pltpu.make_async_copy(ids_v, ids_s, ids_sem)
    fetch.start()
    fetch.wait()

    for part in range(SIDE):
        for unit in range(UNITS):
            for run in range(2):
                where = ids_s[part * UNITS + unit, run]
                place = pl.ds(pl.multiple_of(where * RUN, RUN), RUN)
                first = unit * step + run * RUN
                ka[place, 0:HEAD] = kv[part, first : first + RUN, 0:HEAD]
                va[place, 0:HEAD] = kv[part, first : first + RUN, HEAD : 2 * HEAD]

    for copy in q_copies:
        copy.wait()

    def run_block(a, position, length):
        rows = pl.ds(pl.multiple_of(a * RUN, RUN), RUN)
        for h in range(HEADS):
            qn[h * RUN : (h + 1) * RUN, :] = qs[rows, h * HEAD : (h + 1) * HEAD]
            don[h * RUN : (h + 1) * RUN, :] = dos[rows, h * HEAD : (h + 1) * HEAD]
        qt[0:HEAD, :] = jnp.transpose(qn[...])
        for j in range(length // RUN):
            mask = jnp.where(diff <= (position - j) * RUN, 0.0, NEG).astype(bf16)
            ka[j * RUN : (j + 1) * RUN, HEAD : 2 * HEAD] = mask
        scores = dot(ka[0:length, :], qt[...]) * SCALE2
        sbuf[0:length, :] = scores
        largest = jnp.max(scores.reshape(length // 8, 8, ROWS), axis=0)
        row_max = jnp.max(largest, axis=0, keepdims=True)
        weights = jnp.exp2(sbuf[0:length, :] - row_max).astype(bf16)
        wbuf[0:length, :] = weights
        mixed = dot_t0(va[0:length, 0:HEAD + TAIL], weights)
        inverse = 1.0 / mixed[HEAD : HEAD + 1, :]
        out_t = (mixed[0:HEAD, :] * inverse).astype(bf16)
        out_n = jnp.transpose(out_t)
        do_t = (jnp.transpose(don[...]).astype(f32) * inverse).astype(bf16)
        don[...] = jnp.transpose(do_t)
        delta = -jnp.sum(do_t.astype(f32) * out_t.astype(f32), axis=0, keepdims=True)
        high = delta.astype(bf16).astype(f32)
        middle = (delta - high).astype(bf16).astype(f32)
        low = delta - high - middle
        dot_t[0:HEAD, :] = do_t
        dot_t[HEAD : 2 * HEAD, :] = jnp.where(
            depth_of == 0,
            high,
            jnp.where(depth_of == 1, middle, jnp.where(depth_of == 2, low, 0.0)),
        ).astype(bf16)
        for h in range(HEADS):
            outs[rows, h * HEAD : (h + 1) * HEAD] = out_n[h * RUN : (h + 1) * RUN, :]
        weights = wbuf[0:length, :]
        dscore = weights * dot(va[0:length, :], dot_t[...]).astype(bf16)
        dva[0:length, :] += dot(weights, don[...])
        dka[0:length, :] += dot(dscore, qn[...])
        grad_n = jnp.transpose((dot_t0(ka[0:length, 0:HEAD], dscore) * SCALE).astype(bf16))
        for h in range(HEADS):
            gqs[rows, h * HEAD : (h + 1) * HEAD] = grad_n[h * RUN : (h + 1) * RUN, :]

    @pl.loop(0, 4)
    def _(a):
        position = ids_s[a // 2, a % 2]
        level = position * RUN // GRAIN
        for n in range(tokens // GRAIN):

            @pl.when(level == n)
            def _():
                run_block(a, position, (n + 1) * GRAIN)

    copies = []
    for half in (1, 0):
        place = slice(half * TOK, (half + 1) * TOK)
        copies.append(pltpu.make_async_copy(outs.at[place], out_refs[half], out_sem.at[half]))
        copies.append(pltpu.make_async_copy(gqs.at[place], gq_refs[half], out_sem.at[2 + half]))
        copies[-2].start()
        copies[-1].start()
    for part in PART_ORDER:
        for unit in range(UNITS):
            for run in range(2):
                where = ids_s[part * UNITS + unit, run]
                place = pl.ds(pl.multiple_of(where * RUN, RUN), RUN)
                first = unit * TOK + run * RUN
                dkv_refs[part][first : first + RUN, 0:HEAD] = (dka[place, :] * SCALE).astype(bf16)
                dkv_refs[part][first : first + RUN, HEAD : 2 * HEAD] = dva[place, :].astype(bf16)
    for copy in copies:
        copy.wait()


PART_ORDER = (1, 2, 3, 0)


def attention(core, q, do, kv):
    anywhere = pl.BlockSpec(memory_space=pl.ANY)
    local = pl.BlockSpec(memory_space=pltpu.VMEM)
    smem = pl.BlockSpec(memory_space=pltpu.SMEM)
    tokens = BLOCKS * RUN
    width = HEADS * HEAD
    wide = jax.ShapeDtypeStruct((TOK, width), bf16)
    part = pltpu.VMEM((UNITS * TOK, 2 * HEAD), bf16)
    near = pltpu.VMEM((TOK, width), bf16)
    return pl.pallas_call(
        attention_kernel,
        out_shape=(wide, near, wide, near) + (part,) * SIDE,
        in_specs=[smem] + [anywhere] * 8,
        out_specs=(anywhere, local, anywhere, local) + (local,) * SIDE,
        scratch_shapes=[
            pltpu.VMEM((32, HEAD), jnp.int32),
            pltpu.SMEM((32, HEAD), jnp.int32),
            pltpu.VMEM((SIDE, UNITS * (TOK + TAIL), 2 * HEAD), bf16),
            pltpu.VMEM((2 * TOK, width), bf16),
            pltpu.VMEM((2 * TOK, width), bf16),
            pltpu.VMEM((2 * TOK, width), bf16),
            pltpu.VMEM((2 * TOK, width), bf16),
            pltpu.VMEM((tokens, 2 * HEAD), bf16),
            pltpu.VMEM((tokens, 2 * HEAD), bf16),
            pltpu.VMEM((ROWS, HEAD), bf16),
            pltpu.VMEM((2 * HEAD, ROWS), bf16),
            pltpu.VMEM((ROWS, HEAD), bf16),
            pltpu.VMEM((2 * HEAD, ROWS), bf16),
            pltpu.VMEM((tokens, ROWS), f32),
            pltpu.VMEM((tokens, ROWS), bf16),
            pltpu.VMEM((tokens, HEAD), f32),
            pltpu.VMEM((tokens, HEAD), f32),
            pltpu.SemaphoreType.DMA((SIDE,)),
            pltpu.SemaphoreType.DMA((4,)),
            pltpu.SemaphoreType.DMA,
            pltpu.SemaphoreType.DMA((4,)),
        ],
        compiler_params=pltpu.CompilerParams(vmem_limit_bytes=VLIMIT * 2**20),
        name="attention",
    )(core, *q, *do, *kv)


VLIMIT = 42


def swap(x):
    return lax.ppermute(x, ("outer", "inner"), [(i, (i + 16) % 32) for i in range(32)])


def shift(x, stage, distance):
    pairs = []
    for core in range(2):
        for z in range(SIDE):
            for y in range(SIDE):
                if core == stage:
                    far = z * SIDE + (y + distance) % SIDE
                else:
                    far = (z + distance) % SIDE * SIDE + y
                pairs.append((core * 16 + z * SIDE + y, core * 16 + far))
    return lax.ppermute(x, ("outer", "inner"), pairs)


def body(queries, keys, values, output_cotangent, positions):
    core = lax.axis_index("outer")

    def pick(x, which):
        width = x.shape[1] // 2
        return lax.dynamic_slice_in_dim(x, which * width, width, axis=1)

    run_ids = jnp.concatenate([positions[0:1], positions[RUN : RUN + 1]]) // RUN
    tail = jnp.zeros((TAIL, 2 * HEAD), bf16).at[0, 0:2].set(run_ids.astype(bf16))

    def unit(which):
        return jnp.concatenate(
            [jnp.concatenate([pick(keys, which), pick(values, which)], 1), tail], 0
        )

    kv_own = jnp.concatenate([unit(core), swap(unit(1 - core))], 0)
    line = [kv_own] + [shift(kv_own, 0, d) for d in ORDER]
    line = lax.optimization_barrier(tuple(line) + (queries, output_cotangent))
    queries, output_cotangent = line[4:]
    line = jnp.concatenate(line[:4], 0)
    lines = [line] + [shift(line, 1, d) for d in ORDER]
    q_other = swap(pick(queries, 1 - core))
    do_other = swap(pick(output_cotangent, 1 - core))

    results = attention(
        core.astype(jnp.int32).reshape(1),
        (queries, q_other),
        (output_cotangent, do_other),
        lines,
    )
    outs, grads, parts = results[:2], results[2:4], results[4:]

    def total(terms):
        return functools.reduce(jnp.add, [t.astype(f32) for t in terms]).astype(bf16)

    def cut(x, i):
        return x[i * 2 * TOK : (i + 1) * 2 * TOK]

    line = total([parts[0]] + [shift(parts[1 + i], 1, -d) for i, d in enumerate(ORDER)])
    dkv = total([cut(line, 0)] + [shift(cut(line, 1 + i), 0, -d) for i, d in enumerate(ORDER)])
    dkv_mine, dkv_other = dkv[:TOK], swap(dkv[TOK:])

    def join(mine, other):
        return jnp.where(
            core == 0, jnp.concatenate([mine, other], 1), jnp.concatenate([other, mine], 1)
        )

    attn_out = join(outs[0], swap(outs[1]))
    grad_queries = join(grads[0], swap(grads[1]))
    key_gradient = join(dkv_mine[:, :HEAD], dkv_other[:, :HEAD])
    value_gradient = join(dkv_mine[:, HEAD:], dkv_other[:, HEAD:])
    return attn_out, grad_queries, key_gradient, value_gradient


ORDER = (2, 1, 3)


def solution(mesh):
    tokens = ("outer", "inner")
    split = P(tokens, "head")
    return jax.shard_map(
        body,
        mesh=mesh,
        in_specs=(split, split, split, split, P(tokens)),
        out_specs=(split, split, split, split),
        check_vma=False,
    )
```

time: 133 us -> 96.1 us (0.72); the launches traced: 135 us -> 95.7 us
  waiting for transfers between devices: 57.1 us -> 26.4 us
  starting transfers between devices: 39.9 us -> 30.6 us
  local copies, waits for them, and re-layouts: 2.93 us -> 5.18 us
    ppermute x30 -> x18, waiting for transfers between devices: 57.1 us -> 26.4 us  [the longest x12 21.7 us: shift(): return lax.ppermute(x, ('outer', 'inner'), pairs)]
    ppermute x30 -> x18, starting transfers between devices: 39.9 us -> 30.6 us  [the longest x12 18.1 us: shift(): return lax.ppermute(x, ('outer', 'inner'), pairs)]
    unnamed x38 -> x21, local copies, waits for them, and re-layouts: 0.8 us -> 3.67 us
    concatenate x4 -> x2, other arithmetic: 2.26 us -> 0.02 us  [the longest x1 0.01 us: body(): kv_own = jnp.concatenate([unit(core), swap(unit(1 - core))], 0)]
    select_n x3 -> x4, other arithmetic: 2.52 us -> 4.22 us  [join(): jnp.where(core == 0, jnp.concatenate([mine, other], 1), jnp.concatenate([...]
    select_n x5 -> x0, other arithmetic: 1.66 us -> none  [the longest x4 1.65 us: halves(): mine = jnp.where(core == 0, first, second)]
    convert_element_type x2 -> x1, other arithmetic: 0.02 us -> 1.37 us  [body(): run_ids.astype(bf16)]
  transfers between devices with their start and end apart: 30 -> 18, of which waited for: 14 -> 15; matrix products, arithmetic and copies ran while one was open for 4% -> 3% of each run, Pallas kernels for 0% -> 0%
where the time goes in v1:
time: 96.1 us; the launch traced here: 95.7 us
  starting transfers between devices  30.6 us (32%)
  Pallas kernels  26.8 us (28%)
  waiting for transfers between devices  26.4 us (27%)
  other arithmetic  5.94 us (6%)
  local copies, waits for them, and re-layouts  5.18 us (5%)
    pallas_call x1, Pallas kernels, attention(): pl.pallas_call(attention_kernel, out_shape=(wide, near, wide, near) + (pa...  26.8 us
    ppermute x12, waiting for transfers between devices, shift(): return lax.ppermute(x, ('outer', 'inner'), pairs)  21.7 us
    ppermute x12, starting transfers between devices, shift(): return lax.ppermute(x, ('outer', 'inner'), pairs)  18.1 us
    ppermute x6, starting transfers between devices, swap(): lax.ppermute(x, ('outer', 'inner'), [(i, (i + 16) % 32) for i in range(32)])  12.5 us
    ppermute x6, waiting for transfers between devices, swap(): lax.ppermute(x, ('outer', 'inner'), [(i, (i + 16) % 32) for i in range(32)])  4.68 us
    select_n x4, other arithmetic, join(): jnp.where(core == 0, jnp.concatenate([mine, other], 1), jnp.concatenate([...  4.22 us
    unnamed x21, local copies, waits for them, and re-layouts  3.67 us
  transfers between devices with their start and end apart: 18, of which 15 were waited for; matrix products, arithmetic and copies ran while one was open for 3% of the time, Pallas kernels for 0%

profile of v1, /device:TPU:1, one launch (start us, length us, event | category | flops | bytes accessed | tf_op | source)
XLA Modules:
  0.0 95.7 jit_solution(16962826964181968983)
XLA Ops:
  1.9 1.4 %fusion = bf16[1,2]{1,0:T(2,128)(2,1)S(1)} fusion(s32[1,1]{1,0:T(1,128)} %bitcast.2, s32[1,1]{1,0:T(1,128)} %bitcast.1), kind=kLoop, calls=%fused_computation.23 | loop fusion | flops 34 | bytes 12 | tf_op jit(solution)/shard_map/convert_element_type | solution.py:243
  4.1 1.5 %collective-permute-start = (bf16[144,256]{1,0:T(8,128)(2,1)S(1)}, bf16[144,256]{1,0:T(8,128)(2,1)S(1)}, u32[]{:S(2)}, u32[]{:S(2)}) collective-permute-start(bf16[144,256]{1,0:T(8,128)(2,1)S(1)} %pad_maximum_fusion.1), channel_id=1, source_target_pairs={{0,64},{4,68},{8,72},{12,76},{16,80},{20,84},{24,88},{28,92},{32,9... | collective-permute-start | bytes 221192 | tf_op jit(solution)/shard_map/ppermute | solution.py:219
  5.6 0.9 collective-permute-done
  6.5 3.8 %collective-permute-start.1 = (bf16[288,256]{1,0:T(8,128)(2,1)S(1)}, bf16[288,256]{1,0:T(8,128)(2,1)S(1)}, u32[]{:S(2)}, u32[]{:S(2)}) collective-permute-start(bf16[288,256]{1,0:T(8,128)(2,1)S(1)} %pad_maximum_fusion), channel_id=1, source_target_pairs={{0,8},{4,12},{8,0},{12,4},{16,24},{20,28},{24,16},{28,20},{32,40},... | collective-permute-start | bytes 442376 | tf_op jit(solution)/shard_map/ppermute | solution.py:232
  11.0 1.9 %collective-permute-start.3 = (bf16[288,256]{1,0:T(8,128)(2,1)S(1)}, bf16[288,256]{1,0:T(8,128)(2,1)S(1)}, u32[]{:S(2)}, u32[]{:S(2)}) collective-permute-start(bf16[288,256]{1,0:T(8,128)(2,1)S(1)} %pad_maximum_fusion), channel_id=1, source_target_pairs={{0,12},{4,0},{8,4},{12,8},{16,28},{20,16},{24,20},{28,24},{32,44},... | collective-permute-start | bytes 442376 | tf_op jit(solution)/shard_map/ppermute | solution.py:232
  13.1 2.7 %collective-permute-done.2 = bf16[288,256]{1,0:T(8,128)(2,1)S(1)} collective-permute-done((bf16[288,256]{1,0:T(8,128)(2,1)S(1)}, bf16[288,256]{1,0:T(8,128)(2,1)S(1)}, u32[]{:S(2)}, u32[]{:S(2)}) %collective-permute-start.2) | collective-permute-done | bytes 147488 | tf_op jit(solution)/shard_map/ppermute | solution.py:232
  15.9 2.7 %collective-permute-start.6 = (bf16[1152,256]{1,0:T(8,128)(2,1)S(1)}, bf16[1152,256]{1,0:T(8,128)(2,1)S(1)}, u32[]{:S(2)}, u32[]{:S(2)}) collective-permute-start(bf16[1152,256]{1,0:T(8,128)(2,1)S(1)} %constant_dynamic-update-slice_fusion.refs_5_), channel_id=1, source_target_pairs={{0,32},{4,36},{8,40},{12,44},{16,48},{20,52},{24,56},{28,60},{32,0... | collective-permute-start | bytes 1769480 | tf_op jit(solution)/shard_map/ppermute | solution.py:232
  19.3 2.0 %collective-permute-start.8 = (bf16[1152,256]{1,0:T(8,128)(2,1)S(1)}, bf16[1152,256]{1,0:T(8,128)(2,1)S(1)}, u32[]{:S(2)}, u32[]{:S(2)}) collective-permute-start(bf16[1152,256]{1,0:T(8,128)(2,1)S(1)} %constant_dynamic-update-slice_fusion.refs_5_), channel_id=1, source_target_pairs={{0,48},{4,52},{8,56},{12,60},{16,0},{20,4},{24,8},{28,12},{32,16},... | collective-permute-start | bytes 1769480 | tf_op jit(solution)/shard_map/ppermute | solution.py:232
  21.3 2.7 %collective-permute-start.5 = (bf16[128,1024]{1,0:T(8,128)(2,1)S(1)}, bf16[128,1024]{1,0:T(8,128)(2,1)S(1)}, u32[]{:S(2)}, u32[]{:S(2)}) collective-permute-start(bf16[128,1024]{1,0:T(8,128)(2,1)S(1)} %constant_dynamic-slice_fusion), channel_id=1, source_target_pairs={{0,64},{4,68},{8,72},{12,76},{16,80},{20,84},{24,88},{28,92},{32,9... | collective-permute-start | bytes 786440 | tf_op jit(solution)/shard_map/ppermute | solution.py:219
  24.1 1.0 %collective-permute-done.5.refs_4_ = bf16[128,1024]{1,0:T(8,128)(2,1)S(1)} collective-permute-done((bf16[128,1024]{1,0:T(8,128)(2,1)S(1)}, bf16[128,1024]{1,0:T(8,128)(2,1)S(1)}, u32[]{:S(2)}, u32[]{:S(2)}) %collective-permute-start.5) | collective-permute-done | bytes 262176 | tf_op jit(solution)/shard_map/ppermute | solution.py:219
  25.6 0.9 collective-permute-done.6.refs_6_
  26.6 6.3 %collective-permute-done.7.refs_7_ = bf16[1152,256]{1,0:T(8,128)(2,1)S(1)} collective-permute-done((bf16[1152,256]{1,0:T(8,128)(2,1)S(1)}, bf16[1152,256]{1,0:T(8,128)(2,1)S(1)}, u32[]{:S(2)}, u32[]{:S(2)}) %collective-permute-start.7) | collective-permute-done | bytes 589856 | tf_op jit(solution)/shard_map/ppermute | solution.py:232
  33.2 26.8 %attention.1 = (bf16[128,1024]{1,0:T(8,128)(2,1)S(1)}, bf16[128,1024]{1,0:T(8,128)(2,1)S(1)}, bf16[128,1024]{1,0:T(8,128)(2,1)S(1)}, bf16[128,1024]{1,0:T(8,128)...) custom-call(s32[1]{0:T(128)} %bitcast.refs_0_, ...), custom_call_target="tpu_custom_call" | custom-call | tf_op jit(solution)/shard_map/attention/pallas_call | solution.py:182
  63.3 4.4 %collective-permute-start.12 = (bf16[1024,256]{1,0:T(8,128)(2,1)}, bf16[1024,256]{1,0:T(8,128)(2,1)S(1)}, u32[]{:S(2)}, u32[]{:S(2)}) collective-permute-start(bf16[1024,256]{1,0:T(8,128)(2,1)} %get-tuple-element.42), channel_id=1, source_target_pairs={{0,48},{4,52},{8,56},{12,60},{16,0},{20,4},{24,8},{28,12},{32,16},... | collective-permute-start | bytes 1572872 | tf_op jit(solution)/shard_map/ppermute | solution.py:232
  68.3 1.4 %collective-permute-done.10 = bf16[128,1024]{1,0:T(8,128)(2,1)S(1)} collective-permute-done((bf16[128,1024]{1,0:T(8,128)(2,1)}, bf16[128,1024]{1,0:T(8,128)(2,1)S(1)}, u32[]{:S(2)}, u32[]{:S(2)}) %collective-permute-start.10) | collective-permute-done | bytes 262176 | tf_op jit(solution)/shard_map/ppermute | solution.py:219
  69.6 2.0 %maximum_select_fusion.1 = bf16[128,2048]{1,0:T(8,128)(2,1)} fusion(bf16[128,1024]{1,0:T(8,128)(2,1)S(1)} %collective-permute-done.10, bf16[128,1024]{1,0:T(8,128)(2,1)} %copy-done.6, pred[]{:T(512)S(6)} %eq.2), kind=kLoop, calls=%fused_computation.2 | loop fusion | flops 2359296 | bytes 1048577 | tf_op jit(solution)/shard_map/jit(_where)/select_n | solution.py:278
  71.6 1.4 %collective-permute-done.11 = bf16[1024,256]{1,0:T(8,128)(2,1)S(1)} collective-permute-done((bf16[1024,256]{1,0:T(8,128)(2,1)}, bf16[1024,256]{1,0:T(8,128)(2,1)S(1)}, u32[]{:S(2)}, u32[]{:S(2)}) %collective-permute-start.11) | collective-permute-done | bytes 524320 | tf_op jit(solution)/shard_map/ppermute | solution.py:232
  73.1 4.9 %collective-permute-done.12 = bf16[1024,256]{1,0:T(8,128)(2,1)S(1)} collective-permute-done((bf16[1024,256]{1,0:T(8,128)(2,1)}, bf16[1024,256]{1,0:T(8,128)(2,1)S(1)}, u32[]{:S(2)}, u32[]{:S(2)}) %collective-permute-start.12) | collective-permute-done | bytes 524320 | tf_op jit(solution)/shard_map/ppermute | solution.py:232
  79.1 1.1 %collective-permute-start.15 = (bf16[256,256]{1,0:T(8,128)(2,1)S(1)}, bf16[256,256]{1,0:T(8,128)(2,1)S(1)}, u32[]{:S(2)}, u32[]{:S(2)}) collective-permute-start(bf16[256,256]{1,0:T(8,128)(2,1)S(1)} %get-tuple-element.46), channel_id=1, source_target_pairs={{0,12},{4,0},{8,4},{12,8},{16,28},{20,16},{24,20},{28,24},{32,44},... | collective-permute-start | bytes 393224 | tf_op jit(solution)/shard_map/ppermute | solution.py:232
  80.6 0.9 maximum_select_fusion
  81.6 2.9 %collective-permute-done.14 = bf16[256,256]{1,0:T(8,128)(2,1)S(1)} collective-permute-done((bf16[256,256]{1,0:T(8,128)(2,1)S(1)}, bf16[256,256]{1,0:T(8,128)(2,1)S(1)}, u32[]{:S(2)}, u32[]{:S(2)}) %collective-permute-start.14) | collective-permute-done | bytes 131104 | tf_op jit(solution)/shard_map/ppermute | solution.py:232
  84.5 1.3 %collective-permute-done.16 = bf16[256,256]{1,0:T(8,128)(2,1)S(1)} collective-permute-done((bf16[256,256]{1,0:T(8,128)(2,1)S(1)}, bf16[256,256]{1,0:T(8,128)(2,1)S(1)}, u32[]{:S(2)}, u32[]{:S(2)}) %collective-permute-start.16) | collective-permute-done | bytes 131104 | tf_op jit(solution)/shard_map/ppermute | solution.py:232
  85.9 7.6 %collective-permute-start.17 = (bf16[128,256]{1,0:T(8,128)(2,1)S(1)}, bf16[128,256]{1,0:T(8,128)(2,1)S(1)}, u32[]{:S(2)}, u32[]{:S(2)}) collective-permute-start(bf16[128,256]{1,0:T(8,128)(2,1)S(1)} %slice.68), channel_id=1, source_target_pairs={{0,64},{4,68},{8,72},{12,76},{16,80},{20,84},{24,88},{28,92},{32,9... | collective-permute-start | bytes 196616 | tf_op jit(solution)/shard_map/ppermute | solution.py:219
  93.5 0.9 collective-permute-done.17
  (53 shorter events, 11.4 us)
Async XLA Ops:
  4.1 2.4 %collective-permute-start = (bf16[144,256]{1,0:T(8,128)(2,1)S(1)}, bf16[144,256]{1,0:T(8,128)(2,1)S(1)}, u32[]{:S(2)}, u32[]{:S(2)}) collective-permute-start(bf16[144,256]{1,0:T(8,128)(2,1)S(1)} %pad_maximum_fusion.1), channel_id=1, source_target_pairs={{0,64},{4,68},{8,72},{12,76},{16,80},{20,84},{24,88},{28,92},{32,9... | collective-permute-start | bytes 221192 | tf_op jit(solution)/shard_map/ppermute | solution.py:219
  6.5 14.7 %copy-start.1 = (bf16[128,2048]{1,0:T(8,128)(2,1)S(1)}, bf16[128,2048]{1,0:T(8,128)(2,1)}, u32[]{:S(2)}) copy-start(bf16[128,2048]{1,0:T(8,128)(2,1)} %refs_3_) | copy-start | bytes 1572868
  6.5 6.6 %collective-permute-start.1 = (bf16[288,256]{1,0:T(8,128)(2,1)S(1)}, bf16[288,256]{1,0:T(8,128)(2,1)S(1)}, u32[]{:S(2)}, u32[]{:S(2)}) collective-permute-start(bf16[288,256]{1,0:T(8,128)(2,1)S(1)} %pad_maximum_fusion), channel_id=1, source_target_pairs={{0,8},{4,12},{8,0},{12,4},{16,24},{20,28},{24,16},{28,20},{32,40},... | collective-permute-start | bytes 442376 | tf_op jit(solution)/shard_map/ppermute | solution.py:232
  10.3 5.5 %collective-permute-start.2 = (bf16[288,256]{1,0:T(8,128)(2,1)S(1)}, bf16[288,256]{1,0:T(8,128)(2,1)S(1)}, u32[]{:S(2)}, u32[]{:S(2)}) collective-permute-start(bf16[288,256]{1,0:T(8,128)(2,1)S(1)} %pad_maximum_fusion), channel_id=1, source_target_pairs={{0,4},{4,8},{8,12},{12,0},{16,20},{20,24},{24,28},{28,16},{32,36},... | collective-permute-start | bytes 442376 | tf_op jit(solution)/shard_map/ppermute | solution.py:232
  11.0 4.8 %collective-permute-start.3 = (bf16[288,256]{1,0:T(8,128)(2,1)S(1)}, bf16[288,256]{1,0:T(8,128)(2,1)S(1)}, u32[]{:S(2)}, u32[]{:S(2)}) collective-permute-start(bf16[288,256]{1,0:T(8,128)(2,1)S(1)} %pad_maximum_fusion), channel_id=1, source_target_pairs={{0,12},{4,0},{8,4},{12,8},{16,28},{20,16},{24,20},{28,24},{32,44},... | collective-permute-start | bytes 442376 | tf_op jit(solution)/shard_map/ppermute | solution.py:232
  15.8 8.2 %copy-start = (bf16[128,2048]{1,0:T(8,128)(2,1)S(1)}, bf16[128,2048]{1,0:T(8,128)(2,1)}, u32[]{:S(2)}) copy-start(bf16[128,2048]{1,0:T(8,128)(2,1)} %refs_1_) | copy-start | bytes 1572868
  15.9 10.7 %collective-permute-start.6 = (bf16[1152,256]{1,0:T(8,128)(2,1)S(1)}, bf16[1152,256]{1,0:T(8,128)(2,1)S(1)}, u32[]{:S(2)}, u32[]{:S(2)}) collective-permute-start(bf16[1152,256]{1,0:T(8,128)(2,1)S(1)} %constant_dynamic-update-slice_fusion.refs_5_), channel_id=1, source_target_pairs={{0,32},{4,36},{8,40},{12,44},{16,48},{20,52},{24,56},{28,60},{32,0... | collective-permute-start | bytes 1769480 | tf_op jit(solution)/shard_map/ppermute | solution.py:232
  18.6 14.2 %collective-permute-start.7 = (bf16[1152,256]{1,0:T(8,128)(2,1)S(1)}, bf16[1152,256]{1,0:T(8,128)(2,1)S(1)}, u32[]{:S(2)}, u32[]{:S(2)}) collective-permute-start(bf16[1152,256]{1,0:T(8,128)(2,1)S(1)} %constant_dynamic-update-slice_fusion.refs_5_), channel_id=1, source_target_pairs={{0,16},{4,20},{8,24},{12,28},{16,32},{20,36},{24,40},{28,44},{32,4... | collective-permute-start | bytes 1769480 | tf_op jit(solution)/shard_map/ppermute | solution.py:232
  19.3 13.9 %collective-permute-start.8 = (bf16[1152,256]{1,0:T(8,128)(2,1)S(1)}, bf16[1152,256]{1,0:T(8,128)(2,1)S(1)}, u32[]{:S(2)}, u32[]{:S(2)}) collective-permute-start(bf16[1152,256]{1,0:T(8,128)(2,1)S(1)} %constant_dynamic-update-slice_fusion.refs_5_), channel_id=1, source_target_pairs={{0,48},{4,52},{8,56},{12,60},{16,0},{20,4},{24,8},{28,12},{32,16},... | collective-permute-start | bytes 1769480 | tf_op jit(solution)/shard_map/ppermute | solution.py:232
  21.3 3.9 %collective-permute-start.5 = (bf16[128,1024]{1,0:T(8,128)(2,1)S(1)}, bf16[128,1024]{1,0:T(8,128)(2,1)S(1)}, u32[]{:S(2)}, u32[]{:S(2)}) collective-permute-start(bf16[128,1024]{1,0:T(8,128)(2,1)S(1)} %constant_dynamic-slice_fusion), channel_id=1, source_target_pairs={{0,64},{4,68},{8,72},{12,76},{16,80},{20,84},{24,88},{28,92},{32,9... | collective-permute-start | bytes 786440 | tf_op jit(solution)/shard_map/ppermute | solution.py:219
  24.0 1.6 %collective-permute-start.4 = (bf16[128,1024]{1,0:T(8,128)(2,1)S(1)}, bf16[128,1024]{1,0:T(8,128)(2,1)S(1)}, u32[]{:S(2)}, u32[]{:S(2)}) collective-permute-start(bf16[128,1024]{1,0:T(8,128)(2,1)S(1)} %constant_dynamic-slice_fusion.1), channel_id=1, source_target_pairs={{0,64},{4,68},{8,72},{12,76},{16,80},{20,84},{24,88},{28,92},{32,9... | collective-permute-start | bytes 786440 | tf_op jit(solution)/shard_map/ppermute | solution.py:219
  60.1 0.8 copy-start.2
  60.9 0.7 copy-start.4
  63.0 10.0 %collective-permute-start.11 = (bf16[1024,256]{1,0:T(8,128)(2,1)}, bf16[1024,256]{1,0:T(8,128)(2,1)S(1)}, u32[]{:S(2)}, u32[]{:S(2)}) collective-permute-start(bf16[1024,256]{1,0:T(8,128)(2,1)} %get-tuple-element.41), channel_id=1, source_target_pairs={{0,32},{4,36},{8,40},{12,44},{16,48},{20,52},{24,56},{28,60},{32,0... | collective-permute-start | bytes 1572872 | tf_op jit(solution)/shard_map/ppermute | solution.py:232
  63.3 14.7 %collective-permute-start.12 = (bf16[1024,256]{1,0:T(8,128)(2,1)}, bf16[1024,256]{1,0:T(8,128)(2,1)S(1)}, u32[]{:S(2)}, u32[]{:S(2)}) collective-permute-start(bf16[1024,256]{1,0:T(8,128)(2,1)} %get-tuple-element.42), channel_id=1, source_target_pairs={{0,48},{4,52},{8,56},{12,60},{16,0},{20,4},{24,8},{28,12},{32,16},... | collective-permute-start | bytes 1572872 | tf_op jit(solution)/shard_map/ppermute | solution.py:232
  67.7 11.0 %collective-permute-start.13 = (bf16[1024,256]{1,0:T(8,128)(2,1)}, bf16[1024,256]{1,0:T(8,128)(2,1)S(1)}, u32[]{:S(2)}, u32[]{:S(2)}) collective-permute-start(bf16[1024,256]{1,0:T(8,128)(2,1)} %get-tuple-element.43), channel_id=1, source_target_pairs={{0,16},{4,20},{8,24},{12,28},{16,32},{20,36},{24,40},{28,44},{32,4... | collective-permute-start | bytes 1572872 | tf_op jit(solution)/shard_map/ppermute | solution.py:232
  67.7 1.9 %collective-permute-start.10 = (bf16[128,1024]{1,0:T(8,128)(2,1)}, bf16[128,1024]{1,0:T(8,128)(2,1)S(1)}, u32[]{:S(2)}, u32[]{:S(2)}) collective-permute-start(bf16[128,1024]{1,0:T(8,128)(2,1)} %get-tuple-element.39), channel_id=1, source_target_pairs={{0,64},{4,68},{8,72},{12,76},{16,80},{20,84},{24,88},{28,92},{32,9... | collective-permute-start | bytes 786440 | tf_op jit(solution)/shard_map/ppermute | solution.py:219
  68.3 12.4 %collective-permute-start.9 = (bf16[128,1024]{1,0:T(8,128)(2,1)}, bf16[128,1024]{1,0:T(8,128)(2,1)S(1)}, u32[]{:S(2)}, u32[]{:S(2)}) collective-permute-start(bf16[128,1024]{1,0:T(8,128)(2,1)} %copy-done.7), channel_id=1, source_target_pairs={{0,64},{4,68},{8,72},{12,76},{16,80},{20,84},{24,88},{28,92},{32,9... | collective-permute-start | bytes 786440 | tf_op jit(solution)/shard_map/ppermute | solution.py:219
  69.6 9.1 %copy-start.3 = (bf16[1024,256]{1,0:T(8,128)(2,1)S(1)}, bf16[1024,256]{1,0:T(8,128)(2,1)}, u32[]{:S(2)}) copy-start(bf16[1024,256]{1,0:T(8,128)(2,1)} %copy-done.2) | copy-start | bytes 1572868
  79.0 1.7 %copy-start.5 = (bf16[128,1024]{1,0:T(8,128)(2,1)S(1)}, bf16[128,1024]{1,0:T(8,128)(2,1)}, u32[]{:S(2)}) copy-start(bf16[128,1024]{1,0:T(8,128)(2,1)} %copy-done.4) | copy-start | bytes 786436
  79.0 5.5 %collective-permute-start.14 = (bf16[256,256]{1,0:T(8,128)(2,1)S(1)}, bf16[256,256]{1,0:T(8,128)(2,1)S(1)}, u32[]{:S(2)}, u32[]{:S(2)}) collective-permute-start(bf16[256,256]{1,0:T(8,128)(2,1)S(1)} %get-tuple-element.44), channel_id=1, source_target_pairs={{0,8},{4,12},{8,0},{12,4},{16,24},{20,28},{24,16},{28,20},{32,40},... | collective-permute-start | bytes 393224 | tf_op jit(solution)/shard_map/ppermute | solution.py:232
  79.1 5.4 %collective-permute-start.15 = (bf16[256,256]{1,0:T(8,128)(2,1)S(1)}, bf16[256,256]{1,0:T(8,128)(2,1)S(1)}, u32[]{:S(2)}, u32[]{:S(2)}) collective-permute-start(bf16[256,256]{1,0:T(8,128)(2,1)S(1)} %get-tuple-element.46), channel_id=1, source_target_pairs={{0,12},{4,0},{8,4},{12,8},{16,28},{20,16},{24,20},{28,24},{32,44},... | collective-permute-start | bytes 393224 | tf_op jit(solution)/shard_map/ppermute | solution.py:232
  80.2 5.6 %collective-permute-start.16 = (bf16[256,256]{1,0:T(8,128)(2,1)S(1)}, bf16[256,256]{1,0:T(8,128)(2,1)S(1)}, u32[]{:S(2)}, u32[]{:S(2)}) collective-permute-start(bf16[256,256]{1,0:T(8,128)(2,1)S(1)} %get-tuple-element.45), channel_id=1, source_target_pairs={{0,4},{4,8},{8,12},{12,0},{16,20},{20,24},{24,28},{28,16},{32,36},... | collective-permute-start | bytes 393224 | tf_op jit(solution)/shard_map/ppermute | solution.py:232
  85.9 8.5 %collective-permute-start.17 = (bf16[128,256]{1,0:T(8,128)(2,1)S(1)}, bf16[128,256]{1,0:T(8,128)(2,1)S(1)}, u32[]{:S(2)}, u32[]{:S(2)}) collective-permute-start(bf16[128,256]{1,0:T(8,128)(2,1)S(1)} %slice.68), channel_id=1, source_target_pairs={{0,64},{4,68},{8,72},{12,76},{16,80},{20,84},{24,88},{28,92},{32,9... | collective-permute-start | bytes 196616 | tf_op jit(solution)/shard_map/ppermute | solution.py:219
  (3 other events, 2.1 us)

commit v2 on v1

--- a/solution.py
+++ b/solution.py
@@ -18,7 +18,7 @@
 UNITS = 2 * SIDE
 BLOCKS = 64
 CHUNK = 1024
-GRAIN = 1024
+LENGTHS = (1024, 2048, 2560, 3072, 3584, 4096)
 SCALE = HEAD**-0.5
 SCALE2 = SCALE * math.log2(math.e)
 NEG = -1e30
@@ -41,8 +41,8 @@
     kv_refs = refs[5:9]
     out_refs, gq_refs = refs[9:11], refs[11:13]
     dkv_refs = refs[13:17]
-    (ids_v, ids_s, kv, qs, dos, outs, gqs, ka, va, qn, qt, don, dot_t, sbuf, wbuf) = refs[17:32]
-    (dka, dva, kv_sem, q_sem, ids_sem, out_sem) = refs[32:]
+    (ids_v, ids_s, kv, qs, dos, outs, gqs, dkv, ka, va, qn, qt, don, dot_t, sbuf, wbuf) = refs[17:33]
+    (dka, dva, kv_sem, q_sem, ids_sem, out_sem, dkv_sem) = refs[33:]
     tokens = BLOCKS * RUN
     step = TOK + TAIL
     width = HEADS * HEAD
@@ -141,15 +141,15 @@
     @pl.loop(0, 4)
     def _(a):
         position = ids_s[a // 2, a % 2]
-        level = position * RUN // GRAIN
-        for n in range(tokens // GRAIN):
-
-            @pl.when(level == n)
+        needed = (position + 1) * RUN
+        for short, length in zip((0,) + LENGTHS, LENGTHS):
+
+            @pl.when((needed > short) & (needed <= length))
             def _():
-                run_block(a, position, (n + 1) * GRAIN)
+                run_block(a, position, length)
 
     copies = []
-    for half in (1, 0):
+    for half in range(2):
         place = slice(half * TOK, (half + 1) * TOK)
         copies.append(pltpu.make_async_copy(outs.at[place], out_refs[half], out_sem.at[half]))
         copies.append(pltpu.make_async_copy(gqs.at[place], gq_refs[half], out_sem.at[2 + half]))
@@ -161,8 +161,10 @@
                 where = ids_s[part * UNITS + unit, run]
                 place = pl.ds(pl.multiple_of(where * RUN, RUN), RUN)
                 first = unit * TOK + run * RUN
-                dkv_refs[part][first : first + RUN, 0:HEAD] = (dka[place, :] * SCALE).astype(bf16)
-                dkv_refs[part][first : first + RUN, HEAD : 2 * HEAD] = dva[place, :].astype(bf16)
+                dkv[part, first : first + RUN, 0:HEAD] = (dka[place, :] * SCALE).astype(bf16)
+                dkv[part, first : first + RUN, HEAD : 2 * HEAD] = dva[place, :].astype(bf16)
+        copies.append(pltpu.make_async_copy(dkv.at[part], dkv_refs[part], dkv_sem.at[part]))
+        copies[-1].start()
     for copy in copies:
         copy.wait()
 
@@ -172,18 +174,16 @@
 
 def attention(core, q, do, kv):
     anywhere = pl.BlockSpec(memory_space=pl.ANY)
-    local = pl.BlockSpec(memory_space=pltpu.VMEM)
     smem = pl.BlockSpec(memory_space=pltpu.SMEM)
     tokens = BLOCKS * RUN
     width = HEADS * HEAD
-    wide = jax.ShapeDtypeStruct((TOK, width), bf16)
-    part = pltpu.VMEM((UNITS * TOK, 2 * HEAD), bf16)
-    near = pltpu.VMEM((TOK, width), bf16)
+    wide = pltpu.HBM((TOK, width), bf16)
+    part = pltpu.HBM((UNITS * TOK, 2 * HEAD), bf16)
     return pl.pallas_call(
         attention_kernel,
-        out_shape=(wide, near, wide, near) + (part,) * SIDE,
+        out_shape=(wide,) * 4 + (part,) * SIDE,
         in_specs=[smem] + [anywhere] * 8,
-        out_specs=(anywhere, local, anywhere, local) + (local,) * SIDE,
+        out_specs=(pl.BlockSpec(memory_space=pltpu.HBM),) * 8,
         scratch_shapes=[
             pltpu.VMEM((32, HEAD), jnp.int32),
             pltpu.SMEM((32, HEAD), jnp.int32),
@@ -192,6 +192,7 @@
             pltpu.VMEM((2 * TOK, width), bf16),
             pltpu.VMEM((2 * TOK, width), bf16),
             pltpu.VMEM((2 * TOK, width), bf16),
+            pltpu.VMEM((SIDE, UNITS * TOK, 2 * HEAD), bf16),
             pltpu.VMEM((tokens, 2 * HEAD), bf16),
             pltpu.VMEM((tokens, 2 * HEAD), bf16),
             pltpu.VMEM((ROWS, HEAD), bf16),
@@ -206,6 +207,7 @@
             pltpu.SemaphoreType.DMA((4,)),
             pltpu.SemaphoreType.DMA,
             pltpu.SemaphoreType.DMA((4,)),
+            pltpu.SemaphoreType.DMA((SIDE,)),
         ],
         compiler_params=pltpu.CompilerParams(vmem_limit_bytes=VLIMIT * 2**20),
         name="attention",
@@ -213,6 +215,57 @@
 
 
 VLIMIT = 42
+
+
+def unit_kernel(core_ref, where_hbm, keys_hbm, values_hbm, mine_ref, other_ref, where, keys, values, sem):
+    copies = [
+        pltpu.make_async_copy(where_hbm, where, sem.at[0]),
+        pltpu.make_async_copy(keys_hbm, keys, sem.at[1]),
+        pltpu.make_async_copy(values_hbm, values, sem.at[2]),
+    ]
+    for copy in copies:
+        copy.start()
+    for copy in copies:
+        copy.wait()
+    lane = lax.broadcasted_iota(jnp.int32, (TAIL, 2 * HEAD), 1)
+    first, second = where[0] // RUN, where[RUN] // RUN
+    tail = jnp.where(lane == 0, first, jnp.where(lane == 1, second, 0)).astype(f32).astype(bf16)
+    mine_ref[TOK : TOK + TAIL, :] = tail
+    other_ref[TOK : TOK + TAIL, :] = tail
+
+    def fill(low_ref, high_ref):
+        low_ref[0:TOK, 0:HEAD] = keys[:, 0:HEAD]
+        low_ref[0:TOK, HEAD : 2 * HEAD] = values[:, 0:HEAD]
+        high_ref[0:TOK, 0:HEAD] = keys[:, HEAD : 2 * HEAD]
+        high_ref[0:TOK, HEAD : 2 * HEAD] = values[:, HEAD : 2 * HEAD]
+
+    @pl.when(core_ref[0] == 0)
+    def _():
+        fill(mine_ref, other_ref)
+
+    @pl.when(core_ref[0] != 0)
+    def _():
+        fill(other_ref, mine_ref)
+
+
+def key_units(core, positions, keys, values):
+    vmem = pl.BlockSpec(memory_space=pltpu.VMEM)
+    hbm = pl.BlockSpec(memory_space=pltpu.HBM)
+    unit = jax.ShapeDtypeStruct((TOK + TAIL, 2 * HEAD), bf16)
+    return pl.pallas_call(
+        unit_kernel,
+        out_shape=(unit, unit),
+        in_specs=[pl.BlockSpec(memory_space=pltpu.SMEM), hbm, hbm, hbm],
+        out_specs=(vmem, vmem),
+        scratch_shapes=[
+            pltpu.SMEM((TOK,), jnp.int32),
+            pltpu.VMEM((TOK, 2 * HEAD), bf16),
+            pltpu.VMEM((TOK, 2 * HEAD), bf16),
+            pltpu.SemaphoreType.DMA((3,)),
+        ],
+        compiler_params=pltpu.CompilerParams(vmem_limit_bytes=8 * 2**20),
+        name="units",
+    )(core, positions, keys, values)
 
 
 def swap(x):
@@ -239,15 +292,9 @@
         width = x.shape[1] // 2
         return lax.dynamic_slice_in_dim(x, which * width, width, axis=1)
 
-    run_ids = jnp.concatenate([positions[0:1], positions[RUN : RUN + 1]]) // RUN
-    tail = jnp.zeros((TAIL, 2 * HEAD), bf16).at[0, 0:2].set(run_ids.astype(bf16))
-
-    def unit(which):
-        return jnp.concatenate(
-            [jnp.concatenate([pick(keys, which), pick(values, which)], 1), tail], 0
-        )
-
-    kv_own = jnp.concatenate([unit(core), swap(unit(1 - core))], 0)
+    core_index = core.astype(jnp.int32).reshape(1)
+    kv_mine, kv_other = key_units(core_index, positions, keys, values)
+    kv_own = jnp.concatenate([kv_mine, swap(kv_other)], 0)
     line = [kv_own] + [shift(kv_own, 0, d) for d in ORDER]
     line = lax.optimization_barrier(tuple(line) + (queries, output_cotangent))
     queries, output_cotangent = line[4:]
@@ -257,7 +304,7 @@
     do_other = swap(pick(output_cotangent, 1 - core))
 
     results = attention(
-        core.astype(jnp.int32).reshape(1),
+        core_index,
         (queries, q_other),
         (output_cotangent, do_other),
         lines,

time: 96.1 us -> 87.5 us (0.911)
  Pallas kernels: 26.8 us -> 20.1 us
  starting transfers between devices: 30.6 us -> 36.4 us
  waiting for transfers between devices: 26.4 us -> 23.6 us
  local copies, waits for them, and re-layouts: 5.18 us -> 2.48 us
  other arithmetic: 5.94 us -> 3.94 us
    pallas_call x1 -> x2, Pallas kernels: 26.8 us -> 20.1 us  [the longest x1 19.5 us: attention(): pl.pallas_call(attention_kernel, out_shape=(wide,) * 4 + (part,) * SIDE,...]
    ppermute x12, starting transfers between devices: 18.1 us -> 23.8 us  [shift(): return lax.ppermute(x, ('outer', 'inner'), pairs)]
    ppermute x12, waiting for transfers between devices: 21.7 us -> 18.9 us  [shift(): return lax.ppermute(x, ('outer', 'inner'), pairs)]
    convert_element_type x1 -> x0, other arithmetic: 1.37 us -> none  [body(): run_ids.astype(bf16)]
    unnamed x21 -> x18, local copies, waits for them, and re-layouts: 3.67 us -> 2.38 us
    select_n x4 -> x3, other arithmetic: 4.22 us -> 3.61 us  [join(): jnp.where(core == 0, jnp.concatenate([mine, other], 1), jnp.concatenate([...]
  transfers between devices with their start and end apart: 18 -> 18, of which waited for: 15 -> 13; matrix products, arithmetic and copies ran while one was open for 3% -> 4% of each run, Pallas kernels for 0% -> 0%
where the time goes in v2:
time: 87.5 us; the launch traced here: 87.2 us
  starting transfers between devices  36.4 us (42%)
  waiting for transfers between devices  23.6 us (27%)
  Pallas kernels  20.1 us (23%)
  other arithmetic  3.94 us (5%)
  local copies, waits for them, and re-layouts  2.48 us (3%)
    ppermute x12, starting transfers between devices, shift(): return lax.ppermute(x, ('outer', 'inner'), pairs)  23.8 us
    pallas_call x1, Pallas kernels, attention(): pl.pallas_call(attention_kernel, out_shape=(wide,) * 4 + (part,) * SIDE,...  19.5 us
    ppermute x12, waiting for transfers between devices, shift(): return lax.ppermute(x, ('outer', 'inner'), pairs)  18.9 us
    ppermute x6, starting transfers between devices, swap(): lax.ppermute(x, ('outer', 'inner'), [(i, (i + 16) % 32) for i in range(32)])  12.6 us
    ppermute x6, waiting for transfers between devices, swap(): lax.ppermute(x, ('outer', 'inner'), [(i, (i + 16) % 32) for i in range(32)])  4.68 us
    select_n x3, other arithmetic, join(): jnp.where(core == 0, jnp.concatenate([mine, other], 1), jnp.concatenate([...  3.61 us
    unnamed x18, local copies, waits for them, and re-layouts  2.38 us
  transfers between devices with their start and end apart: 18, of which 13 were waited for; matrix products, arithmetic and copies ran while one was open for 4% of the time, Pallas kernels for 0%

profile of v2, /device:TPU:1, one launch (start us, length us, event | category | flops | bytes accessed | tf_op | source)
XLA Modules:
  0.0 87.2 jit_solution(3415031522731900531)
XLA Ops:
  3.6 1.5 %collective-permute-start = (bf16[144,256]{1,0:T(8,128)(2,1)S(1)}, bf16[144,256]{1,0:T(8,128)(2,1)S(1)}, u32[]{:S(2)}, u32[]{:S(2)}) collective-permute-start(bf16[144,256]{1,0:T(8,128)(2,1)S(1)} %get-tuple-element.21), channel_id=1, source_target_pairs={{0,64},{4,68},{8,72},{12,76},{16,80},{20,84},{24,88},{28,92},{32,9... | collective-permute-start | bytes 221192 | tf_op jit(solution)/shard_map/ppermute | solution.py:272
  5.1 0.9 %collective-permute-done = bf16[144,256]{1,0:T(8,128)(2,1)S(1)} collective-permute-done((bf16[144,256]{1,0:T(8,128)(2,1)S(1)}, bf16[144,256]{1,0:T(8,128)(2,1)S(1)}, u32[]{:S(2)}, u32[]{:S(2)}) %collective-permute-start) | collective-permute-done | bytes 73760 | tf_op jit(solution)/shard_map/ppermute | solution.py:272
  6.0 3.8 %collective-permute-start.1 = (bf16[288,256]{1,0:T(8,128)(2,1)S(1)}, bf16[288,256]{1,0:T(8,128)(2,1)S(1)}, u32[]{:S(2)}, u32[]{:S(2)}) collective-permute-start(bf16[288,256]{1,0:T(8,128)(2,1)S(1)} %constant_dynamic-update-slice_fusion), channel_id=1, source_target_pairs={{0,8},{4,12},{8,0},{12,4},{16,24},{20,28},{24,16},{28,20},{32,40},... | collective-permute-start | bytes 442376 | tf_op jit(solution)/shard_map/ppermute | solution.py:285
  10.5 1.9 %collective-permute-start.3 = (bf16[288,256]{1,0:T(8,128)(2,1)S(1)}, bf16[288,256]{1,0:T(8,128)(2,1)S(1)}, u32[]{:S(2)}, u32[]{:S(2)}) collective-permute-start(bf16[288,256]{1,0:T(8,128)(2,1)S(1)} %constant_dynamic-update-slice_fusion), channel_id=1, source_target_pairs={{0,12},{4,0},{8,4},{12,8},{16,28},{20,16},{24,20},{28,24},{32,44},... | collective-permute-start | bytes 442376 | tf_op jit(solution)/shard_map/ppermute | solution.py:285
  12.6 2.7 %collective-permute-done.2 = bf16[288,256]{1,0:T(8,128)(2,1)S(1)} collective-permute-done((bf16[288,256]{1,0:T(8,128)(2,1)S(1)}, bf16[288,256]{1,0:T(8,128)(2,1)S(1)}, u32[]{:S(2)}, u32[]{:S(2)}) %collective-permute-start.2) | collective-permute-done | bytes 147488 | tf_op jit(solution)/shard_map/ppermute | solution.py:285
  15.4 2.7 %collective-permute-start.6 = (bf16[1152,256]{1,0:T(8,128)(2,1)S(1)}, bf16[1152,256]{1,0:T(8,128)(2,1)S(1)}, u32[]{:S(2)}, u32[]{:S(2)}) collective-permute-start(bf16[1152,256]{1,0:T(8,128)(2,1)S(1)} %constant_dynamic-update-slice_fusion.2.refs_5_), channel_id=1, source_target_pairs={{0,32},{4,36},{8,40},{12,44},{16,48},{20,52},{24,56},{28,60},{32,0... | collective-permute-start | bytes 1769480 | tf_op jit(solution)/shard_map/ppermute | solution.py:285
  18.8 2.0 %collective-permute-start.8 = (bf16[1152,256]{1,0:T(8,128)(2,1)S(1)}, bf16[1152,256]{1,0:T(8,128)(2,1)S(1)}, u32[]{:S(2)}, u32[]{:S(2)}) collective-permute-start(bf16[1152,256]{1,0:T(8,128)(2,1)S(1)} %constant_dynamic-update-slice_fusion.2.refs_5_), channel_id=1, source_target_pairs={{0,48},{4,52},{8,56},{12,60},{16,0},{20,4},{24,8},{28,12},{32,16},... | collective-permute-start | bytes 1769480 | tf_op jit(solution)/shard_map/ppermute | solution.py:285
  20.8 2.7 %collective-permute-start.5 = (bf16[128,1024]{1,0:T(8,128)(2,1)S(1)}, bf16[128,1024]{1,0:T(8,128)(2,1)S(1)}, u32[]{:S(2)}, u32[]{:S(2)}) collective-permute-start(bf16[128,1024]{1,0:T(8,128)(2,1)S(1)} %constant_dynamic-slice_fusion), channel_id=1, source_target_pairs={{0,64},{4,68},{8,72},{12,76},{16,80},{20,84},{24,88},{28,92},{32,9... | collective-permute-start | bytes 786440 | tf_op jit(solution)/shard_map/ppermute | solution.py:272
  23.6 1.0 %collective-permute-done.5.refs_4_ = bf16[128,1024]{1,0:T(8,128)(2,1)S(1)} collective-permute-done((bf16[128,1024]{1,0:T(8,128)(2,1)S(1)}, bf16[128,1024]{1,0:T(8,128)(2,1)S(1)}, u32[]{:S(2)}, u32[]{:S(2)}) %collective-permute-start.5) | collective-permute-done | bytes 262176 | tf_op jit(solution)/shard_map/ppermute | solution.py:272
  25.1 0.9 %collective-permute-done.6.refs_6_ = bf16[1152,256]{1,0:T(8,128)(2,1)S(1)} collective-permute-done((bf16[1152,256]{1,0:T(8,128)(2,1)S(1)}, bf16[1152,256]{1,0:T(8,128)(2,1)S(1)}, u32[]{:S(2)}, u32[]{:S(2)}) %collective-permute-start.6) | collective-permute-done | bytes 589856 | tf_op jit(solution)/shard_map/ppermute | solution.py:285
  26.0 6.3 %collective-permute-done.7.refs_7_ = bf16[1152,256]{1,0:T(8,128)(2,1)S(1)} collective-permute-done((bf16[1152,256]{1,0:T(8,128)(2,1)S(1)}, bf16[1152,256]{1,0:T(8,128)(2,1)S(1)}, u32[]{:S(2)}, u32[]{:S(2)}) %collective-permute-start.7) | collective-permute-done | bytes 589856 | tf_op jit(solution)/shard_map/ppermute | solution.py:285
  32.7 19.5 %attention.1 = (bf16[128,1024]{1,0:T(8,128)(2,1)}, bf16[128,1024]{1,0:T(8,128)(2,1)}, bf16[128,1024]{1,0:T(8,128)(2,1)}, bf16[128,1024]{1,0:T(8,128)(2,1)}, bf16...) custom-call(s32[1]{0:T(128)} %bitcast.core_ref.refs_0_, ...), custom_call_target="tpu_custom_call" | custom-call | tf_op jit(solution)/shard_map/attention/pallas_call | solution.py:182
  52.2 4.8 %collective-permute-start.11 = (bf16[1024,256]{1,0:T(8,128)(2,1)}, bf16[1024,256]{1,0:T(8,128)(2,1)S(1)}, u32[]{:S(2)}, u32[]{:S(2)}) collective-permute-start(bf16[1024,256]{1,0:T(8,128)(2,1)} %get-tuple-element.33), channel_id=1, source_target_pairs={{0,32},{4,36},{8,40},{12,44},{16,48},{20,52},{24,56},{28,60},{32,0... | collective-permute-start | bytes 1572872 | tf_op jit(solution)/shard_map/ppermute | solution.py:285
  58.4 3.5 %collective-permute-start.10 = (bf16[128,1024]{1,0:T(8,128)(2,1)}, bf16[128,1024]{1,0:T(8,128)(2,1)S(1)}, u32[]{:S(2)}, u32[]{:S(2)}) collective-permute-start(bf16[128,1024]{1,0:T(8,128)(2,1)} %get-tuple-element.31), channel_id=1, source_target_pairs={{0,64},{4,68},{8,72},{12,76},{16,80},{20,84},{24,88},{28,92},{32,9... | collective-permute-start | bytes 786440 | tf_op jit(solution)/shard_map/ppermute | solution.py:272
  62.0 1.4 %collective-permute-done.10 = bf16[128,1024]{1,0:T(8,128)(2,1)S(1)} collective-permute-done((bf16[128,1024]{1,0:T(8,128)(2,1)}, bf16[128,1024]{1,0:T(8,128)(2,1)S(1)}, u32[]{:S(2)}, u32[]{:S(2)}) %collective-permute-start.10) | collective-permute-done | bytes 262176 | tf_op jit(solution)/shard_map/ppermute | solution.py:272
  63.3 2.0 %maximum_select_fusion.1 = bf16[128,2048]{1,0:T(8,128)(2,1)} fusion(bf16[128,1024]{1,0:T(8,128)(2,1)S(1)} %collective-permute-done.10, bf16[128,1024]{1,0:T(8,128)(2,1)} %get-tuple-element.30, pred[]{:T(512)S(6)} %eq.2), kind=kLoop, calls=%fused_computation.2 | loop fusion | flops 2359296 | bytes 1048577 | tf_op jit(solution)/shard_map/jit(_where)/select_n | solution.py:325
  65.3 5.6 %collective-permute-done.12 = bf16[1024,256]{1,0:T(8,128)(2,1)S(1)} collective-permute-done((bf16[1024,256]{1,0:T(8,128)(2,1)}, bf16[1024,256]{1,0:T(8,128)(2,1)S(1)}, u32[]{:S(2)}, u32[]{:S(2)}) %collective-permute-start.12) | collective-permute-done | bytes 524320 | tf_op jit(solution)/shard_map/ppermute | solution.py:285
  71.2 4.3 %collective-permute-start.14 = (bf16[256,256]{1,0:T(8,128)(2,1)S(1)}, bf16[256,256]{1,0:T(8,128)(2,1)S(1)}, u32[]{:S(2)}, u32[]{:S(2)}) collective-permute-start(bf16[256,256]{1,0:T(8,128)(2,1)S(1)} %get-tuple-element.36), channel_id=1, source_target_pairs={{0,8},{4,12},{8,0},{12,4},{16,24},{20,28},{24,16},{28,20},{32,40},... | collective-permute-start | bytes 393224 | tf_op jit(solution)/shard_map/ppermute | solution.py:285
  75.5 1.5 %collective-permute-start.16 = (bf16[256,256]{1,0:T(8,128)(2,1)S(1)}, bf16[256,256]{1,0:T(8,128)(2,1)S(1)}, u32[]{:S(2)}, u32[]{:S(2)}) collective-permute-start(bf16[256,256]{1,0:T(8,128)(2,1)S(1)} %get-tuple-element.37), channel_id=1, source_target_pairs={{0,4},{4,8},{8,12},{12,0},{16,20},{20,24},{24,28},{28,16},{32,36},... | collective-permute-start | bytes 393224 | tf_op jit(solution)/shard_map/ppermute | solution.py:285
  77.0 0.9 %maximum_select_fusion = bf16[128,2048]{1,0:T(8,128)(2,1)} fusion(bf16[128,1024]{1,0:T(8,128)(2,1)S(1)} %collective-permute-done.9, bf16[128,1024]{1,0:T(8,128)(2,1)S(1)} %copy-done.6, pred[]{:T(512)S(6)} %eq.2), kind=kLoop, calls=%fused_computation.1 | loop fusion | flops 2359296 | bytes 1048577 | tf_op jit(solution)/shard_map/jit(_where)/select_n | solution.py:325
  77.9 1.4 %collective-permute-done.15 = bf16[256,256]{1,0:T(8,128)(2,1)S(1)} collective-permute-done((bf16[256,256]{1,0:T(8,128)(2,1)S(1)}, bf16[256,256]{1,0:T(8,128)(2,1)S(1)}, u32[]{:S(2)}, u32[]{:S(2)}) %collective-permute-start.15) | collective-permute-done | bytes 131104 | tf_op jit(solution)/shard_map/ppermute | solution.py:285
  79.3 1.5 %collective-permute-done.16 = bf16[256,256]{1,0:T(8,128)(2,1)S(1)} collective-permute-done((bf16[256,256]{1,0:T(8,128)(2,1)S(1)}, bf16[256,256]{1,0:T(8,128)(2,1)S(1)}, u32[]{:S(2)}, u32[]{:S(2)}) %collective-permute-start.16) | collective-permute-done | bytes 131104 | tf_op jit(solution)/shard_map/ppermute | solution.py:285
  80.9 4.7 %collective-permute-start.17 = (bf16[128,256]{1,0:T(8,128)(2,1)S(1)}, bf16[128,256]{1,0:T(8,128)(2,1)S(1)}, u32[]{:S(2)}, u32[]{:S(2)}) collective-permute-start(bf16[128,256]{1,0:T(8,128)(2,1)S(1)} %slice.44), channel_id=1, source_target_pairs={{0,64},{4,68},{8,72},{12,76},{16,80},{20,84},{24,88},{28,92},{32,9... | collective-permute-start | bytes 196616 | tf_op jit(solution)/shard_map/ppermute | solution.py:272
  85.6 0.9 %collective-permute-done.17 = bf16[128,256]{1,0:T(8,128)(2,1)S(1)} collective-permute-done((bf16[128,256]{1,0:T(8,128)(2,1)S(1)}, bf16[128,256]{1,0:T(8,128)(2,1)S(1)}, u32[]{:S(2)}, u32[]{:S(2)}) %collective-permute-start.17) | collective-permute-done | bytes 65568 | tf_op jit(solution)/shard_map/ppermute | solution.py:272
  (45 shorter events, 8.1 us)
Async XLA Ops:
  1.3 0.8 copy-start.2
  2.1 0.8 copy-start.3
  3.6 2.4 %collective-permute-start = (bf16[144,256]{1,0:T(8,128)(2,1)S(1)}, bf16[144,256]{1,0:T(8,128)(2,1)S(1)}, u32[]{:S(2)}, u32[]{:S(2)}) collective-permute-start(bf16[144,256]{1,0:T(8,128)(2,1)S(1)} %get-tuple-element.21), channel_id=1, source_target_pairs={{0,64},{4,68},{8,72},{12,76},{16,80},{20,84},{24,88},{28,92},{32,9... | collective-permute-start | bytes 221192 | tf_op jit(solution)/shard_map/ppermute | solution.py:272
  6.0 14.7 %copy-start.1 = (bf16[128,2048]{1,0:T(8,128)(2,1)S(1)}, bf16[128,2048]{1,0:T(8,128)(2,1)}, u32[]{:S(2)}) copy-start(bf16[128,2048]{1,0:T(8,128)(2,1)} %refs_3_) | copy-start | bytes 1572868
  6.0 6.6 %collective-permute-start.1 = (bf16[288,256]{1,0:T(8,128)(2,1)S(1)}, bf16[288,256]{1,0:T(8,128)(2,1)S(1)}, u32[]{:S(2)}, u32[]{:S(2)}) collective-permute-start(bf16[288,256]{1,0:T(8,128)(2,1)S(1)} %constant_dynamic-update-slice_fusion), channel_id=1, source_target_pairs={{0,8},{4,12},{8,0},{12,4},{16,24},{20,28},{24,16},{28,20},{32,40},... | collective-permute-start | bytes 442376 | tf_op jit(solution)/shard_map/ppermute | solution.py:285
  9.8 5.5 %collective-permute-start.2 = (bf16[288,256]{1,0:T(8,128)(2,1)S(1)}, bf16[288,256]{1,0:T(8,128)(2,1)S(1)}, u32[]{:S(2)}, u32[]{:S(2)}) collective-permute-start(bf16[288,256]{1,0:T(8,128)(2,1)S(1)} %constant_dynamic-update-slice_fusion), channel_id=1, source_target_pairs={{0,4},{4,8},{8,12},{12,0},{16,20},{20,24},{24,28},{28,16},{32,36},... | collective-permute-start | bytes 442376 | tf_op jit(solution)/shard_map/ppermute | solution.py:285
  10.5 4.8 %collective-permute-start.3 = (bf16[288,256]{1,0:T(8,128)(2,1)S(1)}, bf16[288,256]{1,0:T(8,128)(2,1)S(1)}, u32[]{:S(2)}, u32[]{:S(2)}) collective-permute-start(bf16[288,256]{1,0:T(8,128)(2,1)S(1)} %constant_dynamic-update-slice_fusion), channel_id=1, source_target_pairs={{0,12},{4,0},{8,4},{12,8},{16,28},{20,16},{24,20},{28,24},{32,44},... | collective-permute-start | bytes 442376 | tf_op jit(solution)/shard_map/ppermute | solution.py:285
  15.3 8.2 %copy-start = (bf16[128,2048]{1,0:T(8,128)(2,1)S(1)}, bf16[128,2048]{1,0:T(8,128)(2,1)}, u32[]{:S(2)}) copy-start(bf16[128,2048]{1,0:T(8,128)(2,1)} %refs_1_) | copy-start | bytes 1572868
  15.4 10.7 %collective-permute-start.6 = (bf16[1152,256]{1,0:T(8,128)(2,1)S(1)}, bf16[1152,256]{1,0:T(8,128)(2,1)S(1)}, u32[]{:S(2)}, u32[]{:S(2)}) collective-permute-start(bf16[1152,256]{1,0:T(8,128)(2,1)S(1)} %constant_dynamic-update-slice_fusion.2.refs_5_), channel_id=1, source_target_pairs={{0,32},{4,36},{8,40},{12,44},{16,48},{20,52},{24,56},{28,60},{32,0... | collective-permute-start | bytes 1769480 | tf_op jit(solution)/shard_map/ppermute | solution.py:285
  18.1 14.2 %collective-permute-start.7 = (bf16[1152,256]{1,0:T(8,128)(2,1)S(1)}, bf16[1152,256]{1,0:T(8,128)(2,1)S(1)}, u32[]{:S(2)}, u32[]{:S(2)}) collective-permute-start(bf16[1152,256]{1,0:T(8,128)(2,1)S(1)} %constant_dynamic-update-slice_fusion.2.refs_5_), channel_id=1, source_target_pairs={{0,16},{4,20},{8,24},{12,28},{16,32},{20,36},{24,40},{28,44},{32,4... | collective-permute-start | bytes 1769480 | tf_op jit(solution)/shard_map/ppermute | solution.py:285
  18.8 13.9 %collective-permute-start.8 = (bf16[1152,256]{1,0:T(8,128)(2,1)S(1)}, bf16[1152,256]{1,0:T(8,128)(2,1)S(1)}, u32[]{:S(2)}, u32[]{:S(2)}) collective-permute-start(bf16[1152,256]{1,0:T(8,128)(2,1)S(1)} %constant_dynamic-update-slice_fusion.2.refs_5_), channel_id=1, source_target_pairs={{0,48},{4,52},{8,56},{12,60},{16,0},{20,4},{24,8},{28,12},{32,16},... | collective-permute-start | bytes 1769480 | tf_op jit(solution)/shard_map/ppermute | solution.py:285
  20.8 3.9 %collective-permute-start.5 = (bf16[128,1024]{1,0:T(8,128)(2,1)S(1)}, bf16[128,1024]{1,0:T(8,128)(2,1)S(1)}, u32[]{:S(2)}, u32[]{:S(2)}) collective-permute-start(bf16[128,1024]{1,0:T(8,128)(2,1)S(1)} %constant_dynamic-slice_fusion), channel_id=1, source_target_pairs={{0,64},{4,68},{8,72},{12,76},{16,80},{20,84},{24,88},{28,92},{32,9... | collective-permute-start | bytes 786440 | tf_op jit(solution)/shard_map/ppermute | solution.py:272
  23.5 1.6 %collective-permute-start.4 = (bf16[128,1024]{1,0:T(8,128)(2,1)S(1)}, bf16[128,1024]{1,0:T(8,128)(2,1)S(1)}, u32[]{:S(2)}, u32[]{:S(2)}) collective-permute-start(bf16[128,1024]{1,0:T(8,128)(2,1)S(1)} %constant_dynamic-slice_fusion.1), channel_id=1, source_target_pairs={{0,64},{4,68},{8,72},{12,76},{16,80},{20,84},{24,88},{28,92},{32,9... | collective-permute-start | bytes 786440 | tf_op jit(solution)/shard_map/ppermute | solution.py:272
  52.2 13.2 %collective-permute-start.11 = (bf16[1024,256]{1,0:T(8,128)(2,1)}, bf16[1024,256]{1,0:T(8,128)(2,1)S(1)}, u32[]{:S(2)}, u32[]{:S(2)}) collective-permute-start(bf16[1024,256]{1,0:T(8,128)(2,1)} %get-tuple-element.33), channel_id=1, source_target_pairs={{0,32},{4,36},{8,40},{12,44},{16,48},{20,52},{24,56},{28,60},{32,0... | collective-permute-start | bytes 1572872 | tf_op jit(solution)/shard_map/ppermute | solution.py:285
  57.0 13.9 %collective-permute-start.12 = (bf16[1024,256]{1,0:T(8,128)(2,1)}, bf16[1024,256]{1,0:T(8,128)(2,1)S(1)}, u32[]{:S(2)}, u32[]{:S(2)}) collective-permute-start(bf16[1024,256]{1,0:T(8,128)(2,1)} %get-tuple-element.34), channel_id=1, source_target_pairs={{0,48},{4,52},{8,56},{12,60},{16,0},{20,4},{24,8},{28,12},{32,16},... | collective-permute-start | bytes 1572872 | tf_op jit(solution)/shard_map/ppermute | solution.py:285
  57.7 13.2 %collective-permute-start.13 = (bf16[1024,256]{1,0:T(8,128)(2,1)}, bf16[1024,256]{1,0:T(8,128)(2,1)S(1)}, u32[]{:S(2)}, u32[]{:S(2)}) collective-permute-start(bf16[1024,256]{1,0:T(8,128)(2,1)} %get-tuple-element.35), channel_id=1, source_target_pairs={{0,16},{4,20},{8,24},{12,28},{16,32},{20,36},{24,40},{28,44},{32,4... | collective-permute-start | bytes 1572872 | tf_op jit(solution)/shard_map/ppermute | solution.py:285
  58.4 4.9 %collective-permute-start.10 = (bf16[128,1024]{1,0:T(8,128)(2,1)}, bf16[128,1024]{1,0:T(8,128)(2,1)S(1)}, u32[]{:S(2)}, u32[]{:S(2)}) collective-permute-start(bf16[128,1024]{1,0:T(8,128)(2,1)} %get-tuple-element.31), channel_id=1, source_target_pairs={{0,64},{4,68},{8,72},{12,76},{16,80},{20,84},{24,88},{28,92},{32,9... | collective-permute-start | bytes 786440 | tf_op jit(solution)/shard_map/ppermute | solution.py:272
  62.0 15.0 %collective-permute-start.9 = (bf16[128,1024]{1,0:T(8,128)(2,1)}, bf16[128,1024]{1,0:T(8,128)(2,1)S(1)}, u32[]{:S(2)}, u32[]{:S(2)}) collective-permute-start(bf16[128,1024]{1,0:T(8,128)(2,1)} %get-tuple-element.29), channel_id=1, source_target_pairs={{0,64},{4,68},{8,72},{12,76},{16,80},{20,84},{24,88},{28,92},{32,9... | collective-permute-start | bytes 786440 | tf_op jit(solution)/shard_map/ppermute | solution.py:272
  63.3 7.6 %copy-start.5 = (bf16[1024,256]{1,0:T(8,128)(2,1)S(1)}, bf16[1024,256]{1,0:T(8,128)(2,1)}, u32[]{:S(2)}) copy-start(bf16[1024,256]{1,0:T(8,128)(2,1)} %get-tuple-element.32) | copy-start | bytes 1572868
  71.2 5.8 %copy-start.6 = (bf16[128,1024]{1,0:T(8,128)(2,1)S(1)}, bf16[128,1024]{1,0:T(8,128)(2,1)}, u32[]{:S(2)}) copy-start(bf16[128,1024]{1,0:T(8,128)(2,1)} %get-tuple-element.28) | copy-start | bytes 786436
  71.2 6.7 %collective-permute-start.14 = (bf16[256,256]{1,0:T(8,128)(2,1)S(1)}, bf16[256,256]{1,0:T(8,128)(2,1)S(1)}, u32[]{:S(2)}, u32[]{:S(2)}) collective-permute-start(bf16[256,256]{1,0:T(8,128)(2,1)S(1)} %get-tuple-element.36), channel_id=1, source_target_pairs={{0,8},{4,12},{8,0},{12,4},{16,24},{20,28},{24,16},{28,20},{32,40},... | collective-permute-start | bytes 393224 | tf_op jit(solution)/shard_map/ppermute | solution.py:285
  75.5 3.8 %collective-permute-start.15 = (bf16[256,256]{1,0:T(8,128)(2,1)S(1)}, bf16[256,256]{1,0:T(8,128)(2,1)S(1)}, u32[]{:S(2)}, u32[]{:S(2)}) collective-permute-start(bf16[256,256]{1,0:T(8,128)(2,1)S(1)} %get-tuple-element.38), channel_id=1, source_target_pairs={{0,12},{4,0},{8,4},{12,8},{16,28},{20,16},{24,20},{28,24},{32,44},... | collective-permute-start | bytes 393224 | tf_op jit(solution)/shard_map/ppermute | solution.py:285
  75.5 5.3 %collective-permute-start.16 = (bf16[256,256]{1,0:T(8,128)(2,1)S(1)}, bf16[256,256]{1,0:T(8,128)(2,1)S(1)}, u32[]{:S(2)}, u32[]{:S(2)}) collective-permute-start(bf16[256,256]{1,0:T(8,128)(2,1)S(1)} %get-tuple-element.37), channel_id=1, source_target_pairs={{0,4},{4,8},{8,12},{12,0},{16,20},{20,24},{24,28},{28,16},{32,36},... | collective-permute-start | bytes 393224 | tf_op jit(solution)/shard_map/ppermute | solution.py:285
  80.9 5.6 %collective-permute-start.17 = (bf16[128,256]{1,0:T(8,128)(2,1)S(1)}, bf16[128,256]{1,0:T(8,128)(2,1)S(1)}, u32[]{:S(2)}, u32[]{:S(2)}) collective-permute-start(bf16[128,256]{1,0:T(8,128)(2,1)S(1)} %slice.44), channel_id=1, source_target_pairs={{0,64},{4,68},{8,72},{12,76},{16,80},{20,84},{24,88},{28,92},{32,9... | collective-permute-start | bytes 196616 | tf_op jit(solution)/shard_map/ppermute | solution.py:272
  (1 other events, 0.7 us)

commit v3 on v2

--- a/solution.py
+++ b/solution.py
@@ -41,24 +41,11 @@
     kv_refs = refs[5:9]
     out_refs, gq_refs = refs[9:11], refs[11:13]
     dkv_refs = refs[13:17]
-    (ids_v, ids_s, kv, qs, dos, outs, gqs, dkv, ka, va, qn, qt, don, dot_t, sbuf, wbuf) = refs[17:33]
-    (dka, dva, kv_sem, q_sem, ids_sem, out_sem, dkv_sem) = refs[33:]
+    (ids_v, ids_s, outs, gqs, dkv, ka, va, qn, qt, don, dot_t, sbuf, wbuf) = refs[17:30]
+    (dka, dva, ids_sem, out_sem, dkv_sem) = refs[30:]
     tokens = BLOCKS * RUN
     step = TOK + TAIL
     width = HEADS * HEAD
-
-    kv_copies = [
-        pltpu.make_async_copy(kv_refs[part], kv.at[part], kv_sem.at[part]) for part in range(SIDE)
-    ]
-    own_columns = pl.ds(pl.multiple_of(core_ref[0] * width, width), width)
-    q_copies = [
-        pltpu.make_async_copy(q_refs[0].at[:, own_columns], qs.at[0:TOK], q_sem.at[0]),
-        pltpu.make_async_copy(q_refs[1], qs.at[TOK : 2 * TOK], q_sem.at[1]),
-        pltpu.make_async_copy(do_refs[0].at[:, own_columns], dos.at[0:TOK], q_sem.at[2]),
-        pltpu.make_async_copy(do_refs[1], dos.at[TOK : 2 * TOK], q_sem.at[3]),
-    ]
-    for copy in kv_copies + q_copies:
-        copy.start()
 
     lane = lax.broadcasted_iota(jnp.int32, (RUN, HEAD), 1)
     sub = lax.broadcasted_iota(jnp.int32, (RUN, HEAD), 0)
@@ -76,9 +63,8 @@
         dva[s, :] = jnp.zeros((CHUNK, HEAD), f32)
 
     for part in range(SIDE):
-        kv_copies[part].wait()
         for unit in range(UNITS):
-            tail = kv[part, unit * step + TOK : (unit + 1) * step, 0:HEAD]
+            tail = kv_refs[part][unit * step + TOK : (unit + 1) * step, 0:HEAD]
             row = part * UNITS + unit
             ids_v[row : row + 1, :] = tail.astype(f32)[0:1, :].astype(jnp.int32)
     fetch = pltpu.make_async_copy(ids_v, ids_s, ids_sem)
@@ -91,17 +77,11 @@
                 where = ids_s[part * UNITS + unit, run]
                 place = pl.ds(pl.multiple_of(where * RUN, RUN), RUN)
                 first = unit * step + run * RUN
-                ka[place, 0:HEAD] = kv[part, first : first + RUN, 0:HEAD]
-                va[place, 0:HEAD] = kv[part, first : first + RUN, HEAD : 2 * HEAD]
-
-    for copy in q_copies:
-        copy.wait()
+                ka[place, 0:HEAD] = kv_refs[part][first : first + RUN, 0:HEAD]
+                va[place, 0:HEAD] = kv_refs[part][first : first + RUN, HEAD : 2 * HEAD]
 
     def run_block(a, position, length):
         rows = pl.ds(pl.multiple_of(a * RUN, RUN), RUN)
-        for h in range(HEADS):
-            qn[h * RUN : (h + 1) * RUN, :] = qs[rows, h * HEAD : (h + 1) * HEAD]
-            don[h * RUN : (h + 1) * RUN, :] = dos[rows, h * HEAD : (h + 1) * HEAD]
         qt[0:HEAD, :] = jnp.transpose(qn[...])
         for j in range(length // RUN):
             mask = jnp.where(diff <= (position - j) * RUN, 0.0, NEG).astype(bf16)
@@ -142,6 +122,22 @@
     def _(a):
         position = ids_s[a // 2, a % 2]
         needed = (position + 1) * RUN
+        line = pl.ds(pl.multiple_of(a % 2 * RUN, RUN), RUN)
+
+        def take(q_ref, do_ref, base):
+            for h in range(HEADS):
+                columns = pl.ds(pl.multiple_of(base + h * HEAD, HEAD), HEAD)
+                qn[h * RUN : (h + 1) * RUN, :] = q_ref[line, columns]
+                don[h * RUN : (h + 1) * RUN, :] = do_ref[line, columns]
+
+        @pl.when(a < 2)
+        def _():
+            take(q_refs[0], do_refs[0], core_ref[0] * width)
+
+        @pl.when(a >= 2)
+        def _():
+            take(q_refs[1], do_refs[1], 0)
+
         for short, length in zip((0,) + LENGTHS, LENGTHS):
 
             @pl.when((needed > short) & (needed <= length))
@@ -173,7 +169,7 @@
 
 
 def attention(core, q, do, kv):
-    anywhere = pl.BlockSpec(memory_space=pl.ANY)
+    local = pl.BlockSpec(memory_space=pltpu.VMEM)
     smem = pl.BlockSpec(memory_space=pltpu.SMEM)
     tokens = BLOCKS * RUN
     width = HEADS * HEAD
@@ -182,14 +178,11 @@
     return pl.pallas_call(
         attention_kernel,
         out_shape=(wide,) * 4 + (part,) * SIDE,
-        in_specs=[smem] + [anywhere] * 8,
+        in_specs=[smem] + [local] * 8,
         out_specs=(pl.BlockSpec(memory_space=pltpu.HBM),) * 8,
         scratch_shapes=[
             pltpu.VMEM((32, HEAD), jnp.int32),
             pltpu.SMEM((32, HEAD), jnp.int32),
-            pltpu.VMEM((SIDE, UNITS * (TOK + TAIL), 2 * HEAD), bf16),
-            pltpu.VMEM((2 * TOK, width), bf16),
-            pltpu.VMEM((2 * TOK, width), bf16),
             pltpu.VMEM((2 * TOK, width), bf16),
             pltpu.VMEM((2 * TOK, width), bf16),
             pltpu.VMEM((SIDE, UNITS * TOK, 2 * HEAD), bf16),
@@ -203,8 +196,6 @@
             pltpu.VMEM((tokens, ROWS), bf16),
             pltpu.VMEM((tokens, HEAD), f32),
             pltpu.VMEM((tokens, HEAD), f32),
-            pltpu.SemaphoreType.DMA((SIDE,)),
-            pltpu.SemaphoreType.DMA((4,)),
             pltpu.SemaphoreType.DMA,
             pltpu.SemaphoreType.DMA((4,)),
             pltpu.SemaphoreType.DMA((SIDE,)),
@@ -214,7 +205,7 @@
     )(core, *q, *do, *kv)
 
 
-VLIMIT = 42
+VLIMIT = 40
 
 
 def unit_kernel(core_ref, where_hbm, keys_hbm, values_hbm, mine_ref, other_ref, where, keys, values, sem):
@@ -265,7 +256,7 @@
         ],
         compiler_params=pltpu.CompilerParams(vmem_limit_bytes=8 * 2**20),
         name="units",
-    )(core, positions, keys, values)
+    )(core, *(pltpu.with_memory_space_constraint(x, pltpu.HBM) for x in (positions, keys, values)))
 
 
 def swap(x):

time: 87.5 us -> 87.6 us (level); the launches traced: 87.2 us -> 89.3 us
  starting transfers between devices: 36.4 us -> 42.7 us
  Pallas kernels: 20.1 us -> 16.9 us
  local copies, waits for them, and re-layouts: 2.48 us -> 0.16 us
  waiting for transfers between devices: 23.6 us -> 24.8 us
    ppermute x12, starting transfers between devices: 23.8 us -> 28 us  [shift(): return lax.ppermute(x, ('outer', 'inner'), pairs)]
    pallas_call x1, Pallas kernels: 19.5 us -> 16 us  [attention(): pl.pallas_call(attention_kernel, out_shape=(wide,) * 4 + (part,) * SIDE,...]
    unnamed x18 -> x12, local copies, waits for them, and re-layouts: 2.38 us -> 0.06 us
    ppermute x6, starting transfers between devices: 12.6 us -> 14.8 us  [swap(): lax.ppermute(x, ('outer', 'inner'), [(i, (i + 16) % 32) for i in range(32)])]
    ppermute x12, waiting for transfers between devices: 18.9 us -> 20.1 us  [shift(): return lax.ppermute(x, ('outer', 'inner'), pairs)]
where the time goes in v3:
time: 87.6 us; the launch traced here: 89.3 us
  starting transfers between devices  42.7 us (49%)
  waiting for transfers between devices  24.8 us (28%)
  Pallas kernels  16.9 us (19%)
  other arithmetic  3.94 us (4%)
    ppermute x12, starting transfers between devices, shift(): return lax.ppermute(x, ('outer', 'inner'), pairs)  28 us
    ppermute x12, waiting for transfers between devices, shift(): return lax.ppermute(x, ('outer', 'inner'), pairs)  20.1 us
    pallas_call x1, Pallas kernels, attention(): pl.pallas_call(attention_kernel, out_shape=(wide,) * 4 + (part,) * SIDE,...  16 us
    ppermute x6, starting transfers between devices, swap(): lax.ppermute(x, ('outer', 'inner'), [(i, (i + 16) % 32) for i in range(32)])  14.8 us
    ppermute x6, waiting for transfers between devices, swap(): lax.ppermute(x, ('outer', 'inner'), [(i, (i + 16) % 32) for i in range(32)])  4.68 us
    select_n x3, other arithmetic, join(): jnp.where(core == 0, jnp.concatenate([mine, other], 1), jnp.concatenate([...  3.61 us
  transfers between devices with their start and end apart: 18, of which 13 were waited for; matrix products, arithmetic and copies ran while one was open for 4% of the time, Pallas kernels for 0%

profile of v3, /device:TPU:1, one launch (start us, length us, event | category | flops | bytes accessed | tf_op | source)
XLA Modules:
  0.0 89.3 jit_solution(17742510533921529610)
XLA Ops:
  0.6 0.9 %units.1 = (bf16[144,256]{1,0:T(8,128)(2,1)S(1)}, bf16[144,256]{1,0:T(8,128)(2,1)S(1)}) custom-call(s32[1]{0:T(128)} %bitcast.core_ref.refs_0_, s32[128]{0:T(128)} %where_hbm.1, bf16[128,256]{1,0:T(8,128)(2,1)} %keys_hbm.1, bf16[128,256]{1,0:T(8,128)(2,1)} %values_hbm.1), custom_call_target="tpu_custom_call" | custom-call | tf_op jit(solution)/shard_map/units/pallas_call | solution.py:246
  1.6 1.5 %collective-permute-start = (bf16[144,256]{1,0:T(8,128)(2,1)S(1)}, bf16[144,256]{1,0:T(8,128)(2,1)S(1)}, u32[]{:S(2)}, u32[]{:S(2)}) collective-permute-start(bf16[144,256]{1,0:T(8,128)(2,1)S(1)} %get-tuple-element.21), channel_id=1, source_target_pairs={{0,64},{4,68},{8,72},{12,76},{16,80},{20,84},{24,88},{28,92},{32,9... | collective-permute-start | bytes 221192 | tf_op jit(solution)/shard_map/ppermute | solution.py:263
  3.1 0.9 %collective-permute-done = bf16[144,256]{1,0:T(8,128)(2,1)S(1)} collective-permute-done((bf16[144,256]{1,0:T(8,128)(2,1)S(1)}, bf16[144,256]{1,0:T(8,128)(2,1)S(1)}, u32[]{:S(2)}, u32[]{:S(2)}) %collective-permute-start) | collective-permute-done | bytes 73760 | tf_op jit(solution)/shard_map/ppermute | solution.py:263
  4.0 3.8 %collective-permute-start.1 = (bf16[288,256]{1,0:T(8,128)(2,1)S(1)}, bf16[288,256]{1,0:T(8,128)(2,1)S(1)}, u32[]{:S(2)}, u32[]{:S(2)}) collective-permute-start(bf16[288,256]{1,0:T(8,128)(2,1)S(1)} %constant_dynamic-update-slice_fusion), channel_id=1, source_target_pairs={{0,8},{4,12},{8,0},{12,4},{16,24},{20,28},{24,16},{28,20},{32,40},... | collective-permute-start | bytes 442376 | tf_op jit(solution)/shard_map/ppermute | solution.py:276
  8.5 1.9 %collective-permute-start.3 = (bf16[288,256]{1,0:T(8,128)(2,1)S(1)}, bf16[288,256]{1,0:T(8,128)(2,1)S(1)}, u32[]{:S(2)}, u32[]{:S(2)}) collective-permute-start(bf16[288,256]{1,0:T(8,128)(2,1)S(1)} %constant_dynamic-update-slice_fusion), channel_id=1, source_target_pairs={{0,12},{4,0},{8,4},{12,8},{16,28},{20,16},{24,20},{28,24},{32,44},... | collective-permute-start | bytes 442376 | tf_op jit(solution)/shard_map/ppermute | solution.py:276
  10.6 2.7 %collective-permute-done.2 = bf16[288,256]{1,0:T(8,128)(2,1)S(1)} collective-permute-done((bf16[288,256]{1,0:T(8,128)(2,1)S(1)}, bf16[288,256]{1,0:T(8,128)(2,1)S(1)}, u32[]{:S(2)}, u32[]{:S(2)}) %collective-permute-start.2) | collective-permute-done | bytes 147488 | tf_op jit(solution)/shard_map/ppermute | solution.py:276
  13.3 2.7 %collective-permute-start.6 = (bf16[1152,256]{1,0:T(8,128)(2,1)S(1)}, bf16[1152,256]{1,0:T(8,128)(2,1)S(1)}, u32[]{:S(2)}, u32[]{:S(2)}) collective-permute-start(bf16[1152,256]{1,0:T(8,128)(2,1)S(1)} %constant_dynamic-update-slice_fusion.2.refs_5_), channel_id=1, source_target_pairs={{0,32},{4,36},{8,40},{12,44},{16,48},{20,52},{24,56},{28,60},{32,0... | collective-permute-start | bytes 1769480 | tf_op jit(solution)/shard_map/ppermute | solution.py:276
  16.7 2.0 %collective-permute-start.8 = (bf16[1152,256]{1,0:T(8,128)(2,1)S(1)}, bf16[1152,256]{1,0:T(8,128)(2,1)S(1)}, u32[]{:S(2)}, u32[]{:S(2)}) collective-permute-start(bf16[1152,256]{1,0:T(8,128)(2,1)S(1)} %constant_dynamic-update-slice_fusion.2.refs_5_), channel_id=1, source_target_pairs={{0,48},{4,52},{8,56},{12,60},{16,0},{20,4},{24,8},{28,12},{32,16},... | collective-permute-start | bytes 1769480 | tf_op jit(solution)/shard_map/ppermute | solution.py:276
  18.7 2.7 %collective-permute-start.5 = (bf16[128,1024]{1,0:T(8,128)(2,1)S(1)}, bf16[128,1024]{1,0:T(8,128)(2,1)S(1)}, u32[]{:S(2)}, u32[]{:S(2)}) collective-permute-start(bf16[128,1024]{1,0:T(8,128)(2,1)S(1)} %constant_dynamic-slice_fusion), channel_id=1, source_target_pairs={{0,64},{4,68},{8,72},{12,76},{16,80},{20,84},{24,88},{28,92},{32,9... | collective-permute-start | bytes 786440 | tf_op jit(solution)/shard_map/ppermute | solution.py:263
  21.6 1.0 %collective-permute-done.5.refs_4_ = bf16[128,1024]{1,0:T(8,128)(2,1)S(1)} collective-permute-done((bf16[128,1024]{1,0:T(8,128)(2,1)S(1)}, bf16[128,1024]{1,0:T(8,128)(2,1)S(1)}, u32[]{:S(2)}, u32[]{:S(2)}) %collective-permute-start.5) | collective-permute-done | bytes 262176 | tf_op jit(solution)/shard_map/ppermute | solution.py:263
  23.1 0.9 %collective-permute-done.6.refs_6_ = bf16[1152,256]{1,0:T(8,128)(2,1)S(1)} collective-permute-done((bf16[1152,256]{1,0:T(8,128)(2,1)S(1)}, bf16[1152,256]{1,0:T(8,128)(2,1)S(1)}, u32[]{:S(2)}, u32[]{:S(2)}) %collective-permute-start.6) | collective-permute-done | bytes 589856 | tf_op jit(solution)/shard_map/ppermute | solution.py:276
  24.0 6.3 %collective-permute-done.7.refs_7_ = bf16[1152,256]{1,0:T(8,128)(2,1)S(1)} collective-permute-done((bf16[1152,256]{1,0:T(8,128)(2,1)S(1)}, bf16[1152,256]{1,0:T(8,128)(2,1)S(1)}, u32[]{:S(2)}, u32[]{:S(2)}) %collective-permute-start.7) | collective-permute-done | bytes 589856 | tf_op jit(solution)/shard_map/ppermute | solution.py:276
  30.7 16.0 %attention.1 = (bf16[128,1024]{1,0:T(8,128)(2,1)}, bf16[128,1024]{1,0:T(8,128)(2,1)}, bf16[128,1024]{1,0:T(8,128)(2,1)}, bf16[128,1024]{1,0:T(8,128)(2,1)}, bf16...) custom-call(s32[1]{0:T(128)} %bitcast.core_ref.refs_0_, ...), custom_call_target="tpu_custom_call" | custom-call | tf_op jit(solution)/shard_map/attention/pallas_call | solution.py:178
  46.7 1.8 %collective-permute-start.11 = (bf16[1024,256]{1,0:T(8,128)(2,1)}, bf16[1024,256]{1,0:T(8,128)(2,1)S(1)}, u32[]{:S(2)}, u32[]{:S(2)}) collective-permute-start(bf16[1024,256]{1,0:T(8,128)(2,1)} %get-tuple-element.33), channel_id=1, source_target_pairs={{0,32},{4,36},{8,40},{12,44},{16,48},{20,52},{24,56},{28,60},{32,0... | collective-permute-start | bytes 1572872 | tf_op jit(solution)/shard_map/ppermute | solution.py:276
  48.5 8.2 %collective-permute-start.12 = (bf16[1024,256]{1,0:T(8,128)(2,1)}, bf16[1024,256]{1,0:T(8,128)(2,1)S(1)}, u32[]{:S(2)}, u32[]{:S(2)}) collective-permute-start(bf16[1024,256]{1,0:T(8,128)(2,1)} %get-tuple-element.34), channel_id=1, source_target_pairs={{0,48},{4,52},{8,56},{12,60},{16,0},{20,4},{24,8},{28,12},{32,16},... | collective-permute-start | bytes 1572872 | tf_op jit(solution)/shard_map/ppermute | solution.py:276
  57.2 3.2 %collective-permute-start.10 = (bf16[128,1024]{1,0:T(8,128)(2,1)}, bf16[128,1024]{1,0:T(8,128)(2,1)S(1)}, u32[]{:S(2)}, u32[]{:S(2)}) collective-permute-start(bf16[128,1024]{1,0:T(8,128)(2,1)} %get-tuple-element.31), channel_id=1, source_target_pairs={{0,64},{4,68},{8,72},{12,76},{16,80},{20,84},{24,88},{28,92},{32,9... | collective-permute-start | bytes 786440 | tf_op jit(solution)/shard_map/ppermute | solution.py:263
  60.4 1.4 %collective-permute-done.10 = bf16[128,1024]{1,0:T(8,128)(2,1)S(1)} collective-permute-done((bf16[128,1024]{1,0:T(8,128)(2,1)}, bf16[128,1024]{1,0:T(8,128)(2,1)S(1)}, u32[]{:S(2)}, u32[]{:S(2)}) %collective-permute-start.10) | collective-permute-done | bytes 262176 | tf_op jit(solution)/shard_map/ppermute | solution.py:263
  61.7 2.0 %maximum_select_fusion.1 = bf16[128,2048]{1,0:T(8,128)(2,1)} fusion(bf16[128,1024]{1,0:T(8,128)(2,1)S(1)} %collective-permute-done.10, bf16[128,1024]{1,0:T(8,128)(2,1)} %get-tuple-element.30, pred[]{:T(512)S(6)} %eq.2), kind=kLoop, calls=%fused_computation.2 | loop fusion | flops 2359296 | bytes 1048577 | tf_op jit(solution)/shard_map/jit(_where)/select_n | solution.py:316
  63.8 6.1 %collective-permute-done.12 = bf16[1024,256]{1,0:T(8,128)(2,1)S(1)} collective-permute-done((bf16[1024,256]{1,0:T(8,128)(2,1)}, bf16[1024,256]{1,0:T(8,128)(2,1)S(1)}, u32[]{:S(2)}, u32[]{:S(2)}) %collective-permute-start.12) | collective-permute-done | bytes 524320 | tf_op jit(solution)/shard_map/ppermute | solution.py:276
  70.2 3.8 %collective-permute-start.14 = (bf16[256,256]{1,0:T(8,128)(2,1)S(1)}, bf16[256,256]{1,0:T(8,128)(2,1)S(1)}, u32[]{:S(2)}, u32[]{:S(2)}) collective-permute-start(bf16[256,256]{1,0:T(8,128)(2,1)S(1)} %get-tuple-element.36), channel_id=1, source_target_pairs={{0,8},{4,12},{8,0},{12,4},{16,24},{20,28},{24,16},{28,20},{32,40},... | collective-permute-start | bytes 393224 | tf_op jit(solution)/shard_map/ppermute | solution.py:276
  74.0 1.3 %collective-permute-start.15 = (bf16[256,256]{1,0:T(8,128)(2,1)S(1)}, bf16[256,256]{1,0:T(8,128)(2,1)S(1)}, u32[]{:S(2)}, u32[]{:S(2)}) collective-permute-start(bf16[256,256]{1,0:T(8,128)(2,1)S(1)} %get-tuple-element.38), channel_id=1, source_target_pairs={{0,12},{4,0},{8,4},{12,8},{16,28},{20,16},{24,20},{28,24},{32,44},... | collective-permute-start | bytes 393224 | tf_op jit(solution)/shard_map/ppermute | solution.py:276
  75.9 0.9 %maximum_select_fusion = bf16[128,2048]{1,0:T(8,128)(2,1)} fusion(bf16[128,1024]{1,0:T(8,128)(2,1)S(1)} %collective-permute-done.9, bf16[128,1024]{1,0:T(8,128)(2,1)S(1)} %copy-done.3, pred[]{:T(512)S(6)} %eq.2), kind=kLoop, calls=%fused_computation.1 | loop fusion | flops 2359296 | bytes 1048577 | tf_op jit(solution)/shard_map/jit(_where)/select_n | solution.py:316
  76.8 3.1 %collective-permute-done.15 = bf16[256,256]{1,0:T(8,128)(2,1)S(1)} collective-permute-done((bf16[256,256]{1,0:T(8,128)(2,1)S(1)}, bf16[256,256]{1,0:T(8,128)(2,1)S(1)}, u32[]{:S(2)}, u32[]{:S(2)}) %collective-permute-start.15) | collective-permute-done | bytes 131104 | tf_op jit(solution)/shard_map/ppermute | solution.py:276
  80.5 7.2 %collective-permute-start.17 = (bf16[128,256]{1,0:T(8,128)(2,1)S(1)}, bf16[128,256]{1,0:T(8,128)(2,1)S(1)}, u32[]{:S(2)}, u32[]{:S(2)}) collective-permute-start(bf16[128,256]{1,0:T(8,128)(2,1)S(1)} %slice.44), channel_id=1, source_target_pairs={{0,64},{4,68},{8,72},{12,76},{16,80},{20,84},{24,88},{28,92},{32,9... | collective-permute-start | bytes 196616 | tf_op jit(solution)/shard_map/ppermute | solution.py:263
  (39 shorter events, 6.1 us)
Async XLA Ops:
  1.6 2.4 %collective-permute-start = (bf16[144,256]{1,0:T(8,128)(2,1)S(1)}, bf16[144,256]{1,0:T(8,128)(2,1)S(1)}, u32[]{:S(2)}, u32[]{:S(2)}) collective-permute-start(bf16[144,256]{1,0:T(8,128)(2,1)S(1)} %get-tuple-element.21), channel_id=1, source_target_pairs={{0,64},{4,68},{8,72},{12,76},{16,80},{20,84},{24,88},{28,92},{32,9... | collective-permute-start | bytes 221192 | tf_op jit(solution)/shard_map/ppermute | solution.py:263
  4.0 14.7 %copy-start.1 = (bf16[128,2048]{1,0:T(8,128)(2,1)S(1)}, bf16[128,2048]{1,0:T(8,128)(2,1)}, u32[]{:S(2)}) copy-start(bf16[128,2048]{1,0:T(8,128)(2,1)} %refs_3_) | copy-start | bytes 1572868
  4.0 6.6 %collective-permute-start.1 = (bf16[288,256]{1,0:T(8,128)(2,1)S(1)}, bf16[288,256]{1,0:T(8,128)(2,1)S(1)}, u32[]{:S(2)}, u32[]{:S(2)}) collective-permute-start(bf16[288,256]{1,0:T(8,128)(2,1)S(1)} %constant_dynamic-update-slice_fusion), channel_id=1, source_target_pairs={{0,8},{4,12},{8,0},{12,4},{16,24},{20,28},{24,16},{28,20},{32,40},... | collective-permute-start | bytes 442376 | tf_op jit(solution)/shard_map/ppermute | solution.py:276
  7.8 5.5 %collective-permute-start.2 = (bf16[288,256]{1,0:T(8,128)(2,1)S(1)}, bf16[288,256]{1,0:T(8,128)(2,1)S(1)}, u32[]{:S(2)}, u32[]{:S(2)}) collective-permute-start(bf16[288,256]{1,0:T(8,128)(2,1)S(1)} %constant_dynamic-update-slice_fusion), channel_id=1, source_target_pairs={{0,4},{4,8},{8,12},{12,0},{16,20},{20,24},{24,28},{28,16},{32,36},... | collective-permute-start | bytes 442376 | tf_op jit(solution)/shard_map/ppermute | solution.py:276
  8.5 4.8 %collective-permute-start.3 = (bf16[288,256]{1,0:T(8,128)(2,1)S(1)}, bf16[288,256]{1,0:T(8,128)(2,1)S(1)}, u32[]{:S(2)}, u32[]{:S(2)}) collective-permute-start(bf16[288,256]{1,0:T(8,128)(2,1)S(1)} %constant_dynamic-update-slice_fusion), channel_id=1, source_target_pairs={{0,12},{4,0},{8,4},{12,8},{16,28},{20,16},{24,20},{28,24},{32,44},... | collective-permute-start | bytes 442376 | tf_op jit(solution)/shard_map/ppermute | solution.py:276
  13.3 8.2 %copy-start = (bf16[128,2048]{1,0:T(8,128)(2,1)S(1)}, bf16[128,2048]{1,0:T(8,128)(2,1)}, u32[]{:S(2)}) copy-start(bf16[128,2048]{1,0:T(8,128)(2,1)} %refs_1_) | copy-start | bytes 1572868
  13.3 10.7 %collective-permute-start.6 = (bf16[1152,256]{1,0:T(8,128)(2,1)S(1)}, bf16[1152,256]{1,0:T(8,128)(2,1)S(1)}, u32[]{:S(2)}, u32[]{:S(2)}) collective-permute-start(bf16[1152,256]{1,0:T(8,128)(2,1)S(1)} %constant_dynamic-update-slice_fusion.2.refs_5_), channel_id=1, source_target_pairs={{0,32},{4,36},{8,40},{12,44},{16,48},{20,52},{24,56},{28,60},{32,0... | collective-permute-start | bytes 1769480 | tf_op jit(solution)/shard_map/ppermute | solution.py:276
  16.0 14.2 %collective-permute-start.7 = (bf16[1152,256]{1,0:T(8,128)(2,1)S(1)}, bf16[1152,256]{1,0:T(8,128)(2,1)S(1)}, u32[]{:S(2)}, u32[]{:S(2)}) collective-permute-start(bf16[1152,256]{1,0:T(8,128)(2,1)S(1)} %constant_dynamic-update-slice_fusion.2.refs_5_), channel_id=1, source_target_pairs={{0,16},{4,20},{8,24},{12,28},{16,32},{20,36},{24,40},{28,44},{32,4... | collective-permute-start | bytes 1769480 | tf_op jit(solution)/shard_map/ppermute | solution.py:276
  16.7 13.9 %collective-permute-start.8 = (bf16[1152,256]{1,0:T(8,128)(2,1)S(1)}, bf16[1152,256]{1,0:T(8,128)(2,1)S(1)}, u32[]{:S(2)}, u32[]{:S(2)}) collective-permute-start(bf16[1152,256]{1,0:T(8,128)(2,1)S(1)} %constant_dynamic-update-slice_fusion.2.refs_5_), channel_id=1, source_target_pairs={{0,48},{4,52},{8,56},{12,60},{16,0},{20,4},{24,8},{28,12},{32,16},... | collective-permute-start | bytes 1769480 | tf_op jit(solution)/shard_map/ppermute | solution.py:276
  18.7 3.9 %collective-permute-start.5 = (bf16[128,1024]{1,0:T(8,128)(2,1)S(1)}, bf16[128,1024]{1,0:T(8,128)(2,1)S(1)}, u32[]{:S(2)}, u32[]{:S(2)}) collective-permute-start(bf16[128,1024]{1,0:T(8,128)(2,1)S(1)} %constant_dynamic-slice_fusion), channel_id=1, source_target_pairs={{0,64},{4,68},{8,72},{12,76},{16,80},{20,84},{24,88},{28,92},{32,9... | collective-permute-start | bytes 786440 | tf_op jit(solution)/shard_map/ppermute | solution.py:263
  21.5 1.6 %collective-permute-start.4 = (bf16[128,1024]{1,0:T(8,128)(2,1)S(1)}, bf16[128,1024]{1,0:T(8,128)(2,1)S(1)}, u32[]{:S(2)}, u32[]{:S(2)}) collective-permute-start(bf16[128,1024]{1,0:T(8,128)(2,1)S(1)} %constant_dynamic-slice_fusion.1), channel_id=1, source_target_pairs={{0,64},{4,68},{8,72},{12,76},{16,80},{20,84},{24,88},{28,92},{32,9... | collective-permute-start | bytes 786440 | tf_op jit(solution)/shard_map/ppermute | solution.py:263
  46.7 17.1 %collective-permute-start.11 = (bf16[1024,256]{1,0:T(8,128)(2,1)}, bf16[1024,256]{1,0:T(8,128)(2,1)S(1)}, u32[]{:S(2)}, u32[]{:S(2)}) collective-permute-start(bf16[1024,256]{1,0:T(8,128)(2,1)} %get-tuple-element.33), channel_id=1, source_target_pairs={{0,32},{4,36},{8,40},{12,44},{16,48},{20,52},{24,56},{28,60},{32,0... | collective-permute-start | bytes 1572872 | tf_op jit(solution)/shard_map/ppermute | solution.py:276
  48.5 21.4 %collective-permute-start.12 = (bf16[1024,256]{1,0:T(8,128)(2,1)}, bf16[1024,256]{1,0:T(8,128)(2,1)S(1)}, u32[]{:S(2)}, u32[]{:S(2)}) collective-permute-start(bf16[1024,256]{1,0:T(8,128)(2,1)} %get-tuple-element.34), channel_id=1, source_target_pairs={{0,48},{4,52},{8,56},{12,60},{16,0},{20,4},{24,8},{28,12},{32,16},... | collective-permute-start | bytes 1572872 | tf_op jit(solution)/shard_map/ppermute | solution.py:276
  56.7 13.2 %collective-permute-start.13 = (bf16[1024,256]{1,0:T(8,128)(2,1)}, bf16[1024,256]{1,0:T(8,128)(2,1)S(1)}, u32[]{:S(2)}, u32[]{:S(2)}) collective-permute-start(bf16[1024,256]{1,0:T(8,128)(2,1)} %get-tuple-element.35), channel_id=1, source_target_pairs={{0,16},{4,20},{8,24},{12,28},{16,32},{20,36},{24,40},{28,44},{32,4... | collective-permute-start | bytes 1572872 | tf_op jit(solution)/shard_map/ppermute | solution.py:276
  57.2 4.6 %collective-permute-start.10 = (bf16[128,1024]{1,0:T(8,128)(2,1)}, bf16[128,1024]{1,0:T(8,128)(2,1)S(1)}, u32[]{:S(2)}, u32[]{:S(2)}) collective-permute-start(bf16[128,1024]{1,0:T(8,128)(2,1)} %get-tuple-element.31), channel_id=1, source_target_pairs={{0,64},{4,68},{8,72},{12,76},{16,80},{20,84},{24,88},{28,92},{32,9... | collective-permute-start | bytes 786440 | tf_op jit(solution)/shard_map/ppermute | solution.py:263
  60.4 15.5 %collective-permute-start.9 = (bf16[128,1024]{1,0:T(8,128)(2,1)}, bf16[128,1024]{1,0:T(8,128)(2,1)S(1)}, u32[]{:S(2)}, u32[]{:S(2)}) collective-permute-start(bf16[128,1024]{1,0:T(8,128)(2,1)} %get-tuple-element.29), channel_id=1, source_target_pairs={{0,64},{4,68},{8,72},{12,76},{16,80},{20,84},{24,88},{28,92},{32,9... | collective-permute-start | bytes 786440 | tf_op jit(solution)/shard_map/ppermute | solution.py:263
  61.7 8.1 %copy-start.2 = (bf16[1024,256]{1,0:T(8,128)(2,1)S(1)}, bf16[1024,256]{1,0:T(8,128)(2,1)}, u32[]{:S(2)}) copy-start(bf16[1024,256]{1,0:T(8,128)(2,1)} %get-tuple-element.32) | copy-start | bytes 1572868
  70.1 5.7 %copy-start.3 = (bf16[128,1024]{1,0:T(8,128)(2,1)S(1)}, bf16[128,1024]{1,0:T(8,128)(2,1)}, u32[]{:S(2)}) copy-start(bf16[128,1024]{1,0:T(8,128)(2,1)} %get-tuple-element.28) | copy-start | bytes 786436
  70.2 6.6 %collective-permute-start.14 = (bf16[256,256]{1,0:T(8,128)(2,1)S(1)}, bf16[256,256]{1,0:T(8,128)(2,1)S(1)}, u32[]{:S(2)}, u32[]{:S(2)}) collective-permute-start(bf16[256,256]{1,0:T(8,128)(2,1)S(1)} %get-tuple-element.36), channel_id=1, source_target_pairs={{0,8},{4,12},{8,0},{12,4},{16,24},{20,28},{24,16},{28,20},{32,40},... | collective-permute-start | bytes 393224 | tf_op jit(solution)/shard_map/ppermute | solution.py:276
  74.0 5.8 %collective-permute-start.15 = (bf16[256,256]{1,0:T(8,128)(2,1)S(1)}, bf16[256,256]{1,0:T(8,128)(2,1)S(1)}, u32[]{:S(2)}, u32[]{:S(2)}) collective-permute-start(bf16[256,256]{1,0:T(8,128)(2,1)S(1)} %get-tuple-element.38), channel_id=1, source_target_pairs={{0,12},{4,0},{8,4},{12,8},{16,28},{20,16},{24,20},{28,24},{32,44},... | collective-permute-start | bytes 393224 | tf_op jit(solution)/shard_map/ppermute | solution.py:276
  75.3 5.0 %collective-permute-start.16 = (bf16[256,256]{1,0:T(8,128)(2,1)S(1)}, bf16[256,256]{1,0:T(8,128)(2,1)S(1)}, u32[]{:S(2)}, u32[]{:S(2)}) collective-permute-start(bf16[256,256]{1,0:T(8,128)(2,1)S(1)} %get-tuple-element.37), channel_id=1, source_target_pairs={{0,4},{4,8},{8,12},{12,0},{16,20},{20,24},{24,28},{28,16},{32,36},... | collective-permute-start | bytes 393224 | tf_op jit(solution)/shard_map/ppermute | solution.py:276
  80.5 8.2 %collective-permute-start.17 = (bf16[128,256]{1,0:T(8,128)(2,1)S(1)}, bf16[128,256]{1,0:T(8,128)(2,1)S(1)}, u32[]{:S(2)}, u32[]{:S(2)}) collective-permute-start(bf16[128,256]{1,0:T(8,128)(2,1)S(1)} %slice.44), channel_id=1, source_target_pairs={{0,64},{4,68},{8,72},{12,76},{16,80},{20,84},{24,88},{28,92},{32,9... | collective-permute-start | bytes 196616 | tf_op jit(solution)/shard_map/ppermute | solution.py:263

commit v4 on v3

--- a/solution.py
+++ b/solution.py
@@ -44,8 +44,16 @@
     (ids_v, ids_s, outs, gqs, dkv, ka, va, qn, qt, don, dot_t, sbuf, wbuf) = refs[17:30]
     (dka, dva, ids_sem, out_sem, dkv_sem) = refs[30:]
     tokens = BLOCKS * RUN
-    step = TOK + TAIL
+    step = 2 * TOK + TAIL
     width = HEADS * HEAD
+
+    for part in range(SIDE):
+        for pair in range(SIDE):
+            tail = kv_refs[part][pair * step + 2 * TOK : (pair + 1) * step, 0:HEAD]
+            row = part * SIDE + pair
+            ids_v[row : row + 1, :] = tail.astype(f32)[0:1, :].astype(jnp.int32)
+    fetch = pltpu.make_async_copy(ids_v, ids_s, ids_sem)
+    fetch.start()
 
     lane = lax.broadcasted_iota(jnp.int32, (RUN, HEAD), 1)
     sub = lax.broadcasted_iota(jnp.int32, (RUN, HEAD), 0)
@@ -62,21 +70,14 @@
         dka[s, :] = jnp.zeros((CHUNK, HEAD), f32)
         dva[s, :] = jnp.zeros((CHUNK, HEAD), f32)
 
-    for part in range(SIDE):
-        for unit in range(UNITS):
-            tail = kv_refs[part][unit * step + TOK : (unit + 1) * step, 0:HEAD]
-            row = part * UNITS + unit
-            ids_v[row : row + 1, :] = tail.astype(f32)[0:1, :].astype(jnp.int32)
-    fetch = pltpu.make_async_copy(ids_v, ids_s, ids_sem)
-    fetch.start()
     fetch.wait()
 
     for part in range(SIDE):
         for unit in range(UNITS):
             for run in range(2):
-                where = ids_s[part * UNITS + unit, run]
+                where = ids_s[part * SIDE + unit // 2, unit % 2 * 2 + run]
                 place = pl.ds(pl.multiple_of(where * RUN, RUN), RUN)
-                first = unit * step + run * RUN
+                first = unit // 2 * step + unit % 2 * TOK + run * RUN
                 ka[place, 0:HEAD] = kv_refs[part][first : first + RUN, 0:HEAD]
                 va[place, 0:HEAD] = kv_refs[part][first : first + RUN, HEAD : 2 * HEAD]
 
@@ -120,7 +121,7 @@
 
     @pl.loop(0, 4)
     def _(a):
-        position = ids_s[a // 2, a % 2]
+        position = ids_s[0, a]
         needed = (position + 1) * RUN
         line = pl.ds(pl.multiple_of(a % 2 * RUN, RUN), RUN)
 
@@ -154,7 +155,7 @@
     for part in PART_ORDER:
         for unit in range(UNITS):
             for run in range(2):
-                where = ids_s[part * UNITS + unit, run]
+                where = ids_s[part * SIDE + unit // 2, unit % 2 * 2 + run]
                 place = pl.ds(pl.multiple_of(where * RUN, RUN), RUN)
                 first = unit * TOK + run * RUN
                 dkv[part, first : first + RUN, 0:HEAD] = (dka[place, :] * SCALE).astype(bf16)
@@ -181,8 +182,8 @@
         in_specs=[smem] + [local] * 8,
         out_specs=(pl.BlockSpec(memory_space=pltpu.HBM),) * 8,
         scratch_shapes=[
-            pltpu.VMEM((32, HEAD), jnp.int32),
-            pltpu.SMEM((32, HEAD), jnp.int32),
+            pltpu.VMEM((SIDE * SIDE, HEAD), jnp.int32),
+            pltpu.SMEM((SIDE * SIDE, HEAD), jnp.int32),
             pltpu.VMEM((2 * TOK, width), bf16),
             pltpu.VMEM((2 * TOK, width), bf16),
             pltpu.VMEM((SIDE, UNITS * TOK, 2 * HEAD), bf16),
@@ -220,9 +221,13 @@
         copy.wait()
     lane = lax.broadcasted_iota(jnp.int32, (TAIL, 2 * HEAD), 1)
     first, second = where[0] // RUN, where[RUN] // RUN
-    tail = jnp.where(lane == 0, first, jnp.where(lane == 1, second, 0)).astype(f32).astype(bf16)
-    mine_ref[TOK : TOK + TAIL, :] = tail
-    other_ref[TOK : TOK + TAIL, :] = tail
+
+    def tail(base):
+        ids = jnp.where(lane == base, first, jnp.where(lane == base + 1, second, 0))
+        return ids.astype(f32).astype(bf16)
+
+    mine_ref[TOK : TOK + TAIL, :] = tail(0)
+    other_ref[TOK : TOK + TAIL, :] = tail(2)
 
     def fill(low_ref, high_ref):
         low_ref[0:TOK, 0:HEAD] = keys[:, 0:HEAD]
@@ -285,7 +290,8 @@
 
     core_index = core.astype(jnp.int32).reshape(1)
     kv_mine, kv_other = key_units(core_index, positions, keys, values)
-    kv_own = jnp.concatenate([kv_mine, swap(kv_other)], 0)
+    kv_other = swap(kv_other)
+    kv_own = jnp.concatenate([kv_mine[:TOK], kv_other[:TOK], kv_mine[TOK:] + kv_other[TOK:]], 0)
     line = [kv_own] + [shift(kv_own, 0, d) for d in ORDER]
     line = lax.optimization_barrier(tuple(line) + (queries, output_cotangent))
     queries, output_cotangent = line[4:]

time: 87.6 us -> 85.8 us (0.979); the launches traced: 89.3 us -> 86.4 us
  starting transfers between devices: 42.7 us -> 38.9 us
  Pallas kernels: 16.9 us -> 18.6 us
    ppermute x12, starting transfers between devices: 28 us -> 25.3 us  [shift(): return lax.ppermute(x, ('outer', 'inner'), pairs)]
    pallas_call x1, Pallas kernels: 16 us -> 17.7 us  [attention(): pl.pallas_call(attention_kernel, out_shape=(wide,) * 4 + (part,) * SIDE,...]
    ppermute x6, starting transfers between devices: 14.8 us -> 13.6 us  [swap(): lax.ppermute(x, ('outer', 'inner'), [(i, (i + 16) % 32) for i in range(32)])]
where the time goes in v4:
time: 85.8 us; the launch traced here: 86.4 us
  starting transfers between devices  38.9 us (45%)
  waiting for transfers between devices  24.1 us (28%)
  Pallas kernels  18.6 us (22%)
  other arithmetic  3.95 us (5%)
    ppermute x12, starting transfers between devices, shift(): return lax.ppermute(x, ('outer', 'inner'), pairs)  25.3 us
    ppermute x12, waiting for transfers between devices, shift(): return lax.ppermute(x, ('outer', 'inner'), pairs)  19.4 us
    pallas_call x1, Pallas kernels, attention(): pl.pallas_call(attention_kernel, out_shape=(wide,) * 4 + (part,) * SIDE,...  17.7 us
    ppermute x6, starting transfers between devices, swap(): lax.ppermute(x, ('outer', 'inner'), [(i, (i + 16) % 32) for i in range(32)])  13.6 us
    ppermute x6, waiting for transfers between devices, swap(): lax.ppermute(x, ('outer', 'inner'), [(i, (i + 16) % 32) for i in range(32)])  4.68 us
    select_n x3, other arithmetic, join(): jnp.where(core == 0, jnp.concatenate([mine, other], 1), jnp.concatenate([...  3.61 us
  transfers between devices with their start and end apart: 18, of which 13 were waited for; matrix products, arithmetic and copies ran while one was open for 4% of the time, Pallas kernels for 0%

profile of v4, /device:TPU:1, one launch (start us, length us, event | category | flops | bytes accessed | tf_op | source)
XLA Modules:
  0.0 86.4 jit_solution(17493036940020265259)
XLA Ops:
  0.6 0.9 %units.1 = (bf16[144,256]{1,0:T(8,128)(2,1)S(1)}, bf16[144,256]{1,0:T(8,128)(2,1)S(1)}) custom-call(s32[1]{0:T(128)} %bitcast.core_ref.refs_0_, s32[128]{0:T(128)} %where_hbm.1, bf16[128,256]{1,0:T(8,128)(2,1)} %keys_hbm.1, bf16[128,256]{1,0:T(8,128)(2,1)} %values_hbm.1), custom_call_target="tpu_custom_call" | custom-call | tf_op jit(solution)/shard_map/units/pallas_call | solution.py:251
  1.6 1.5 %collective-permute-start = (bf16[144,256]{1,0:T(8,128)(2,1)S(1)}, bf16[144,256]{1,0:T(8,128)(2,1)S(1)}, u32[]{:S(2)}, u32[]{:S(2)}) collective-permute-start(bf16[144,256]{1,0:T(8,128)(2,1)S(1)} %get-tuple-element.21), channel_id=1, source_target_pairs={{0,64},{4,68},{8,72},{12,76},{16,80},{20,84},{24,88},{28,92},{32,9... | collective-permute-start | bytes 221192 | tf_op jit(solution)/shard_map/ppermute | solution.py:268
  3.1 0.9 %collective-permute-done = bf16[144,256]{1,0:T(8,128)(2,1)S(1)} collective-permute-done((bf16[144,256]{1,0:T(8,128)(2,1)S(1)}, bf16[144,256]{1,0:T(8,128)(2,1)S(1)}, u32[]{:S(2)}, u32[]{:S(2)}) %collective-permute-start) | collective-permute-done | bytes 73760 | tf_op jit(solution)/shard_map/ppermute | solution.py:268
  4.0 3.8 %collective-permute-start.1 = (bf16[272,256]{1,0:T(8,128)(2,1)S(1)}, bf16[272,256]{1,0:T(8,128)(2,1)S(1)}, u32[]{:S(2)}, u32[]{:S(2)}) collective-permute-start(bf16[272,256]{1,0:T(8,128)(2,1)S(1)} %pad_maximum_fusion), channel_id=1, source_target_pairs={{0,8},{4,12},{8,0},{12,4},{16,24},{20,28},{24,16},{28,20},{32,40},... | collective-permute-start | bytes 417800 | tf_op jit(solution)/shard_map/ppermute | solution.py:281
  8.5 1.9 %collective-permute-start.3 = (bf16[272,256]{1,0:T(8,128)(2,1)S(1)}, bf16[272,256]{1,0:T(8,128)(2,1)S(1)}, u32[]{:S(2)}, u32[]{:S(2)}) collective-permute-start(bf16[272,256]{1,0:T(8,128)(2,1)S(1)} %pad_maximum_fusion), channel_id=1, source_target_pairs={{0,12},{4,0},{8,4},{12,8},{16,28},{20,16},{24,20},{28,24},{32,44},... | collective-permute-start | bytes 417800 | tf_op jit(solution)/shard_map/ppermute | solution.py:281
  10.5 2.7 %collective-permute-done.2 = bf16[272,256]{1,0:T(8,128)(2,1)S(1)} collective-permute-done((bf16[272,256]{1,0:T(8,128)(2,1)S(1)}, bf16[272,256]{1,0:T(8,128)(2,1)S(1)}, u32[]{:S(2)}, u32[]{:S(2)}) %collective-permute-start.2) | collective-permute-done | bytes 139296 | tf_op jit(solution)/shard_map/ppermute | solution.py:281
  13.3 2.7 %collective-permute-start.6 = (bf16[1088,256]{1,0:T(8,128)(2,1)S(1)}, bf16[1088,256]{1,0:T(8,128)(2,1)S(1)}, u32[]{:S(2)}, u32[]{:S(2)}) collective-permute-start(bf16[1088,256]{1,0:T(8,128)(2,1)S(1)} %constant_dynamic-update-slice_fusion.refs_5_), channel_id=1, source_target_pairs={{0,32},{4,36},{8,40},{12,44},{16,48},{20,52},{24,56},{28,60},{32,0... | collective-permute-start | bytes 1671176 | tf_op jit(solution)/shard_map/ppermute | solution.py:281
  16.7 2.0 %collective-permute-start.8 = (bf16[1088,256]{1,0:T(8,128)(2,1)S(1)}, bf16[1088,256]{1,0:T(8,128)(2,1)S(1)}, u32[]{:S(2)}, u32[]{:S(2)}) collective-permute-start(bf16[1088,256]{1,0:T(8,128)(2,1)S(1)} %constant_dynamic-update-slice_fusion.refs_5_), channel_id=1, source_target_pairs={{0,48},{4,52},{8,56},{12,60},{16,0},{20,4},{24,8},{28,12},{32,16},... | collective-permute-start | bytes 1671176 | tf_op jit(solution)/shard_map/ppermute | solution.py:281
  18.7 2.7 %collective-permute-start.5 = (bf16[128,1024]{1,0:T(8,128)(2,1)S(1)}, bf16[128,1024]{1,0:T(8,128)(2,1)S(1)}, u32[]{:S(2)}, u32[]{:S(2)}) collective-permute-start(bf16[128,1024]{1,0:T(8,128)(2,1)S(1)} %constant_dynamic-slice_fusion), channel_id=1, source_target_pairs={{0,64},{4,68},{8,72},{12,76},{16,80},{20,84},{24,88},{28,92},{32,9... | collective-permute-start | bytes 786440 | tf_op jit(solution)/shard_map/ppermute | solution.py:268
  21.5 1.0 %collective-permute-done.5.refs_4_ = bf16[128,1024]{1,0:T(8,128)(2,1)S(1)} collective-permute-done((bf16[128,1024]{1,0:T(8,128)(2,1)S(1)}, bf16[128,1024]{1,0:T(8,128)(2,1)S(1)}, u32[]{:S(2)}, u32[]{:S(2)}) %collective-permute-start.5) | collective-permute-done | bytes 262176 | tf_op jit(solution)/shard_map/ppermute | solution.py:268
  23.6 5.9 %collective-permute-done.7.refs_7_ = bf16[1088,256]{1,0:T(8,128)(2,1)S(1)} collective-permute-done((bf16[1088,256]{1,0:T(8,128)(2,1)S(1)}, bf16[1088,256]{1,0:T(8,128)(2,1)S(1)}, u32[]{:S(2)}, u32[]{:S(2)}) %collective-permute-start.7) | collective-permute-done | bytes 557088 | tf_op jit(solution)/shard_map/ppermute | solution.py:281
  29.9 17.7 %attention.1 = (bf16[128,1024]{1,0:T(8,128)(2,1)}, bf16[128,1024]{1,0:T(8,128)(2,1)}, bf16[128,1024]{1,0:T(8,128)(2,1)}, bf16[128,1024]{1,0:T(8,128)(2,1)}, bf16...) custom-call(s32[1]{0:T(128)} %bitcast.core_ref.refs_0_, ...), custom_call_target="tpu_custom_call" | custom-call | tf_op jit(solution)/shard_map/attention/pallas_call | solution.py:179
  47.6 5.6 %collective-permute-start.11 = (bf16[1024,256]{1,0:T(8,128)(2,1)}, bf16[1024,256]{1,0:T(8,128)(2,1)S(1)}, u32[]{:S(2)}, u32[]{:S(2)}) collective-permute-start(bf16[1024,256]{1,0:T(8,128)(2,1)} %get-tuple-element.33), channel_id=1, source_target_pairs={{0,32},{4,36},{8,40},{12,44},{16,48},{20,52},{24,56},{28,60},{32,0... | collective-permute-start | bytes 1572872 | tf_op jit(solution)/shard_map/ppermute | solution.py:281
  53.1 2.9 %collective-permute-start.12 = (bf16[1024,256]{1,0:T(8,128)(2,1)}, bf16[1024,256]{1,0:T(8,128)(2,1)S(1)}, u32[]{:S(2)}, u32[]{:S(2)}) collective-permute-start(bf16[1024,256]{1,0:T(8,128)(2,1)} %get-tuple-element.34), channel_id=1, source_target_pairs={{0,48},{4,52},{8,56},{12,60},{16,0},{20,4},{24,8},{28,12},{32,16},... | collective-permute-start | bytes 1572872 | tf_op jit(solution)/shard_map/ppermute | solution.py:281
  56.5 2.5 %collective-permute-start.10 = (bf16[128,1024]{1,0:T(8,128)(2,1)}, bf16[128,1024]{1,0:T(8,128)(2,1)S(1)}, u32[]{:S(2)}, u32[]{:S(2)}) collective-permute-start(bf16[128,1024]{1,0:T(8,128)(2,1)} %get-tuple-element.31), channel_id=1, source_target_pairs={{0,64},{4,68},{8,72},{12,76},{16,80},{20,84},{24,88},{28,92},{32,9... | collective-permute-start | bytes 786440 | tf_op jit(solution)/shard_map/ppermute | solution.py:268
  59.0 1.4 %collective-permute-done.10 = bf16[128,1024]{1,0:T(8,128)(2,1)S(1)} collective-permute-done((bf16[128,1024]{1,0:T(8,128)(2,1)}, bf16[128,1024]{1,0:T(8,128)(2,1)S(1)}, u32[]{:S(2)}, u32[]{:S(2)}) %collective-permute-start.10) | collective-permute-done | bytes 262176 | tf_op jit(solution)/shard_map/ppermute | solution.py:268
  60.4 2.0 %maximum_select_fusion.1 = bf16[128,2048]{1,0:T(8,128)(2,1)} fusion(bf16[128,1024]{1,0:T(8,128)(2,1)S(1)} %collective-permute-done.10, bf16[128,1024]{1,0:T(8,128)(2,1)} %get-tuple-element.30, pred[]{:T(512)S(6)} %eq.2), kind=kLoop, calls=%fused_computation.2 | loop fusion | flops 2359296 | bytes 1048577 | tf_op jit(solution)/shard_map/jit(_where)/select_n | solution.py:322
  62.4 6.9 %collective-permute-done.12 = bf16[1024,256]{1,0:T(8,128)(2,1)S(1)} collective-permute-done((bf16[1024,256]{1,0:T(8,128)(2,1)}, bf16[1024,256]{1,0:T(8,128)(2,1)S(1)}, u32[]{:S(2)}, u32[]{:S(2)}) %collective-permute-start.12) | collective-permute-done | bytes 524320 | tf_op jit(solution)/shard_map/ppermute | solution.py:281
  69.6 3.0 %collective-permute-start.14 = (bf16[256,256]{1,0:T(8,128)(2,1)S(1)}, bf16[256,256]{1,0:T(8,128)(2,1)S(1)}, u32[]{:S(2)}, u32[]{:S(2)}) collective-permute-start(bf16[256,256]{1,0:T(8,128)(2,1)S(1)} %get-tuple-element.36), channel_id=1, source_target_pairs={{0,8},{4,12},{8,0},{12,4},{16,24},{20,28},{24,16},{28,20},{32,40},... | collective-permute-start | bytes 393224 | tf_op jit(solution)/shard_map/ppermute | solution.py:281
  72.6 1.5 %collective-permute-start.16 = (bf16[256,256]{1,0:T(8,128)(2,1)S(1)}, bf16[256,256]{1,0:T(8,128)(2,1)S(1)}, u32[]{:S(2)}, u32[]{:S(2)}) collective-permute-start(bf16[256,256]{1,0:T(8,128)(2,1)S(1)} %get-tuple-element.37), channel_id=1, source_target_pairs={{0,4},{4,8},{8,12},{12,0},{16,20},{20,24},{24,28},{28,16},{32,36},... | collective-permute-start | bytes 393224 | tf_op jit(solution)/shard_map/ppermute | solution.py:281
  74.1 0.9 %maximum_select_fusion = bf16[128,2048]{1,0:T(8,128)(2,1)} fusion(bf16[128,1024]{1,0:T(8,128)(2,1)S(1)} %collective-permute-done.9, bf16[128,1024]{1,0:T(8,128)(2,1)S(1)} %copy-done.3, pred[]{:T(512)S(6)} %eq.2), kind=kLoop, calls=%fused_computation.1 | loop fusion | flops 2359296 | bytes 1048577 | tf_op jit(solution)/shard_map/jit(_where)/select_n | solution.py:322
  75.0 1.4 %collective-permute-done.15 = bf16[256,256]{1,0:T(8,128)(2,1)S(1)} collective-permute-done((bf16[256,256]{1,0:T(8,128)(2,1)S(1)}, bf16[256,256]{1,0:T(8,128)(2,1)S(1)}, u32[]{:S(2)}, u32[]{:S(2)}) %collective-permute-start.15) | collective-permute-done | bytes 131104 | tf_op jit(solution)/shard_map/ppermute | solution.py:281
  76.4 1.5 %collective-permute-done.16 = bf16[256,256]{1,0:T(8,128)(2,1)S(1)} collective-permute-done((bf16[256,256]{1,0:T(8,128)(2,1)S(1)}, bf16[256,256]{1,0:T(8,128)(2,1)S(1)}, u32[]{:S(2)}, u32[]{:S(2)}) %collective-permute-start.16) | collective-permute-done | bytes 131104 | tf_op jit(solution)/shard_map/ppermute | solution.py:281
  78.0 6.8 %collective-permute-start.17 = (bf16[128,256]{1,0:T(8,128)(2,1)S(1)}, bf16[128,256]{1,0:T(8,128)(2,1)S(1)}, u32[]{:S(2)}, u32[]{:S(2)}) collective-permute-start(bf16[128,256]{1,0:T(8,128)(2,1)S(1)} %slice.62), channel_id=1, source_target_pairs={{0,64},{4,68},{8,72},{12,76},{16,80},{20,84},{24,88},{28,92},{32,9... | collective-permute-start | bytes 196616 | tf_op jit(solution)/shard_map/ppermute | solution.py:268
  (41 shorter events, 5.6 us)
Async XLA Ops:
  1.6 2.4 %collective-permute-start = (bf16[144,256]{1,0:T(8,128)(2,1)S(1)}, bf16[144,256]{1,0:T(8,128)(2,1)S(1)}, u32[]{:S(2)}, u32[]{:S(2)}) collective-permute-start(bf16[144,256]{1,0:T(8,128)(2,1)S(1)} %get-tuple-element.21), channel_id=1, source_target_pairs={{0,64},{4,68},{8,72},{12,76},{16,80},{20,84},{24,88},{28,92},{32,9... | collective-permute-start | bytes 221192 | tf_op jit(solution)/shard_map/ppermute | solution.py:268
  4.0 14.7 %copy-start.1 = (bf16[128,2048]{1,0:T(8,128)(2,1)S(1)}, bf16[128,2048]{1,0:T(8,128)(2,1)}, u32[]{:S(2)}) copy-start(bf16[128,2048]{1,0:T(8,128)(2,1)} %refs_3_) | copy-start | bytes 1572868
  4.0 6.5 %collective-permute-start.1 = (bf16[272,256]{1,0:T(8,128)(2,1)S(1)}, bf16[272,256]{1,0:T(8,128)(2,1)S(1)}, u32[]{:S(2)}, u32[]{:S(2)}) collective-permute-start(bf16[272,256]{1,0:T(8,128)(2,1)S(1)} %pad_maximum_fusion), channel_id=1, source_target_pairs={{0,8},{4,12},{8,0},{12,4},{16,24},{20,28},{24,16},{28,20},{32,40},... | collective-permute-start | bytes 417800 | tf_op jit(solution)/shard_map/ppermute | solution.py:281
  7.8 5.4 %collective-permute-start.2 = (bf16[272,256]{1,0:T(8,128)(2,1)S(1)}, bf16[272,256]{1,0:T(8,128)(2,1)S(1)}, u32[]{:S(2)}, u32[]{:S(2)}) collective-permute-start(bf16[272,256]{1,0:T(8,128)(2,1)S(1)} %pad_maximum_fusion), channel_id=1, source_target_pairs={{0,4},{4,8},{8,12},{12,0},{16,20},{20,24},{24,28},{28,16},{32,36},... | collective-permute-start | bytes 417800 | tf_op jit(solution)/shard_map/ppermute | solution.py:281
  8.5 4.7 %collective-permute-start.3 = (bf16[272,256]{1,0:T(8,128)(2,1)S(1)}, bf16[272,256]{1,0:T(8,128)(2,1)S(1)}, u32[]{:S(2)}, u32[]{:S(2)}) collective-permute-start(bf16[272,256]{1,0:T(8,128)(2,1)S(1)} %pad_maximum_fusion), channel_id=1, source_target_pairs={{0,12},{4,0},{8,4},{12,8},{16,28},{20,16},{24,20},{28,24},{32,44},... | collective-permute-start | bytes 417800 | tf_op jit(solution)/shard_map/ppermute | solution.py:281
  13.2 8.2 %copy-start = (bf16[128,2048]{1,0:T(8,128)(2,1)S(1)}, bf16[128,2048]{1,0:T(8,128)(2,1)}, u32[]{:S(2)}) copy-start(bf16[128,2048]{1,0:T(8,128)(2,1)} %refs_1_) | copy-start | bytes 1572868
  13.3 10.3 %collective-permute-start.6 = (bf16[1088,256]{1,0:T(8,128)(2,1)S(1)}, bf16[1088,256]{1,0:T(8,128)(2,1)S(1)}, u32[]{:S(2)}, u32[]{:S(2)}) collective-permute-start(bf16[1088,256]{1,0:T(8,128)(2,1)S(1)} %constant_dynamic-update-slice_fusion.refs_5_), channel_id=1, source_target_pairs={{0,32},{4,36},{8,40},{12,44},{16,48},{20,52},{24,56},{28,60},{32,0... | collective-permute-start | bytes 1671176 | tf_op jit(solution)/shard_map/ppermute | solution.py:281
  16.0 13.5 %collective-permute-start.7 = (bf16[1088,256]{1,0:T(8,128)(2,1)S(1)}, bf16[1088,256]{1,0:T(8,128)(2,1)S(1)}, u32[]{:S(2)}, u32[]{:S(2)}) collective-permute-start(bf16[1088,256]{1,0:T(8,128)(2,1)S(1)} %constant_dynamic-update-slice_fusion.refs_5_), channel_id=1, source_target_pairs={{0,16},{4,20},{8,24},{12,28},{16,32},{20,36},{24,40},{28,44},{32,4... | collective-permute-start | bytes 1671176 | tf_op jit(solution)/shard_map/ppermute | solution.py:281
  16.7 13.2 %collective-permute-start.8 = (bf16[1088,256]{1,0:T(8,128)(2,1)S(1)}, bf16[1088,256]{1,0:T(8,128)(2,1)S(1)}, u32[]{:S(2)}, u32[]{:S(2)}) collective-permute-start(bf16[1088,256]{1,0:T(8,128)(2,1)S(1)} %constant_dynamic-update-slice_fusion.refs_5_), channel_id=1, source_target_pairs={{0,48},{4,52},{8,56},{12,60},{16,0},{20,4},{24,8},{28,12},{32,16},... | collective-permute-start | bytes 1671176 | tf_op jit(solution)/shard_map/ppermute | solution.py:281
  18.7 3.9 %collective-permute-start.5 = (bf16[128,1024]{1,0:T(8,128)(2,1)S(1)}, bf16[128,1024]{1,0:T(8,128)(2,1)S(1)}, u32[]{:S(2)}, u32[]{:S(2)}) collective-permute-start(bf16[128,1024]{1,0:T(8,128)(2,1)S(1)} %constant_dynamic-slice_fusion), channel_id=1, source_target_pairs={{0,64},{4,68},{8,72},{12,76},{16,80},{20,84},{24,88},{28,92},{32,9... | collective-permute-start | bytes 786440 | tf_op jit(solution)/shard_map/ppermute | solution.py:268
  21.4 1.6 %collective-permute-start.4 = (bf16[128,1024]{1,0:T(8,128)(2,1)S(1)}, bf16[128,1024]{1,0:T(8,128)(2,1)S(1)}, u32[]{:S(2)}, u32[]{:S(2)}) collective-permute-start(bf16[128,1024]{1,0:T(8,128)(2,1)S(1)} %constant_dynamic-slice_fusion.1), channel_id=1, source_target_pairs={{0,64},{4,68},{8,72},{12,76},{16,80},{20,84},{24,88},{28,92},{32,9... | collective-permute-start | bytes 786440 | tf_op jit(solution)/shard_map/ppermute | solution.py:268
  47.6 14.8 %collective-permute-start.11 = (bf16[1024,256]{1,0:T(8,128)(2,1)}, bf16[1024,256]{1,0:T(8,128)(2,1)S(1)}, u32[]{:S(2)}, u32[]{:S(2)}) collective-permute-start(bf16[1024,256]{1,0:T(8,128)(2,1)} %get-tuple-element.33), channel_id=1, source_target_pairs={{0,32},{4,36},{8,40},{12,44},{16,48},{20,52},{24,56},{28,60},{32,0... | collective-permute-start | bytes 1572872 | tf_op jit(solution)/shard_map/ppermute | solution.py:281
  53.1 16.1 %collective-permute-start.12 = (bf16[1024,256]{1,0:T(8,128)(2,1)}, bf16[1024,256]{1,0:T(8,128)(2,1)S(1)}, u32[]{:S(2)}, u32[]{:S(2)}) collective-permute-start(bf16[1024,256]{1,0:T(8,128)(2,1)} %get-tuple-element.34), channel_id=1, source_target_pairs={{0,48},{4,52},{8,56},{12,60},{16,0},{20,4},{24,8},{28,12},{32,16},... | collective-permute-start | bytes 1572872 | tf_op jit(solution)/shard_map/ppermute | solution.py:281
  56.0 13.2 %collective-permute-start.13 = (bf16[1024,256]{1,0:T(8,128)(2,1)}, bf16[1024,256]{1,0:T(8,128)(2,1)S(1)}, u32[]{:S(2)}, u32[]{:S(2)}) collective-permute-start(bf16[1024,256]{1,0:T(8,128)(2,1)} %get-tuple-element.35), channel_id=1, source_target_pairs={{0,16},{4,20},{8,24},{12,28},{16,32},{20,36},{24,40},{28,44},{32,4... | collective-permute-start | bytes 1572872 | tf_op jit(solution)/shard_map/ppermute | solution.py:281
  56.5 3.9 %collective-permute-start.10 = (bf16[128,1024]{1,0:T(8,128)(2,1)}, bf16[128,1024]{1,0:T(8,128)(2,1)S(1)}, u32[]{:S(2)}, u32[]{:S(2)}) collective-permute-start(bf16[128,1024]{1,0:T(8,128)(2,1)} %get-tuple-element.31), channel_id=1, source_target_pairs={{0,64},{4,68},{8,72},{12,76},{16,80},{20,84},{24,88},{28,92},{32,9... | collective-permute-start | bytes 786440 | tf_op jit(solution)/shard_map/ppermute | solution.py:268
  59.0 15.1 %collective-permute-start.9 = (bf16[128,1024]{1,0:T(8,128)(2,1)}, bf16[128,1024]{1,0:T(8,128)(2,1)S(1)}, u32[]{:S(2)}, u32[]{:S(2)}) collective-permute-start(bf16[128,1024]{1,0:T(8,128)(2,1)} %get-tuple-element.29), channel_id=1, source_target_pairs={{0,64},{4,68},{8,72},{12,76},{16,80},{20,84},{24,88},{28,92},{32,9... | collective-permute-start | bytes 786440 | tf_op jit(solution)/shard_map/ppermute | solution.py:268
  60.4 8.9 %copy-start.2 = (bf16[1024,256]{1,0:T(8,128)(2,1)S(1)}, bf16[1024,256]{1,0:T(8,128)(2,1)}, u32[]{:S(2)}) copy-start(bf16[1024,256]{1,0:T(8,128)(2,1)} %get-tuple-element.32) | copy-start | bytes 1572868
  69.5 4.6 %copy-start.3 = (bf16[128,1024]{1,0:T(8,128)(2,1)S(1)}, bf16[128,1024]{1,0:T(8,128)(2,1)}, u32[]{:S(2)}) copy-start(bf16[128,1024]{1,0:T(8,128)(2,1)} %get-tuple-element.28) | copy-start | bytes 786436
  69.6 5.4 %collective-permute-start.14 = (bf16[256,256]{1,0:T(8,128)(2,1)S(1)}, bf16[256,256]{1,0:T(8,128)(2,1)S(1)}, u32[]{:S(2)}, u32[]{:S(2)}) collective-permute-start(bf16[256,256]{1,0:T(8,128)(2,1)S(1)} %get-tuple-element.36), channel_id=1, source_target_pairs={{0,8},{4,12},{8,0},{12,4},{16,24},{20,28},{24,16},{28,20},{32,40},... | collective-permute-start | bytes 393224 | tf_op jit(solution)/shard_map/ppermute | solution.py:281
  72.6 3.8 %collective-permute-start.15 = (bf16[256,256]{1,0:T(8,128)(2,1)S(1)}, bf16[256,256]{1,0:T(8,128)(2,1)S(1)}, u32[]{:S(2)}, u32[]{:S(2)}) collective-permute-start(bf16[256,256]{1,0:T(8,128)(2,1)S(1)} %get-tuple-element.38), channel_id=1, source_target_pairs={{0,12},{4,0},{8,4},{12,8},{16,28},{20,16},{24,20},{28,24},{32,44},... | collective-permute-start | bytes 393224 | tf_op jit(solution)/shard_map/ppermute | solution.py:281
  72.6 5.3 %collective-permute-start.16 = (bf16[256,256]{1,0:T(8,128)(2,1)S(1)}, bf16[256,256]{1,0:T(8,128)(2,1)S(1)}, u32[]{:S(2)}, u32[]{:S(2)}) collective-permute-start(bf16[256,256]{1,0:T(8,128)(2,1)S(1)} %get-tuple-element.37), channel_id=1, source_target_pairs={{0,4},{4,8},{8,12},{12,0},{16,20},{20,24},{24,28},{28,16},{32,36},... | collective-permute-start | bytes 393224 | tf_op jit(solution)/shard_map/ppermute | solution.py:281
  78.0 7.7 %collective-permute-start.17 = (bf16[128,256]{1,0:T(8,128)(2,1)S(1)}, bf16[128,256]{1,0:T(8,128)(2,1)S(1)}, u32[]{:S(2)}, u32[]{:S(2)}) collective-permute-start(bf16[128,256]{1,0:T(8,128)(2,1)S(1)} %slice.62), channel_id=1, source_target_pairs={{0,64},{4,68},{8,72},{12,76},{16,80},{20,84},{24,88},{28,92},{32,9... | collective-permute-start | bytes 196616 | tf_op jit(solution)/shard_map/ppermute | solution.py:268

commit v5 on v4

--- a/solution.py
+++ b/solution.py
@@ -119,8 +119,20 @@
         for h in range(HEADS):
             gqs[rows, h * HEAD : (h + 1) * HEAD] = grad_n[h * RUN : (h + 1) * RUN, :]
 
+    def leaving(half):
+        place = slice(half * TOK, (half + 1) * TOK)
+        return [
+            pltpu.make_async_copy(outs.at[place], out_refs[half], out_sem.at[half]),
+            pltpu.make_async_copy(gqs.at[place], gq_refs[half], out_sem.at[2 + half]),
+        ]
+
     @pl.loop(0, 4)
     def _(a):
+        @pl.when(a == 2)
+        def _():
+            for copy in leaving(0):
+                copy.start()
+
         position = ids_s[0, a]
         needed = (position + 1) * RUN
         line = pl.ds(pl.multiple_of(a % 2 * RUN, RUN), RUN)
@@ -145,13 +157,9 @@
             def _():
                 run_block(a, position, length)
 
-    copies = []
-    for half in range(2):
-        place = slice(half * TOK, (half + 1) * TOK)
-        copies.append(pltpu.make_async_copy(outs.at[place], out_refs[half], out_sem.at[half]))
-        copies.append(pltpu.make_async_copy(gqs.at[place], gq_refs[half], out_sem.at[2 + half]))
-        copies[-2].start()
-        copies[-1].start()
+    for copy in leaving(1):
+        copy.start()
+    copies = leaving(0) + leaving(1)
     for part in PART_ORDER:
         for unit in range(UNITS):
             for run in range(2):

time: 85.8 us -> 85 us (level)
  starting transfers between devices: 38.9 us -> 34.4 us
  Pallas kernels: 18.6 us -> 22.9 us
  waiting for transfers between devices: 24.1 us -> 22.6 us
    ppermute x12, starting transfers between devices: 25.3 us -> 17.3 us  [shift(): return lax.ppermute(x, ('outer', 'inner'), pairs)]
    pallas_call x1, Pallas kernels: 17.7 us -> 22 us  [attention(): pl.pallas_call(attention_kernel, out_shape=(wide,) * 4 + (part,) * SIDE,...]
    ppermute x6, starting transfers between devices: 13.6 us -> 17.1 us  [swap(): lax.ppermute(x, ('outer', 'inner'), [(i, (i + 16) % 32) for i in range(32)])]
    ppermute x12, waiting for transfers between devices: 19.4 us -> 17.9 us  [shift(): return lax.ppermute(x, ('outer', 'inner'), pairs)]
  transfers between devices with their start and end apart: 18 -> 18, of which waited for: 13 -> 15; matrix products, arithmetic and copies ran while one was open for 4% -> 4% of each run, Pallas kernels for 0% -> 0%
where the time goes in v5:
time: 85 us; the launch traced here: 84.8 us
  starting transfers between devices  34.4 us (40%)
  Pallas kernels  22.9 us (27%)
  waiting for transfers between devices  22.6 us (27%)
  other arithmetic  3.95 us (5%)
    pallas_call x1, Pallas kernels, attention(): pl.pallas_call(attention_kernel, out_shape=(wide,) * 4 + (part,) * SIDE,...  22 us
    ppermute x12, waiting for transfers between devices, shift(): return lax.ppermute(x, ('outer', 'inner'), pairs)  17.9 us
    ppermute x12, starting transfers between devices, shift(): return lax.ppermute(x, ('outer', 'inner'), pairs)  17.3 us
    ppermute x6, starting transfers between devices, swap(): lax.ppermute(x, ('outer', 'inner'), [(i, (i + 16) % 32) for i in range(32)])  17.1 us
    ppermute x6, waiting for transfers between devices, swap(): lax.ppermute(x, ('outer', 'inner'), [(i, (i + 16) % 32) for i in range(32)])  4.68 us
    select_n x3, other arithmetic, join(): jnp.where(core == 0, jnp.concatenate([mine, other], 1), jnp.concatenate([...  3.61 us
  transfers between devices with their start and end apart: 18, of which 15 were waited for; matrix products, arithmetic and copies ran while one was open for 4% of the time, Pallas kernels for 0%

profile of v5, /device:TPU:1, one launch (start us, length us, event | category | flops | bytes accessed | tf_op | source)
XLA Modules:
  0.0 84.8 jit_solution(13244963355961395589)
XLA Ops:
  0.6 0.9 %units.1 = (bf16[144,256]{1,0:T(8,128)(2,1)S(1)}, bf16[144,256]{1,0:T(8,128)(2,1)S(1)}) custom-call(s32[1]{0:T(128)} %bitcast.core_ref.refs_0_, s32[128]{0:T(128)} %where_hbm.1, bf16[128,256]{1,0:T(8,128)(2,1)} %keys_hbm.1, bf16[128,256]{1,0:T(8,128)(2,1)} %values_hbm.1), custom_call_target="tpu_custom_call" | custom-call | tf_op jit(solution)/shard_map/units/pallas_call | solution.py:259
  1.6 1.5 %collective-permute-start = (bf16[144,256]{1,0:T(8,128)(2,1)S(1)}, bf16[144,256]{1,0:T(8,128)(2,1)S(1)}, u32[]{:S(2)}, u32[]{:S(2)}) collective-permute-start(bf16[144,256]{1,0:T(8,128)(2,1)S(1)} %get-tuple-element.21), channel_id=1, source_target_pairs={{0,64},{4,68},{8,72},{12,76},{16,80},{20,84},{24,88},{28,92},{32,9... | collective-permute-start | bytes 221192 | tf_op jit(solution)/shard_map/ppermute | solution.py:276
  3.1 0.9 %collective-permute-done = bf16[144,256]{1,0:T(8,128)(2,1)S(1)} collective-permute-done((bf16[144,256]{1,0:T(8,128)(2,1)S(1)}, bf16[144,256]{1,0:T(8,128)(2,1)S(1)}, u32[]{:S(2)}, u32[]{:S(2)}) %collective-permute-start) | collective-permute-done | bytes 73760 | tf_op jit(solution)/shard_map/ppermute | solution.py:276
  4.0 3.8 %collective-permute-start.1 = (bf16[272,256]{1,0:T(8,128)(2,1)S(1)}, bf16[272,256]{1,0:T(8,128)(2,1)S(1)}, u32[]{:S(2)}, u32[]{:S(2)}) collective-permute-start(bf16[272,256]{1,0:T(8,128)(2,1)S(1)} %pad_maximum_fusion), channel_id=1, source_target_pairs={{0,8},{4,12},{8,0},{12,4},{16,24},{20,28},{24,16},{28,20},{32,40},... | collective-permute-start | bytes 417800 | tf_op jit(solution)/shard_map/ppermute | solution.py:289
  8.5 1.9 %collective-permute-start.3 = (bf16[272,256]{1,0:T(8,128)(2,1)S(1)}, bf16[272,256]{1,0:T(8,128)(2,1)S(1)}, u32[]{:S(2)}, u32[]{:S(2)}) collective-permute-start(bf16[272,256]{1,0:T(8,128)(2,1)S(1)} %pad_maximum_fusion), channel_id=1, source_target_pairs={{0,12},{4,0},{8,4},{12,8},{16,28},{20,16},{24,20},{28,24},{32,44},... | collective-permute-start | bytes 417800 | tf_op jit(solution)/shard_map/ppermute | solution.py:289
  10.5 2.7 %collective-permute-done.2 = bf16[272,256]{1,0:T(8,128)(2,1)S(1)} collective-permute-done((bf16[272,256]{1,0:T(8,128)(2,1)S(1)}, bf16[272,256]{1,0:T(8,128)(2,1)S(1)}, u32[]{:S(2)}, u32[]{:S(2)}) %collective-permute-start.2) | collective-permute-done | bytes 139296 | tf_op jit(solution)/shard_map/ppermute | solution.py:289
  13.3 2.7 %collective-permute-start.6 = (bf16[1088,256]{1,0:T(8,128)(2,1)S(1)}, bf16[1088,256]{1,0:T(8,128)(2,1)S(1)}, u32[]{:S(2)}, u32[]{:S(2)}) collective-permute-start(bf16[1088,256]{1,0:T(8,128)(2,1)S(1)} %constant_dynamic-update-slice_fusion.refs_5_), channel_id=1, source_target_pairs={{0,32},{4,36},{8,40},{12,44},{16,48},{20,52},{24,56},{28,60},{32,0... | collective-permute-start | bytes 1671176 | tf_op jit(solution)/shard_map/ppermute | solution.py:289
  16.7 2.0 %collective-permute-start.8 = (bf16[1088,256]{1,0:T(8,128)(2,1)S(1)}, bf16[1088,256]{1,0:T(8,128)(2,1)S(1)}, u32[]{:S(2)}, u32[]{:S(2)}) collective-permute-start(bf16[1088,256]{1,0:T(8,128)(2,1)S(1)} %constant_dynamic-update-slice_fusion.refs_5_), channel_id=1, source_target_pairs={{0,48},{4,52},{8,56},{12,60},{16,0},{20,4},{24,8},{28,12},{32,16},... | collective-permute-start | bytes 1671176 | tf_op jit(solution)/shard_map/ppermute | solution.py:289
  18.7 2.7 %collective-permute-start.5 = (bf16[128,1024]{1,0:T(8,128)(2,1)S(1)}, bf16[128,1024]{1,0:T(8,128)(2,1)S(1)}, u32[]{:S(2)}, u32[]{:S(2)}) collective-permute-start(bf16[128,1024]{1,0:T(8,128)(2,1)S(1)} %constant_dynamic-slice_fusion), channel_id=1, source_target_pairs={{0,64},{4,68},{8,72},{12,76},{16,80},{20,84},{24,88},{28,92},{32,9... | collective-permute-start | bytes 786440 | tf_op jit(solution)/shard_map/ppermute | solution.py:276
  21.5 1.0 %collective-permute-done.5.refs_4_ = bf16[128,1024]{1,0:T(8,128)(2,1)S(1)} collective-permute-done((bf16[128,1024]{1,0:T(8,128)(2,1)S(1)}, bf16[128,1024]{1,0:T(8,128)(2,1)S(1)}, u32[]{:S(2)}, u32[]{:S(2)}) %collective-permute-start.5) | collective-permute-done | bytes 262176 | tf_op jit(solution)/shard_map/ppermute | solution.py:276
  23.6 5.9 %collective-permute-done.7.refs_7_ = bf16[1088,256]{1,0:T(8,128)(2,1)S(1)} collective-permute-done((bf16[1088,256]{1,0:T(8,128)(2,1)S(1)}, bf16[1088,256]{1,0:T(8,128)(2,1)S(1)}, u32[]{:S(2)}, u32[]{:S(2)}) %collective-permute-start.7) | collective-permute-done | bytes 557088 | tf_op jit(solution)/shard_map/ppermute | solution.py:289
  29.9 22.0 %attention.1 = (bf16[128,1024]{1,0:T(8,128)(2,1)}, bf16[128,1024]{1,0:T(8,128)(2,1)}, bf16[128,1024]{1,0:T(8,128)(2,1)}, bf16[128,1024]{1,0:T(8,128)(2,1)}, bf16...) custom-call(s32[1]{0:T(128)} %bitcast.core_ref.refs_0_, ...), custom_call_target="tpu_custom_call" | custom-call | tf_op jit(solution)/shard_map/attention/pallas_call | solution.py:187
  52.0 0.9 %collective-permute-start.12 = (bf16[1024,256]{1,0:T(8,128)(2,1)}, bf16[1024,256]{1,0:T(8,128)(2,1)S(1)}, u32[]{:S(2)}, u32[]{:S(2)}) collective-permute-start(bf16[1024,256]{1,0:T(8,128)(2,1)} %get-tuple-element.34), channel_id=1, source_target_pairs={{0,48},{4,52},{8,56},{12,60},{16,0},{20,4},{24,8},{28,12},{32,16},... | collective-permute-start | bytes 1572872 | tf_op jit(solution)/shard_map/ppermute | solution.py:289
  53.5 6.7 %collective-permute-start.10 = (bf16[128,1024]{1,0:T(8,128)(2,1)}, bf16[128,1024]{1,0:T(8,128)(2,1)S(1)}, u32[]{:S(2)}, u32[]{:S(2)}) collective-permute-start(bf16[128,1024]{1,0:T(8,128)(2,1)} %get-tuple-element.31), channel_id=1, source_target_pairs={{0,64},{4,68},{8,72},{12,76},{16,80},{20,84},{24,88},{28,92},{32,9... | collective-permute-start | bytes 786440 | tf_op jit(solution)/shard_map/ppermute | solution.py:276
  60.2 1.4 %collective-permute-done.10 = bf16[128,1024]{1,0:T(8,128)(2,1)S(1)} collective-permute-done((bf16[128,1024]{1,0:T(8,128)(2,1)}, bf16[128,1024]{1,0:T(8,128)(2,1)S(1)}, u32[]{:S(2)}, u32[]{:S(2)}) %collective-permute-start.10) | collective-permute-done | bytes 262176 | tf_op jit(solution)/shard_map/ppermute | solution.py:276
  61.6 2.0 %maximum_select_fusion.1 = bf16[128,2048]{1,0:T(8,128)(2,1)} fusion(bf16[128,1024]{1,0:T(8,128)(2,1)S(1)} %collective-permute-done.10, bf16[128,1024]{1,0:T(8,128)(2,1)} %get-tuple-element.30, pred[]{:T(512)S(6)} %eq.2), kind=kLoop, calls=%fused_computation.2 | loop fusion | flops 2359296 | bytes 1048577 | tf_op jit(solution)/shard_map/jit(_where)/select_n | solution.py:330
  63.6 2.6 %collective-permute-done.12 = bf16[1024,256]{1,0:T(8,128)(2,1)S(1)} collective-permute-done((bf16[1024,256]{1,0:T(8,128)(2,1)}, bf16[1024,256]{1,0:T(8,128)(2,1)S(1)}, u32[]{:S(2)}, u32[]{:S(2)}) %collective-permute-start.12) | collective-permute-done | bytes 524320 | tf_op jit(solution)/shard_map/ppermute | solution.py:289
  66.1 1.5 %collective-permute-done.13 = bf16[1024,256]{1,0:T(8,128)(2,1)S(1)} collective-permute-done((bf16[1024,256]{1,0:T(8,128)(2,1)}, bf16[1024,256]{1,0:T(8,128)(2,1)S(1)}, u32[]{:S(2)}, u32[]{:S(2)}) %collective-permute-start.13) | collective-permute-done | bytes 524320 | tf_op jit(solution)/shard_map/ppermute | solution.py:289
  67.9 2.4 %collective-permute-start.14 = (bf16[256,256]{1,0:T(8,128)(2,1)S(1)}, bf16[256,256]{1,0:T(8,128)(2,1)S(1)}, u32[]{:S(2)}, u32[]{:S(2)}) collective-permute-start(bf16[256,256]{1,0:T(8,128)(2,1)S(1)} %get-tuple-element.36), channel_id=1, source_target_pairs={{0,8},{4,12},{8,0},{12,4},{16,24},{20,28},{24,16},{28,20},{32,40},... | collective-permute-start | bytes 393224 | tf_op jit(solution)/shard_map/ppermute | solution.py:289
  70.3 1.3 %collective-permute-start.15 = (bf16[256,256]{1,0:T(8,128)(2,1)S(1)}, bf16[256,256]{1,0:T(8,128)(2,1)S(1)}, u32[]{:S(2)}, u32[]{:S(2)}) collective-permute-start(bf16[256,256]{1,0:T(8,128)(2,1)S(1)} %get-tuple-element.38), channel_id=1, source_target_pairs={{0,12},{4,0},{8,4},{12,8},{16,28},{20,16},{24,20},{28,24},{32,44},... | collective-permute-start | bytes 393224 | tf_op jit(solution)/shard_map/ppermute | solution.py:289
  71.8 0.9 %maximum_select_fusion = bf16[128,2048]{1,0:T(8,128)(2,1)} fusion(bf16[128,1024]{1,0:T(8,128)(2,1)S(1)} %collective-permute-done.9, bf16[128,1024]{1,0:T(8,128)(2,1)S(1)} %copy-done.3, pred[]{:T(512)S(6)} %eq.2), kind=kLoop, calls=%fused_computation.1 | loop fusion | flops 2359296 | bytes 1048577 | tf_op jit(solution)/shard_map/jit(_where)/select_n | solution.py:330
  73.3 2.1 %collective-permute-done.15 = bf16[256,256]{1,0:T(8,128)(2,1)S(1)} collective-permute-done((bf16[256,256]{1,0:T(8,128)(2,1)S(1)}, bf16[256,256]{1,0:T(8,128)(2,1)S(1)}, u32[]{:S(2)}, u32[]{:S(2)}) %collective-permute-start.15) | collective-permute-done | bytes 131104 | tf_op jit(solution)/shard_map/ppermute | solution.py:289
  75.4 1.5 %collective-permute-done.16 = bf16[256,256]{1,0:T(8,128)(2,1)S(1)} collective-permute-done((bf16[256,256]{1,0:T(8,128)(2,1)S(1)}, bf16[256,256]{1,0:T(8,128)(2,1)S(1)}, u32[]{:S(2)}, u32[]{:S(2)}) %collective-permute-start.16) | collective-permute-done | bytes 131104 | tf_op jit(solution)/shard_map/ppermute | solution.py:289
  77.0 6.1 %collective-permute-start.17 = (bf16[128,256]{1,0:T(8,128)(2,1)S(1)}, bf16[128,256]{1,0:T(8,128)(2,1)S(1)}, u32[]{:S(2)}, u32[]{:S(2)}) collective-permute-start(bf16[128,256]{1,0:T(8,128)(2,1)S(1)} %slice.62), channel_id=1, source_target_pairs={{0,64},{4,68},{8,72},{12,76},{16,80},{20,84},{24,88},{28,92},{32,9... | collective-permute-start | bytes 196616 | tf_op jit(solution)/shard_map/ppermute | solution.py:276
  (41 shorter events, 6.6 us)
Async XLA Ops:
  1.6 2.4 %collective-permute-start = (bf16[144,256]{1,0:T(8,128)(2,1)S(1)}, bf16[144,256]{1,0:T(8,128)(2,1)S(1)}, u32[]{:S(2)}, u32[]{:S(2)}) collective-permute-start(bf16[144,256]{1,0:T(8,128)(2,1)S(1)} %get-tuple-element.21), channel_id=1, source_target_pairs={{0,64},{4,68},{8,72},{12,76},{16,80},{20,84},{24,88},{28,92},{32,9... | collective-permute-start | bytes 221192 | tf_op jit(solution)/shard_map/ppermute | solution.py:276
  4.0 14.7 %copy-start.1 = (bf16[128,2048]{1,0:T(8,128)(2,1)S(1)}, bf16[128,2048]{1,0:T(8,128)(2,1)}, u32[]{:S(2)}) copy-start(bf16[128,2048]{1,0:T(8,128)(2,1)} %refs_3_) | copy-start | bytes 1572868
  4.0 6.5 %collective-permute-start.1 = (bf16[272,256]{1,0:T(8,128)(2,1)S(1)}, bf16[272,256]{1,0:T(8,128)(2,1)S(1)}, u32[]{:S(2)}, u32[]{:S(2)}) collective-permute-start(bf16[272,256]{1,0:T(8,128)(2,1)S(1)} %pad_maximum_fusion), channel_id=1, source_target_pairs={{0,8},{4,12},{8,0},{12,4},{16,24},{20,28},{24,16},{28,20},{32,40},... | collective-permute-start | bytes 417800 | tf_op jit(solution)/shard_map/ppermute | solution.py:289
  7.8 5.4 %collective-permute-start.2 = (bf16[272,256]{1,0:T(8,128)(2,1)S(1)}, bf16[272,256]{1,0:T(8,128)(2,1)S(1)}, u32[]{:S(2)}, u32[]{:S(2)}) collective-permute-start(bf16[272,256]{1,0:T(8,128)(2,1)S(1)} %pad_maximum_fusion), channel_id=1, source_target_pairs={{0,4},{4,8},{8,12},{12,0},{16,20},{20,24},{24,28},{28,16},{32,36},... | collective-permute-start | bytes 417800 | tf_op jit(solution)/shard_map/ppermute | solution.py:289
  8.5 4.7 %collective-permute-start.3 = (bf16[272,256]{1,0:T(8,128)(2,1)S(1)}, bf16[272,256]{1,0:T(8,128)(2,1)S(1)}, u32[]{:S(2)}, u32[]{:S(2)}) collective-permute-start(bf16[272,256]{1,0:T(8,128)(2,1)S(1)} %pad_maximum_fusion), channel_id=1, source_target_pairs={{0,12},{4,0},{8,4},{12,8},{16,28},{20,16},{24,20},{28,24},{32,44},... | collective-permute-start | bytes 417800 | tf_op jit(solution)/shard_map/ppermute | solution.py:289
  13.2 8.2 %copy-start = (bf16[128,2048]{1,0:T(8,128)(2,1)S(1)}, bf16[128,2048]{1,0:T(8,128)(2,1)}, u32[]{:S(2)}) copy-start(bf16[128,2048]{1,0:T(8,128)(2,1)} %refs_1_) | copy-start | bytes 1572868
  13.3 10.3 %collective-permute-start.6 = (bf16[1088,256]{1,0:T(8,128)(2,1)S(1)}, bf16[1088,256]{1,0:T(8,128)(2,1)S(1)}, u32[]{:S(2)}, u32[]{:S(2)}) collective-permute-start(bf16[1088,256]{1,0:T(8,128)(2,1)S(1)} %constant_dynamic-update-slice_fusion.refs_5_), channel_id=1, source_target_pairs={{0,32},{4,36},{8,40},{12,44},{16,48},{20,52},{24,56},{28,60},{32,0... | collective-permute-start | bytes 1671176 | tf_op jit(solution)/shard_map/ppermute | solution.py:289
  16.0 13.5 %collective-permute-start.7 = (bf16[1088,256]{1,0:T(8,128)(2,1)S(1)}, bf16[1088,256]{1,0:T(8,128)(2,1)S(1)}, u32[]{:S(2)}, u32[]{:S(2)}) collective-permute-start(bf16[1088,256]{1,0:T(8,128)(2,1)S(1)} %constant_dynamic-update-slice_fusion.refs_5_), channel_id=1, source_target_pairs={{0,16},{4,20},{8,24},{12,28},{16,32},{20,36},{24,40},{28,44},{32,4... | collective-permute-start | bytes 1671176 | tf_op jit(solution)/shard_map/ppermute | solution.py:289
  16.7 13.2 %collective-permute-start.8 = (bf16[1088,256]{1,0:T(8,128)(2,1)S(1)}, bf16[1088,256]{1,0:T(8,128)(2,1)S(1)}, u32[]{:S(2)}, u32[]{:S(2)}) collective-permute-start(bf16[1088,256]{1,0:T(8,128)(2,1)S(1)} %constant_dynamic-update-slice_fusion.refs_5_), channel_id=1, source_target_pairs={{0,48},{4,52},{8,56},{12,60},{16,0},{20,4},{24,8},{28,12},{32,16},... | collective-permute-start | bytes 1671176 | tf_op jit(solution)/shard_map/ppermute | solution.py:289
  18.7 3.9 %collective-permute-start.5 = (bf16[128,1024]{1,0:T(8,128)(2,1)S(1)}, bf16[128,1024]{1,0:T(8,128)(2,1)S(1)}, u32[]{:S(2)}, u32[]{:S(2)}) collective-permute-start(bf16[128,1024]{1,0:T(8,128)(2,1)S(1)} %constant_dynamic-slice_fusion), channel_id=1, source_target_pairs={{0,64},{4,68},{8,72},{12,76},{16,80},{20,84},{24,88},{28,92},{32,9... | collective-permute-start | bytes 786440 | tf_op jit(solution)/shard_map/ppermute | solution.py:276
  21.4 1.6 %collective-permute-start.4 = (bf16[128,1024]{1,0:T(8,128)(2,1)S(1)}, bf16[128,1024]{1,0:T(8,128)(2,1)S(1)}, u32[]{:S(2)}, u32[]{:S(2)}) collective-permute-start(bf16[128,1024]{1,0:T(8,128)(2,1)S(1)} %constant_dynamic-slice_fusion.1), channel_id=1, source_target_pairs={{0,64},{4,68},{8,72},{12,76},{16,80},{20,84},{24,88},{28,92},{32,9... | collective-permute-start | bytes 786440 | tf_op jit(solution)/shard_map/ppermute | solution.py:276
  51.9 11.7 %collective-permute-start.11 = (bf16[1024,256]{1,0:T(8,128)(2,1)}, bf16[1024,256]{1,0:T(8,128)(2,1)S(1)}, u32[]{:S(2)}, u32[]{:S(2)}) collective-permute-start(bf16[1024,256]{1,0:T(8,128)(2,1)} %get-tuple-element.33), channel_id=1, source_target_pairs={{0,32},{4,36},{8,40},{12,44},{16,48},{20,52},{24,56},{28,60},{32,0... | collective-permute-start | bytes 1572872 | tf_op jit(solution)/shard_map/ppermute | solution.py:289
  52.0 14.1 %collective-permute-start.12 = (bf16[1024,256]{1,0:T(8,128)(2,1)}, bf16[1024,256]{1,0:T(8,128)(2,1)S(1)}, u32[]{:S(2)}, u32[]{:S(2)}) collective-permute-start(bf16[1024,256]{1,0:T(8,128)(2,1)} %get-tuple-element.34), channel_id=1, source_target_pairs={{0,48},{4,52},{8,56},{12,60},{16,0},{20,4},{24,8},{28,12},{32,16},... | collective-permute-start | bytes 1572872 | tf_op jit(solution)/shard_map/ppermute | solution.py:289
  52.9 14.7 %collective-permute-start.13 = (bf16[1024,256]{1,0:T(8,128)(2,1)}, bf16[1024,256]{1,0:T(8,128)(2,1)S(1)}, u32[]{:S(2)}, u32[]{:S(2)}) collective-permute-start(bf16[1024,256]{1,0:T(8,128)(2,1)} %get-tuple-element.35), channel_id=1, source_target_pairs={{0,16},{4,20},{8,24},{12,28},{16,32},{20,36},{24,40},{28,44},{32,4... | collective-permute-start | bytes 1572872 | tf_op jit(solution)/shard_map/ppermute | solution.py:289
  53.5 8.0 %collective-permute-start.10 = (bf16[128,1024]{1,0:T(8,128)(2,1)}, bf16[128,1024]{1,0:T(8,128)(2,1)S(1)}, u32[]{:S(2)}, u32[]{:S(2)}) collective-permute-start(bf16[128,1024]{1,0:T(8,128)(2,1)} %get-tuple-element.31), channel_id=1, source_target_pairs={{0,64},{4,68},{8,72},{12,76},{16,80},{20,84},{24,88},{28,92},{32,9... | collective-permute-start | bytes 786440 | tf_op jit(solution)/shard_map/ppermute | solution.py:276
  60.2 11.6 %collective-permute-start.9 = (bf16[128,1024]{1,0:T(8,128)(2,1)}, bf16[128,1024]{1,0:T(8,128)(2,1)S(1)}, u32[]{:S(2)}, u32[]{:S(2)}) collective-permute-start(bf16[128,1024]{1,0:T(8,128)(2,1)} %get-tuple-element.29), channel_id=1, source_target_pairs={{0,64},{4,68},{8,72},{12,76},{16,80},{20,84},{24,88},{28,92},{32,9... | collective-permute-start | bytes 786440 | tf_op jit(solution)/shard_map/ppermute | solution.py:276
  61.6 6.1 %copy-start.2 = (bf16[1024,256]{1,0:T(8,128)(2,1)S(1)}, bf16[1024,256]{1,0:T(8,128)(2,1)}, u32[]{:S(2)}) copy-start(bf16[1024,256]{1,0:T(8,128)(2,1)} %get-tuple-element.32) | copy-start | bytes 1572868
  67.9 3.9 %copy-start.3 = (bf16[128,1024]{1,0:T(8,128)(2,1)S(1)}, bf16[128,1024]{1,0:T(8,128)(2,1)}, u32[]{:S(2)}) copy-start(bf16[128,1024]{1,0:T(8,128)(2,1)} %get-tuple-element.28) | copy-start | bytes 786436
  67.9 5.4 %collective-permute-start.14 = (bf16[256,256]{1,0:T(8,128)(2,1)S(1)}, bf16[256,256]{1,0:T(8,128)(2,1)S(1)}, u32[]{:S(2)}, u32[]{:S(2)}) collective-permute-start(bf16[256,256]{1,0:T(8,128)(2,1)S(1)} %get-tuple-element.36), channel_id=1, source_target_pairs={{0,8},{4,12},{8,0},{12,4},{16,24},{20,28},{24,16},{28,20},{32,40},... | collective-permute-start | bytes 393224 | tf_op jit(solution)/shard_map/ppermute | solution.py:289
  70.3 5.1 %collective-permute-start.15 = (bf16[256,256]{1,0:T(8,128)(2,1)S(1)}, bf16[256,256]{1,0:T(8,128)(2,1)S(1)}, u32[]{:S(2)}, u32[]{:S(2)}) collective-permute-start(bf16[256,256]{1,0:T(8,128)(2,1)S(1)} %get-tuple-element.38), channel_id=1, source_target_pairs={{0,12},{4,0},{8,4},{12,8},{16,28},{20,16},{24,20},{28,24},{32,44},... | collective-permute-start | bytes 393224 | tf_op jit(solution)/shard_map/ppermute | solution.py:289
  71.6 5.3 %collective-permute-start.16 = (bf16[256,256]{1,0:T(8,128)(2,1)S(1)}, bf16[256,256]{1,0:T(8,128)(2,1)S(1)}, u32[]{:S(2)}, u32[]{:S(2)}) collective-permute-start(bf16[256,256]{1,0:T(8,128)(2,1)S(1)} %get-tuple-element.37), channel_id=1, source_target_pairs={{0,4},{4,8},{8,12},{12,0},{16,20},{20,24},{24,28},{28,16},{32,36},... | collective-permute-start | bytes 393224 | tf_op jit(solution)/shard_map/ppermute | solution.py:289
  77.0 7.0 %collective-permute-start.17 = (bf16[128,256]{1,0:T(8,128)(2,1)S(1)}, bf16[128,256]{1,0:T(8,128)(2,1)S(1)}, u32[]{:S(2)}, u32[]{:S(2)}) collective-permute-start(bf16[128,256]{1,0:T(8,128)(2,1)S(1)} %slice.62), channel_id=1, source_target_pairs={{0,64},{4,68},{8,72},{12,76},{16,80},{20,84},{24,88},{28,92},{32,9... | collective-permute-start | bytes 196616 | tf_op jit(solution)/shard_map/ppermute | solution.py:276
